TPU v7x, 256 devices: a whole 4x4x8 slice. The times are simulated.
256 devices in a mesh: ctx: 32 (over x_hi, z, core), tp: 8 (over x_lo, y).
Axes of the slice: x: 4 (x_hi: 2, x_lo: 2; x = x_hi * 2 + x_lo), y: 4, z: 8, core: 2. Of those that a mesh axis runs over, the one named last changes fastest.
Arguments:
- hidden: bfloat16 [4096, 7168], P('ctx', 'tp'), may hold values from -500 to 500
- embed: bfloat16 [4096, 7168], P('ctx', 'tp'), may hold values from -500 to 500
- gain_hidden: float32 [7168], P('tp'), may hold values from 0.1 to 1.9
- gain_embed: float32 [7168], P('tp'), may hold values from 0.1 to 1.9
- proj_hidden: bfloat16 [7168, 576], P('tp'), may hold values from -0.0625 to 0.0625
- proj_embed: bfloat16 [7168, 576], P('tp'), may hold values from -0.0625 to 0.0625
- gain_latent: float32 [512], replicated, may hold values from 0.1 to 1.9
- key_up: bfloat16 [512, 8192], P(None, 'tp'), may hold values from -0.25 to 0.25
- value_up: bfloat16 [512, 8192], P(None, 'tp'), may hold values from -0.25 to 0.25
- queries: bfloat16 [4096, 12288], P('ctx', 'tp'), may hold values from -60 to 60
- grad_out: bfloat16 [4096, 8192], P('ctx', 'tp'), may hold values from -6 to 6
Outputs:
- attended: bfloat16 [4096, 8192], P('ctx', 'tp')
- grad_queries: bfloat16 [4096, 12288], P('ctx', 'tp')
- grad_hidden: bfloat16 [4096, 7168], P('ctx', 'tp')
- grad_embed: bfloat16 [4096, 7168], P('ctx', 'tp')
All inputs are finite; a program needn't handle non-finite values.
Results may differ from a plain program's by a relative error of at most 0.019.
The roundings to bfloat16 on the way count: a program that leaves them out, or rounds other values in their place, can miss the bound.
Values may be sent and summed in bfloat16 or wider, within the bound.
No kernel may reach another device: no remote copies, remote signals or barrier semaphores. Data moves between devices by JAX's collectives and lax.ppermute only.
A program may use at most 128 MiB of HBM per device.

v0:
```python
import jax
import jax.numpy as jnp
from jax import lax
from jax.sharding import PartitionSpec as P

D = 7168
LAT = 512
ROPE = 64
NOPE = 128
VDIM = 128


EPSILON = 1e-06
ROTARY_BASE = 10000.0


def with_halo(x, sides, width):
    for axis, dim in sides:
        size, length = (lax.axis_size(axis), x.shape[dim])
        up = [(i, (i + 1) % size) for i in range(size - 1)]
        down = [(j, i) for i, j in up]
        last = lax.slice_in_dim(x, length - width, length, axis=dim)
        first = lax.slice_in_dim(x, 0, width, axis=dim)
        before = lax.ppermute(last, axis, up)
        after = lax.ppermute(first, axis, down)
        x = jnp.concatenate([before, x, after], axis=dim)
    return x


def copy_for_each(x, axis):
    copies = jnp.broadcast_to(x, (lax.axis_size(axis), *x.shape))
    return lax.all_to_all(copies, axis, split_axis=0, concat_axis=0, tiled=True)


def over_copies(x, axis):
    everything = copy_for_each(x, axis)
    return jnp.sum(everything, axis=0)


def packed_total(arrays, axis):
    line, at, finished = (jnp.concatenate([a.reshape(-1) for a in arrays]), 0, [])
    subtotal = over_copies(line, axis)
    for a in arrays:
        finished.append(subtotal[at : at + a.size].reshape(a.shape))
        at += a.size
    return tuple(finished)


def side_by_side(arrays, axis, dim, along):
    ends, at = ([], 0)
    for a in arrays[:-1]:
        at += a.shape[along]
        ends.append(at)
    both = jnp.concatenate(arrays, axis=along)
    return tuple(jnp.split(lax.all_gather(both, axis, axis=dim, tiled=True), ends, axis=along))


def sent_together(arrays, axis, dim, along):
    ends, at = ([], 0)
    for a in arrays[:-1]:
        at += a.shape[along]
        ends.append(at)
    both = jnp.concatenate(arrays, axis=along)
    return tuple(
        jnp.split(lax.psum_scatter(both, axis, scatter_dimension=dim, tiled=True), ends, axis=along)
    )


def rotation(positions):
    pair_count = ROPE // 2
    frequency = ROTARY_BASE ** (-jnp.arange(pair_count, dtype=jnp.float32) / pair_count)
    angles = positions.astype(jnp.float32)[:, None] * frequency[None, :]
    return (jnp.cos(angles), jnp.sin(angles))


def rotate_pairs(values, cos_table, sin_table):
    pair_count = ROPE // 2
    first_half = values[..., :pair_count]
    second_half = values[..., pair_count:]
    return jnp.concatenate(
        [
            first_half * cos_table - second_half * sin_table,
            first_half * sin_table + second_half * cos_table,
        ],
        axis=-1,
    )


def unrotate(values, cos_table, sin_table):
    pair_count = ROPE // 2
    first_half = values[..., :pair_count]
    second_half = values[..., pair_count:]
    return jnp.concatenate(
        [
            first_half * cos_table + second_half * sin_table,
            second_half * cos_table - first_half * sin_table,
        ],
        axis=-1,
    )


def local_positions(tokens, ctx_index, groups):
    half_rows = tokens // 2
    offsets = jnp.arange(tokens, dtype=jnp.int32)
    early_pos = ctx_index * half_rows + offsets
    late_pos = (2 * groups - 1 - ctx_index) * half_rows + offsets - half_rows
    return jnp.where(offsets < half_rows, early_pos, late_pos)


def to_positions(values, groups):
    half_rows = values.shape[0] // (2 * groups)
    trailing = values.shape[1:]
    shaped = values.reshape((groups, 2, half_rows) + trailing)
    early_rows = shaped[:, 0].reshape((groups * half_rows,) + trailing)
    late_rows = shaped[::-1, 1].reshape((groups * half_rows,) + trailing)
    return jnp.concatenate([early_rows, late_rows], axis=0)


def to_rows(values, groups):
    half_rows = values.shape[0] // (2 * groups)
    trailing = values.shape[1:]
    early_rows = values[: groups * half_rows].reshape((groups, half_rows) + trailing)
    late_rows = values[groups * half_rows :].reshape((groups, half_rows) + trailing)[::-1]
    return jnp.stack([early_rows, late_rows], axis=1).reshape((2 * groups * half_rows,) + trailing)


def finish_latent(part_hidden, part_next, squares, gain_latent, positions):
    inverse = lax.rsqrt(squares / D + EPSILON)
    latent = inverse[:, 0:1] * part_hidden + inverse[:, 1:2] * part_next
    leading = latent[:, :LAT]
    inv_latent = lax.rsqrt(jnp.mean(leading * leading, axis=1, keepdims=True) + EPSILON)
    key_latent = (leading * inv_latent * gain_latent).astype(jnp.bfloat16)
    cos_table, sin_table = rotation(positions)
    key_rope = rotate_pairs(latent[:, LAT:], cos_table, sin_table).astype(jnp.bfloat16)
    return (key_latent, key_rope, latent, inverse, inv_latent)


def latent_backward(
    grad_key_latent,
    grad_key_rope,
    latent,
    inverse,
    inv_latent,
    gain_latent,
    positions,
    part_hidden,
    part_next,
):
    cos_table, sin_table = rotation(positions)
    grad_rope = unrotate(grad_key_rope, cos_table, sin_table)
    leading = latent[:, :LAT]
    gained = gain_latent * grad_key_latent
    grad_leading = (
        inv_latent * gained
        - inv_latent**3 * leading * jnp.sum(gained * leading, axis=1, keepdims=True) / LAT
    )
    grad_latent = jnp.concatenate([grad_leading, grad_rope], axis=1)
    part_grad_hidden = (inverse[:, 0:1] * grad_latent).astype(jnp.bfloat16)
    part_grad_next = (inverse[:, 1:2] * grad_latent).astype(jnp.bfloat16)
    inv_sums = jnp.concatenate(
        [
            jnp.sum(grad_latent * part_hidden, axis=1, keepdims=True),
            jnp.sum(grad_latent * part_next, axis=1, keepdims=True),
        ],
        axis=1,
    )
    coefficient = inv_sums * inverse**3 / D
    return (part_grad_hidden, part_grad_next, coefficient)


def attend_half(
    query_rows, grad_rows, query_pos, key_table, block_count, key_block, score_scale, grad_keys
):
    key_total = key_table.shape[0]
    row_total = query_rows.shape[0]
    key_offsets = jnp.arange(key_block, dtype=jnp.int32)

    def score_step(block_index, loop_state):
        buffer, running = loop_state
        first_key = block_index * key_block
        key_slab = lax.dynamic_slice_in_dim(key_table, first_key, key_block, 0)
        scores = (
            jnp.einsum("rc,kc->rk", query_rows, key_slab, preferred_element_type=jnp.float32)
            * score_scale
        )
        allowed = (first_key + key_offsets)[None, :] <= query_pos[:, None]
        scores = jnp.where(allowed, scores, -jnp.inf)
        buffer = lax.dynamic_update_slice_in_dim(buffer, scores, first_key, 1)
        return (buffer, jnp.maximum(running, jnp.max(scores, axis=1)))

    initial = (
        jnp.full((row_total, key_total), -jnp.inf, jnp.float32),
        jnp.full((row_total,), -jnp.inf, jnp.float32),
    )
    buffer, running = lax.fori_loop(0, block_count, score_step, initial)
    weights = jnp.exp(buffer - running[:, None])
    prob_table = (weights / jnp.sum(weights, axis=1, keepdims=True)).astype(jnp.bfloat16)

    def value_step(block_index, running_sum):
        first_key = block_index * key_block
        prob_slab = lax.dynamic_slice_in_dim(prob_table, first_key, key_block, 1)
        value_slab = lax.dynamic_slice_in_dim(key_table, first_key, key_block, 0)[:, :LAT]
        return running_sum + jnp.dot(prob_slab, value_slab, preferred_element_type=jnp.float32)

    out_latent = lax.fori_loop(0, block_count, value_step, jnp.zeros((row_total, LAT), jnp.float32))
    delta_rows = jnp.sum(grad_rows.astype(jnp.float32) * out_latent, axis=1, keepdims=True)

    def grad_step(block_index, loop_state):
        grad_query, grad_keys = loop_state
        first_key = block_index * key_block
        key_slab = lax.dynamic_slice_in_dim(key_table, first_key, key_block, 0)
        prob_slab = lax.dynamic_slice_in_dim(prob_table, first_key, key_block, 1)
        grad_prob = jnp.einsum(
            "rl,kl->rk", grad_rows, key_slab[:, :LAT], preferred_element_type=jnp.float32
        )
        grad_score = (
            prob_slab.astype(jnp.float32) * (grad_prob - delta_rows) * score_scale
        ).astype(jnp.bfloat16)
        grad_query = grad_query + jnp.dot(grad_score, key_slab, preferred_element_type=jnp.float32)
        grad_lead = jnp.einsum(
            "rk,rl->kl", grad_score, query_rows[:, :LAT], preferred_element_type=jnp.float32
        ) + jnp.einsum("rk,rl->kl", prob_slab, grad_rows, preferred_element_type=jnp.float32)
        grad_tail = jnp.einsum(
            "rk,rc->kc", grad_score, query_rows[:, LAT:], preferred_element_type=jnp.float32
        )
        previous = lax.dynamic_slice_in_dim(grad_keys, first_key, key_block, 0)
        update = previous + jnp.concatenate([grad_lead, grad_tail], axis=1)
        return (grad_query, lax.dynamic_update_slice_in_dim(grad_keys, update, first_key, 0))

    grad_query, grad_keys = lax.fori_loop(
        0, block_count, grad_step, (jnp.zeros((row_total, LAT + ROPE), jnp.float32), grad_keys)
    )
    return (out_latent, grad_query, grad_keys)


def on_device(
    hidden,
    embed,
    gain_hidden,
    gain_embed,
    proj_hidden,
    proj_embed,
    gain_latent,
    key_up,
    value_up,
    queries,
    grad_out,
):
    tokens = hidden.shape[0]
    half_rows = tokens // 2
    groups = lax.axis_size("ctx")
    ctx_index = lax.axis_index("ctx")
    head_count = key_up.shape[1] // NOPE
    score_scale = (NOPE + ROPE) ** (-0.5)
    key_total = tokens * groups
    key_block = max(256, key_total // 16)
    edge_rows = jnp.stack([embed[0], embed[half_rows]], axis=0)
    padded = with_halo(edge_rows, (("ctx", 0),), 1)
    after_early = jnp.where(ctx_index == groups - 1, embed[half_rows], padded[3])
    next_embed = jnp.concatenate(
        [embed[1:half_rows], after_early[None], embed[half_rows + 1 :], padded[0][None]], axis=0
    )
    hidden_wide = hidden.astype(jnp.float32)
    next_wide = next_embed.astype(jnp.float32)
    squares = jnp.stack(
        [jnp.sum(hidden_wide * hidden_wide, axis=1), jnp.sum(next_wide * next_wide, axis=1)], axis=1
    )
    scaled_hidden = (hidden_wide * gain_hidden).astype(jnp.bfloat16)
    scaled_next = (next_wide * gain_embed).astype(jnp.bfloat16)
    part_hidden = jnp.dot(scaled_hidden, proj_hidden, preferred_element_type=jnp.float32)
    part_next = jnp.dot(scaled_next, proj_embed, preferred_element_type=jnp.float32)
    positions = local_positions(tokens, ctx_index, groups)
    part_hidden, part_next, squares = packed_total((part_hidden, part_next, squares), "tp")
    key_latent, key_rope, latent, inverse, inv_latent = finish_latent(
        part_hidden, part_next, squares, gain_latent, positions
    )
    all_latent, all_rope = side_by_side((key_latent, key_rope), "ctx", 0, 1)
    key_table = jnp.concatenate(
        [to_positions(all_latent, groups), to_positions(all_rope, groups)], axis=1
    )
    query_heads = queries.reshape(tokens, head_count, NOPE + ROPE)
    cos_table, sin_table = rotation(positions)
    query_rot = rotate_pairs(
        query_heads[..., NOPE:].astype(jnp.float32), cos_table[:, None], sin_table[:, None]
    ).astype(jnp.bfloat16)
    key_up_heads = key_up.reshape(LAT, head_count, NOPE)
    value_up_heads = value_up.reshape(LAT, head_count, VDIM)
    query_latent = jnp.einsum(
        "shn,lhn->shl", query_heads[..., :NOPE], key_up_heads, preferred_element_type=jnp.float32
    ).astype(jnp.bfloat16)
    query_full = jnp.concatenate([query_latent, query_rot], axis=2)
    grad_latent_rows = jnp.einsum(
        "shv,lhv->shl",
        grad_out.reshape(tokens, head_count, VDIM),
        value_up_heads,
        preferred_element_type=jnp.float32,
    ).astype(jnp.bfloat16)
    grad_keys = jnp.zeros((key_total, LAT + ROPE), jnp.float32)
    attended_parts = []
    grad_query_parts = []
    for segment in range(2):
        if segment == 0:
            first_pos = ctx_index * half_rows
        else:
            first_pos = (2 * groups - 1 - ctx_index) * half_rows
        rows_slice = slice(segment * half_rows, (segment + 1) * half_rows)
        query_rows = query_full[rows_slice].reshape(half_rows * head_count, LAT + ROPE)
        grad_rows = grad_latent_rows[rows_slice].reshape(half_rows * head_count, LAT)
        query_pos = jnp.repeat(first_pos + jnp.arange(half_rows, dtype=jnp.int32), head_count)
        block_count = (first_pos + half_rows + key_block - 1) // key_block
        out_latent, grad_query, grad_keys = attend_half(
            query_rows,
            grad_rows,
            query_pos,
            key_table,
            block_count,
            key_block,
            score_scale,
            grad_keys,
        )
        out_rounded = out_latent.astype(jnp.bfloat16).reshape(half_rows, head_count, LAT)
        attended_parts.append(
            jnp.einsum(
                "shl,lhv->shv", out_rounded, value_up_heads, preferred_element_type=jnp.float32
            ).astype(jnp.bfloat16)
        )
        grad_lead = grad_query[:, :LAT].astype(jnp.bfloat16).reshape(half_rows, head_count, LAT)
        grad_nope = jnp.einsum(
            "shl,lhn->shn", grad_lead, key_up_heads, preferred_element_type=jnp.float32
        )
        grad_rope = unrotate(
            grad_query[:, LAT:].reshape(half_rows, head_count, ROPE),
            cos_table[rows_slice][:, None],
            sin_table[rows_slice][:, None],
        )
        grad_query_parts.append(
            jnp.concatenate([grad_nope, grad_rope], axis=2).astype(jnp.bfloat16)
        )
    attended = jnp.concatenate(attended_parts, axis=0).reshape(tokens, head_count * VDIM)
    grad_queries = jnp.concatenate(grad_query_parts, axis=0).reshape(
        tokens, head_count * (NOPE + ROPE)
    )
    grad_key_rows = to_rows(grad_keys, groups)
    grad_key_latent, grad_key_rope = sent_together(
        (grad_key_rows[:, :LAT], grad_key_rows[:, LAT:]), "ctx", 0, 1
    )
    grad_key_latent, grad_key_rope = packed_total((grad_key_latent, grad_key_rope), "tp")
    part_grad_hidden, part_grad_next, coefficient = latent_backward(
        grad_key_latent,
        grad_key_rope,
        latent,
        inverse,
        inv_latent,
        gain_latent,
        positions,
        part_hidden,
        part_next,
    )
    grad_hidden = (
        gain_hidden
        * jnp.einsum("rc,dc->rd", part_grad_hidden, proj_hidden, preferred_element_type=jnp.float32)
        - coefficient[:, 0:1] * hidden_wide
    ).astype(jnp.bfloat16)
    grad_next = (
        gain_embed
        * jnp.einsum("rc,dc->rd", part_grad_next, proj_embed, preferred_element_type=jnp.float32)
        - coefficient[:, 1:2] * next_wide
    )
    grad_next_rounded = grad_next.astype(jnp.bfloat16)
    edge_grads = jnp.stack(
        [grad_next_rounded[tokens - 1], grad_next_rounded[half_rows - 1]], axis=0
    )
    returned = with_halo(edge_grads, (("ctx", 0),), 1)
    before_late = jnp.where(ctx_index == groups - 1, grad_next_rounded[half_rows - 1], returned[3])
    grad_embed = jnp.concatenate(
        [
            returned[0][None],
            grad_next_rounded[: half_rows - 1],
            before_late[None],
            grad_next_rounded[half_rows : tokens - 1],
        ],
        axis=0,
    )
    return (attended, grad_queries, grad_hidden, grad_embed)


def solution(mesh):
    placed = (
        P("ctx", "tp"),
        P("ctx", "tp"),
        P("tp"),
        P("tp"),
        P("tp", None),
        P("tp", None),
        P(),
        P(None, "tp"),
        P(None, "tp"),
        P("ctx", "tp"),
        P("ctx", "tp"),
    )
    return jax.shard_map(
        on_device,
        mesh=mesh,
        in_specs=placed,
        out_specs=(P("ctx", "tp"), P("ctx", "tp"), P("ctx", "tp"), P("ctx", "tp")),
        check_vma=False,
    )
```

profile of v0, /device:TPU:4, one launch (start us, length us, event | category | flops | bytes accessed | tf_op | source)
XLA Modules:
  0.0 718.3 jit_solution(15203592819039717801)
XLA Ops:
  8.0 7.1 collective-permute-start
  21.9 5.4 collective-permute-done.1
  29.6 3.9 broadcast_in_dim.28
  33.5 6.0 all-to-all-start
  39.7 48.9 %all-to-all-done = f32[8,1,147712]{2,1,0:T(1,128)} async-done(((f32[8,1,147712]{2,1,0:T(1,128)}), f32[8,1,147712]{2,1,0:T(1,128)}, u32[]{:S(2)}, u32[]{:S(2)}) %all-to-all-start) | async-done | bytes 4726816 | tf_op jit(solution)/shard_map/all_to_all | solution.py:32
  88.6 8.6 %reduce_sum.110 = f32[147712]{0:T(1024)S(1)} reduce(f32[8,1,147712]{2,1,0:T(1,128)} %all-to-all-done, f32[]{:T(128)} %constant.114.clone.1), dimensions={0,1}, to_apply=%region_2.3 | reduce | flops 1033984 | bytes 5317636 | tf_op jit(solution)/shard_map/reduce_sum | solution.py:37
  110.9 73.7 %all-gather.2.cloned.1.call-done = bf16[4096,576]{0,1:T(8,128)(2,1)} async-done(((bf16[128,576]{0,1:T(8,128)(2,1)}), bf16[4096,576]{0,1:T(8,128)(2,1)}) %all-gather.2.cloned.1.call-update) | async-done | bytes 4718608 | tf_op jit(solution)/shard_map/all_gather | solution.py:55
  184.6 4.8 split.16
  189.3 6.5 copy.302
  195.8 4.8 fusion.119
  200.6 3.2 rev.9
  203.8 2.1 reshape.237
  205.9 4.7 fusion.122
  210.6 3.3 rev.10
  213.9 2.5 copy.304
  216.4 3.6 copy.303
  220.0 10.7 %maximum_maximum_fusion = bf16[4096,576]{1,0:T(8,128)(2,1)} fusion(bf16[2048,64]{1,0:T(8,128)(2,1)S(1)} %bitcast.184, bf16[2048,64]{1,0:T(8,128)(2,1)} %bitcast.185, bf16[2048,512]{1,0:T(8,128)(2,1)} %bitcast.182, bf16[2048,512]{1,0:T(8,128)(2,1)} %bitcast.183), kind=kLoop, calls=%fused_computation.71 | loop fusion | flops 18874368 | bytes 9437184 | tf_op jit(solution)/shard_map/concatenate | solution.py:278
  230.7 4.4 broadcast.157.clone.1
  235.1 12.0 %while.74 = (s32[]{:T(128)}, f32[512,4096]{0,1:T(8,128)}, f32[512]{0:T(512)S(1)}, s32[]{:T(128)}, bf16[4096,576]{1,0:T(8,128)(2,1)}, /*index=5*/bf16[512,576]{1,...) while((s32[]{:T(128)}, f32[512,4096]{0,1:T(8,128)}, ...), condition=%wide.region_6.7_spmd.clone, body=%wide.region_4.6_spmd.clone.sunk | while | flops 151519488 | bytes 1461663 | solution.py:195
  235.3 2.2 fusion.224
  237.6 2.2 fusion.224
  240.0 2.2 fusion.224
  242.4 2.2 fusion.224
  244.8 2.2 fusion.224
  247.1 4.8 fusion.52
  253.1 2.7 divide_convert_fusion.1
  255.9 7.0 while.70
  262.9 4.4 broadcast.157.clone
  267.3 28.6 %while.75 = (s32[]{:T(128)}, f32[512,4096]{0,1:T(8,128)}, f32[512]{0:T(512)S(1)}, s32[]{:T(128)}, bf16[4096,576]{1,0:T(8,128)(2,1)}, /*index=5*/bf16[512,576]{1,...) while((s32[]{:T(128)}, f32[512,4096]{0,1:T(8,128)}, ...), condition=%wide.region_12.13_spmd.clone, body=%wide.region_10.12_spmd.clone.sunk | while | flops 151519488 | bytes 1461663 | solution.py:195
  267.4 2.2 fusion.226
  269.8 2.2 fusion.226
  272.2 2.2 fusion.226
  274.6 2.2 fusion.226
  276.9 2.2 fusion.226
  279.3 2.2 fusion.226
  281.7 2.2 fusion.226
  284.1 2.2 fusion.226
  286.4 2.2 fusion.226
  288.8 2.2 fusion.226
  291.2 2.2 fusion.226
  293.6 2.2 fusion.226
  295.8 4.8 fusion.53
  301.8 2.7 divide_convert_fusion
  304.6 16.7 %while.71 = (s32[]{:T(128)}, f32[512,512]{1,0:T(8,128)S(1)}, s32[]{:T(128)}, bf16[512,4096]{0,1:T(8,128)(2,1)}, bf16[4096,576]{1,0:T(8,128)(2,1)}, /*index=5*/s32[]{:T(128)}, s32[]{:T(128)}, s32[]{:T(128)}, s32[]{:T(128)}) while((s32[]{:T(128)}, f32[512,512]{1,0:T(8,128)S(1)}, s32[]{:T(128)}, bf16[512,4096]{0,1:T(8,128)(2,1)}, ...), condition=%wide.region_15.16_spmd, body=%wide.region_14.15_spmd.sunk | while | flops 134479872 | bytes 2622603 | solution.py:205
  321.3 2.9 multiply_reduce_fusion
  324.3 4.7 broadcast_in_dim.30
  329.1 33.0 %while.72 = (s32[]{:T(128)}, f32[512,576]{0,1:T(8,128)S(1)}, f32[4096,576]{1,0:T(8,128)}, s32[]{:T(128)}, bf16[512,4096]{0,1:T(8,128)(2,1)}, /*index=5*/bf16[409...) while((s32[]{:T(128)}, f32[512,576]{0,1:T(8,128)S(1)}, ...), condition=%wide.region_18.19_spmd, body=%wide.region_17.18_spmd.sunk | while | flops 571801600 | bytes 9768119 | solution.py:230
  338.9 2.0 fusion.208
  345.5 2.0 fusion.208
  362.3 106.7 %while.73 = (s32[]{:T(128)}, f32[512,576]{0,1:T(8,128)S(1)}, f32[4096,576]{1,0:T(8,128)}, s32[]{:T(128)}, bf16[512,4096]{0,1:T(8,128)(2,1)}, /*index=5*/bf16[409...) while((s32[]{:T(128)}, f32[512,576]{0,1:T(8,128)S(1)}, ...), condition=%wide.region_21.22_spmd, body=%wide.region_20.21_spmd.sunk | while | flops 571801600 | bytes 9768119 | solution.py:230
  376.6 2.0 fusion.222
  385.5 2.0 fusion.222
  469.0 4.7 fusion.118
  473.8 2.7 reverse_bitcast_fusion
  476.5 7.5 %pad_maximum_fusion = f32[32,2,64,576]{3,2,1,0:T(8,128)} fusion(f32[32,1,64,576]{3,2,1,0:T(8,128)} %reverse_bitcast_fusion, f32[32,1,64,576]{3,2,1,0:T(8,128)S(1)} %bitcast.179), kind=kLoop, calls=%fused_computation.64 | loop fusion | flops 2359296 | bytes 18874368 | tf_op jit(solution)/shard_map/stack | solution.py:124
  495.9 155.7 %reduce-scatter.2.cloned.1.call-done = f32[128,576]{1,0:T(8,128)} async-done(((f32[4096,576]{1,0:T(8,128)}), f32[128,576]{1,0:T(8,128)}) %reduce-scatter.2.cloned.1.call-update) | async-done | bytes 294928 | tf_op jit(solution)/shard_map/reduce_scatter | solution.py:65
  653.6 2.6 broadcast_in_dim.33
  656.3 5.5 all-to-all-start.1
  665.6 2.1 copy.330
  683.8 3.1 all-to-all-done.1
  686.9 2.9 reduce_sum.116
  698.1 2.5 collective-permute-start.3
  701.9 2.1 collective-permute-start.2
  704.0 6.4 collective-permute-done.2
  (356 shorter events, 226.8 us)
Async XLA Ops:
  7.2 98.6 %copy-start = (bf16[512,1024]{1,0:T(8,128)(2,1)S(1)}, bf16[512,1024]{1,0:T(8,128)(2,1)}, u32[]{:S(2)}) copy-start(bf16[512,1024]{1,0:T(8,128)(2,1)} %param.30) | copy-start | bytes 3145732
  8.0 10.0 %collective-permute-start = (bf16[1,896]{1,0:T(2,128)(2,1)S(1)}, bf16[1,896]{1,0:T(2,128)(2,1)S(1)}, u32[]{:S(2)}, u32[]{:S(2)}) collective-permute-start(bf16[1,896]{1,0:T(2,128)(2,1)S(1)} %slice.211), channel_id=1, source_target_pairs={{8,0},{16,8},{24,16},{32,24},{40,32},{48,40},{56,48},{64,56},{72,6... | collective-permute-start | bytes 5384 | tf_op jit(solution)/shard_map/ppermute | solution.py:25
  18.0 15.5 %copy-start.15 = (bf16[63,896]{1,0:T(8,128)(2,1)}, bf16[63,896]{1,0:T(8,128)(2,1)S(1)}, u32[]{:S(2)}) copy-start(bf16[63,896]{1,0:T(8,128)(2,1)S(1)} %get-tuple-element.526) | copy-start | bytes 338692
  18.0 15.5 %copy-start.17 = (bf16[63,896]{1,0:T(8,128)(2,1)}, bf16[63,896]{1,0:T(8,128)(2,1)S(1)}, u32[]{:S(2)}) copy-start(bf16[63,896]{1,0:T(8,128)(2,1)S(1)} %get-tuple-element.527) | copy-start | bytes 338692
  18.8 8.5 %collective-permute-start.1 = (bf16[1,896]{1,0:T(2,128)(2,1)S(1)}, bf16[1,896]{1,0:T(2,128)(2,1)S(1)}, u32[]{:S(2)}, u32[]{:S(2)}) collective-permute-start(bf16[1,896]{1,0:T(2,128)(2,1)S(1)} %get-tuple-element.529), channel_id=1, source_target_pairs={{0,8},{8,16},{16,24},{24,32},{32,40},{40,48},{48,56},{56,64},{64,7... | collective-permute-start | bytes 5384 | tf_op jit(solution)/shard_map/ppermute | solution.py:24
  27.3 6.2 copy-start.22
  33.5 55.0 %all-to-all-start = ((f32[8,1,147712]{2,1,0:T(1,128)}), f32[8,1,147712]{2,1,0:T(1,128)}, u32[]{:S(2)}, u32[]{:S(2)}) async-start(f32[8,1,147712]{2,1,0:T(1,128)} %broadcast_in_dim.28), calls=%async_computation | async-start | bytes 9453568 | tf_op jit(solution)/shard_map/all_to_all | solution.py:32
  39.6 59.5 %copy-start.20 = (f32[512]{0:T(512)S(1)}, f32[512]{0:T(512)}, u32[]{:S(2)}) copy-start(f32[512]{0:T(512)} %param.29) | copy-start | bytes 6148
  39.6 145.0 %all-gather.2.cloned.1.call-start = ((), (), s32[]{:S(2)}) async-start(), calls=%async_computation.3 | async-start | bytes 4866048 | tf_op jit(solution)/shard_map/all_gather | solution.py:55
  39.6 59.6 %copy-start.26 = (f32[32]{0:T(128)}, f32[32]{0:T(128)S(1)}, u32[]{:S(2)}) copy-start(f32[32]{0:T(128)S(1)} %multiply_power_fusion) | copy-start | bytes 388
  39.7 59.5 %copy-start.28 = (f32[128]{0:T(128)}, f32[128]{0:T(128)S(1)}, u32[]{:S(2)}) copy-start(f32[128]{0:T(128)S(1)} %fusion.113) | copy-start | bytes 1540
  39.7 62.0 %copy-start.14 = (bf16[512,1024]{1,0:T(8,128)(2,1)S(1)}, bf16[512,1024]{1,0:T(8,128)(2,1)}, u32[]{:S(2)}) copy-start(bf16[512,1024]{1,0:T(8,128)(2,1)} %param.31) | copy-start | bytes 3145732
  97.6 0.7 copy-start.24
  97.8 7.9 %copy-start.11 = (f32[128,576]{0,1:T(8,128)}, f32[128,576]{0,1:T(8,128)S(1)}, u32[]{:S(2)}) copy-start(f32[128,576]{0,1:T(8,128)S(1)} %copy.300) | copy-start | bytes 884740
  98.1 8.1 %copy-start.12 = (f32[128,576]{0,1:T(8,128)}, f32[128,576]{0,1:T(8,128)S(1)}, u32[]{:S(2)}) copy-start(f32[128,576]{0,1:T(8,128)S(1)} %copy.301) | copy-start | bytes 884740
  98.2 0.9 copy-start.7
  98.9 7.3 %copy-start.29 = (f32[128]{0:T(128)}, f32[128]{0:T(128)S(1)}, u32[]{:S(2)}) copy-start(f32[128]{0:T(128)S(1)} %get-tuple-element.545) | copy-start | bytes 1540
  99.9 551.7 %reduce-scatter.2.cloned.1.call-start = ((), (), s32[]{:S(2)}) async-start(), calls=%async_computation.4 | async-start | bytes 10813440 | tf_op jit(solution)/shard_map/reduce_scatter | solution.py:65
  103.2 0.8 copy-start.8
  103.2 1.0 copy-start.9
  195.8 7.9 %slice-start = ((bf16[4096,576]{0,1:T(8,128)(2,1)}), bf16[4096,64]{0,1:T(8,128)(2,1)S(1)}, s32[]{:S(2)}) async-start(bf16[4096,576]{0,1:T(8,128)(2,1)} %all-gather.2.cloned.1.call-done), calls=%async_computation.5 | async-start | bytes 1048576 | tf_op jit(solution)/shard_map/split | solution.py:55
  247.1 4.8 copy-start.4
  247.1 6.0 copy-start.2
  295.8 4.8 copy-start.3
  295.8 6.0 copy-start.1
  324.3 4.8 copy-start.5
  324.3 4.8 copy-start.6
  489.3 4.7 copy-start.18
  489.3 4.7 copy-start.19
  656.3 30.7 %all-to-all-start.1 = ((f32[8,1,73728]{2,1,0:T(1,128)}), f32[8,1,73728]{2,1,0:T(1,128)S(1)}, u32[]{:S(2)}, u32[]{:S(2)}) async-start(f32[8,1,73728]{2,1,0:T(1,128)} %broadcast_in_dim.33), calls=%async_computation.2 | async-start | bytes 4718592 | tf_op jit(solution)/shard_map/all_to_all | solution.py:32
  675.8 18.6 %copy-start.27 = (f32[32]{0:T(128)S(1)}, f32[32]{0:T(128)}, u32[]{:S(2)}) copy-start(f32[32]{0:T(128)} %copy-done.26) | copy-start | bytes 388
  677.7 18.7 %copy-start.16 = (bf16[63,896]{1,0:T(8,128)(2,1)S(1)}, bf16[63,896]{1,0:T(8,128)(2,1)}, u32[]{:S(2)}) copy-start(bf16[63,896]{1,0:T(8,128)(2,1)} %copy-done.15) | copy-start | bytes 338692
  677.7 18.7 %copy-start.23 = (bf16[1,896]{1,0:T(2,128)(2,1)S(1)}, bf16[1,896]{1,0:T(2,128)(2,1)}, u32[]{:S(2)}) copy-start(bf16[1,896]{1,0:T(2,128)(2,1)} %copy-done.22) | copy-start | bytes 5380
  677.7 18.7 %copy-start.25 = (f32[128]{0:T(128)S(1)}, f32[128]{0:T(128)}, u32[]{:S(2)}) copy-start(f32[128]{0:T(128)} %copy-done.24) | copy-start | bytes 1540
  680.2 20.4 %copy-start.21 = (f32[896]{0:T(1024)S(1)}, f32[896]{0:T(1024)}, u32[]{:S(2)}) copy-start(f32[896]{0:T(1024)} %param.25) | copy-start | bytes 10756
  689.9 10.8 %copy-start.10 = (bf16[896,576]{0,1:T(8,128)(2,1)S(1)}, bf16[896,576]{0,1:T(8,128)(2,1)}, u32[]{:S(2)}) copy-start(bf16[896,576]{0,1:T(8,128)(2,1)} %param.27) | copy-start | bytes 3096580
  689.9 10.8 %copy-start.13 = (bf16[128,896]{1,0:T(8,128)(2,1)S(1)}, bf16[128,896]{1,0:T(8,128)(2,1)}, u32[]{:S(2)}) copy-start(bf16[128,896]{1,0:T(8,128)(2,1)} %param.23) | copy-start | bytes 688132
  698.1 3.9 collective-permute-start.3
  701.9 8.5 %collective-permute-start.2 = (bf16[1,896]{1,0:T(2,128)(2,1)S(1)}, bf16[1,896]{1,0:T(2,128)(2,1)S(1)}, u32[]{:S(2)}, u32[]{:S(2)}) collective-permute-start(bf16[1,896]{1,0:T(2,128)(2,1)S(1)} %get-tuple-element.522), channel_id=1, source_target_pairs={{0,8},{8,16},{16,24},{24,32},{32,40},{40,48},{48,56},{56,64},{64,7... | collective-permute-start | bytes 5384 | tf_op jit(solution)/shard_map/ppermute | solution.py:24
Sparse Core Ops, SparseCore 0:
  100.0 84.4 all-gather.1
  484.1 167.4 reduce-scatter.1
where the time goes:
time: 730 us; the launch traced here: 718 us
  waiting for transfers between devices  293 us (40%)
  matrix products  179 us (25%)
  local copies, waits for them, and re-layouts  107 us (15%)
  other arithmetic  96.3 us (13%)
  starting transfers between devices  25.8 us (4%)
  between operations  15 us (2%)
    reduce_scatter x1, waiting for transfers between devices, sent_together(): lax.psum_scatter(both, axis, scatter_dimension=dim, tiled=True)  156 us
    all_gather x1, waiting for transfers between devices, side_by_side(): lax.all_gather(both, axis, axis=dim, tiled=True)  73.7 us
    all_to_all x2, waiting for transfers between devices, copy_for_each(): return lax.all_to_all(copies, axis, split_axis=0, concat_axis=0, tiled=True)  52 us
    dot_general x17, matrix products, score_step(): jnp.einsum('rc,kc->rk', query_rows, key_slab, preferred_element_type=jnp....  37.3 us
    dynamic_update_slice x17, other arithmetic, grad_step(): lax.dynamic_update_slice_in_dim(grad_keys, update, first_key, 0)  34.2 us
    dot_general x17, matrix products, grad_step(): jnp.einsum('rl,kl->rk', grad_rows, key_slab[:, :LAT], preferred_element_t...  25.3 us
    dot_general x17, matrix products, grad_step(): jnp.dot(grad_score, key_slab, preferred_element_type=jnp.float32)  23.5 us
    dot_general x17, matrix products, grad_step(): jnp.einsum('rk,rl->kl', prob_slab, grad_rows, preferred_element_type=jnp....  23.4 us
  transfers between devices with their start and end apart: 8, of which 7 were waited for; matrix products, arithmetic and copies ran while one was open for 7% of the time, Pallas kernels for 0%

commit v1 on v0

v1 whole, which is shorter than its diff:
```python
import functools

import jax
import jax.numpy as jnp
from jax import lax
from jax.experimental import pallas as pl
from jax.experimental.pallas import tpu as pltpu
from jax.sharding import Mesh, PartitionSpec as P

D = 7168
LAT = 512
ROPE = 64
NOPE = 128
VDIM = 128
KEYW = LAT + ROPE
WIDE = 640

EPSILON = 1e-06
ROTARY_BASE = 10000.0
SCALE = (NOPE + ROPE) ** (-0.5)

CTX = ("xh", "z", "co")
TP = ("xl", "y")
XZ = ("xh", "z")
N_CTX = 32
N_TP = 8
HEADS = 8
HALF = 64
ROWS = 128
PIECE = ROWS // N_TP
SEG = HALF * HEADS
BLOCK = 512
STEPS = 9

bf16 = jnp.bfloat16
f32 = jnp.float32


def rotation(positions):
    pair_count = ROPE // 2
    frequency = ROTARY_BASE ** (-jnp.arange(pair_count, dtype=f32) / pair_count)
    angles = positions.astype(f32)[:, None] * frequency[None, :]
    return (jnp.cos(angles), jnp.sin(angles))


def rotate_pairs(values, cos_table, sin_table):
    a, b = jnp.split(values, 2, axis=-1)
    return jnp.concatenate(
        [a * cos_table - b * sin_table, a * sin_table + b * cos_table], axis=-1
    )


def unrotate(values, cos_table, sin_table):
    a, b = jnp.split(values, 2, axis=-1)
    return jnp.concatenate(
        [a * cos_table + b * sin_table, b * cos_table - a * sin_table], axis=-1
    )


def row_positions(ctx, rows):
    return jnp.where(rows < HALF, ctx * HALF + rows, (63 - ctx) * HALF + rows - HALF)


def gather_copies(x, axes, n):
    copies = jnp.broadcast_to(x[None], (n, *x.shape))
    return lax.all_to_all(copies, axes, split_axis=0, concat_axis=0, tiled=True)


def edge_exchange(first_row, second_row):
    down = [(i + 1, i) for i in range(N_CTX - 1)]
    up = [(i, i + 1) for i in range(N_CTX - 1)]
    return lax.ppermute(first_row, CTX, down), lax.ppermute(second_row, CTX, up)


def attention_kernel(
    where_ref,
    mine_ref,
    other_ref,
    q_ref,
    qt_ref,
    g_ref,
    gt_ref,
    o_ref,
    lead_ref,
    tail_ref,
    dmine_ref,
    dother_ref,
    keys,
    s_buf,
    dp_buf,
    m_buf,
    l_buf,
    a_buf,
    ot_buf,
    dqt_buf,
    dk_buf,
    sems,
):
    ctx = where_ref[0]
    core = where_ref[1]
    copies = [
        pltpu.make_async_copy(mine_ref, keys.at[core], sems.at[0]),
        pltpu.make_async_copy(other_ref, keys.at[1 - core], sems.at[1]),
    ]
    for copy in copies:
        copy.start()
    m_buf[...] = jnp.full_like(m_buf, -jnp.inf)
    l_buf[...] = jnp.zeros_like(l_buf)
    a_buf[...] = jnp.zeros_like(a_buf)
    ot_buf[...] = jnp.zeros_like(ot_buf)
    dqt_buf[...] = jnp.zeros_like(dqt_buf)
    dk_buf[...] = jnp.zeros_like(dk_buf)
    for copy in copies:
        copy.wait()

    group = ctx // 8
    early_steps = group + 1

    def locate(i):
        late = i >= early_steps
        j = i - early_steps
        half = jnp.logical_and(late, j >= 4).astype(jnp.int32)
        block = jnp.where(late, jnp.where(j >= 4, group + j - 4, j), i)
        return late.astype(jnp.int32), half, block

    def slab(half, block):
        xh = block // 2
        at = pl.multiple_of((block % 2) * 64, 64)
        return jnp.concatenate(
            [
                keys[co, half * 4 + y, xh, pl.ds(at, 64), :]
                for co in range(2)
                for y in range(4)
            ],
            axis=0,
        )

    def nn(a, b):
        return jnp.dot(a, b, preferred_element_type=f32)

    def first(i, carry):
        seg, half, block = locate(i)
        k = slab(half, block)
        s = nn(k, qt_ref[seg]) * SCALE
        idx = lax.broadcasted_iota(jnp.int32, (BLOCK, 1), 0)
        owner = block * 8 + ((idx // 16) % 4) * 2 + idx // 256
        within = ((idx // 64) % 4) * 16 + idx % 16
        key_pos = jnp.where(half == 0, owner, 63 - owner) * 64 + within
        row = lax.broadcasted_iota(jnp.int32, (1, SEG), 1)
        q_pos = jnp.where(seg == 0, ctx, 63 - ctx) * 64 + row % 64
        s = jnp.where(key_pos <= q_pos, s, -jnp.inf)
        s_buf[i] = s
        dp = nn(k[:, :LAT], gt_ref[seg])
        dp_buf[i] = dp
        m_old = m_buf[seg]
        m_new = jnp.maximum(m_old, jnp.max(s, axis=0, keepdims=True))
        alpha = jnp.exp(m_old - m_new)
        e = jnp.exp(s - m_new)
        m_buf[seg] = m_new
        l_buf[seg] = l_buf[seg] * alpha + jnp.sum(e, axis=0, keepdims=True)
        a_buf[seg] = a_buf[seg] * alpha + jnp.sum(e * dp, axis=0, keepdims=True)
        return carry

    lax.fori_loop(0, STEPS, first, 0)

    def second(i, carry):
        seg, half, block = locate(i)
        k = slab(half, block)
        inv = 1.0 / l_buf[seg]
        delta = a_buf[seg] * inv
        p = (jnp.exp(s_buf[i] - m_buf[seg]) * inv).astype(bf16)
        ds = (p.astype(f32) * (dp_buf[i] - delta) * SCALE).astype(bf16)
        kt = k.T
        ot_buf[seg] += nn(kt[:LAT], p)
        dqt_buf[seg] += nn(kt, ds)
        lead = nn(ds, q_ref[seg, :, :LAT]) + nn(p, g_ref[seg])
        tail = nn(ds, q_ref[seg, :, LAT:])
        xh = block // 2
        at = pl.multiple_of((block % 2) * 64, 64)
        for co in range(2):
            for y in range(4):
                j = (co * 4 + y) * 64
                dk_buf[co, half * 4 + y, xh, pl.ds(at, 64), :LAT] += lead[j : j + 64]
                dk_buf[co, half * 4 + y, xh, pl.ds(at, 64), LAT:] += tail[j : j + 64]
        return carry

    lax.fori_loop(0, STEPS, second, 0)

    for seg in range(2):
        o_ref[seg] = ot_buf[seg].astype(bf16).T
        lead_ref[seg] = dqt_buf[seg, :LAT].astype(bf16).T
        tail_ref[seg] = dqt_buf[seg, LAT:].T

    def put(t, carry):
        dmine_ref[t] = dk_buf[core, t].astype(bf16)
        dother_ref[t] = dk_buf[1 - core, t].astype(bf16)
        return carry

    lax.fori_loop(0, N_TP, put, 0)


def attention(where, mine, other, q, qt, g, gt):
    vmem = pl.BlockSpec(memory_space=pltpu.VMEM)
    hbm = pl.BlockSpec(memory_space=pl.ANY)
    half_keys = (N_TP, 2, 128, KEYW)
    return pl.pallas_call(
        attention_kernel,
        in_specs=[pl.BlockSpec(memory_space=pltpu.SMEM), hbm, hbm, vmem, vmem, vmem, vmem],
        out_specs=[vmem] * 5,
        out_shape=[
            jax.ShapeDtypeStruct((2, SEG, LAT), bf16),
            jax.ShapeDtypeStruct((2, SEG, LAT), bf16),
            jax.ShapeDtypeStruct((2, SEG, ROPE), f32),
            jax.ShapeDtypeStruct(half_keys, bf16),
            jax.ShapeDtypeStruct(half_keys, bf16),
        ],
        scratch_shapes=[
            pltpu.VMEM((2,) + half_keys, bf16),
            pltpu.VMEM((STEPS, BLOCK, SEG), f32),
            pltpu.VMEM((STEPS, BLOCK, SEG), f32),
            pltpu.VMEM((2, 1, SEG), f32),
            pltpu.VMEM((2, 1, SEG), f32),
            pltpu.VMEM((2, 1, SEG), f32),
            pltpu.VMEM((2, LAT, SEG), f32),
            pltpu.VMEM((2, KEYW, SEG), f32),
            pltpu.VMEM((2,) + half_keys, f32),
            pltpu.SemaphoreType.DMA((2,)),
        ],
        compiler_params=pltpu.CompilerParams(vmem_limit_bytes=62 * 1024 * 1024),
        cost_estimate=pl.CostEstimate(
            flops=14_000_000_000, bytes_accessed=20_000_000, transcendentals=4_000_000
        ),
        name="attention",
    )(where, mine, other, q, qt, g, gt)


def on_device(
    hidden,
    embed,
    gain_hidden,
    gain_embed,
    proj_hidden,
    proj_embed,
    gain_latent,
    key_up,
    value_up,
    queries,
    grad_out,
):
    ctx = lax.axis_index(CTX)
    core = lax.axis_index("co")
    tp = lax.axis_index(TP)
    last = ctx == N_CTX - 1

    after, before = edge_exchange(embed[0:1], embed[HALF : HALF + 1])
    after_early = jnp.where(last, embed[HALF : HALF + 1], after)
    next_embed = jnp.concatenate(
        [embed[1:HALF], after_early, embed[HALF + 1 :], before], axis=0
    )
    hidden_wide = hidden.astype(f32)
    next_wide = next_embed.astype(f32)
    part_hidden = jnp.dot(
        (hidden_wide * gain_hidden).astype(bf16), proj_hidden, preferred_element_type=f32
    )
    part_next = jnp.dot(
        (next_wide * gain_embed).astype(bf16), proj_embed, preferred_element_type=f32
    )
    spread = (ROWS, WIDE - KEYW)
    parts = jnp.concatenate(
        [
            part_hidden,
            jnp.broadcast_to(jnp.sum(hidden_wide * hidden_wide, axis=1, keepdims=True), spread),
            part_next,
            jnp.broadcast_to(jnp.sum(next_wide * next_wide, axis=1, keepdims=True), spread),
        ],
        axis=1,
    ).reshape(N_TP, PIECE, 2 * WIDE)
    parts = jnp.sum(lax.all_to_all(parts, TP, split_axis=0, concat_axis=0, tiled=True), axis=0)

    part_hidden, part_next = parts[:, :KEYW], parts[:, WIDE : WIDE + KEYW]
    inv_hidden = lax.rsqrt(parts[:, KEYW : KEYW + 1] / D + EPSILON)
    inv_next = lax.rsqrt(parts[:, WIDE + KEYW : WIDE + KEYW + 1] / D + EPSILON)
    latent = inv_hidden * part_hidden + inv_next * part_next
    leading = latent[:, :LAT]
    inv_latent = lax.rsqrt(jnp.mean(leading * leading, axis=1, keepdims=True) + EPSILON)
    piece_cos, piece_sin = rotation(row_positions(ctx, tp * PIECE + jnp.arange(PIECE)))
    key_piece = jnp.concatenate(
        [
            (leading * inv_latent * gain_latent).astype(bf16),
            rotate_pairs(latent[:, LAT:], piece_cos, piece_sin).astype(bf16),
        ],
        axis=1,
    )
    same = gather_copies(key_piece, XZ, 16).reshape(2, 128, KEYW)
    mine = gather_copies(same, TP, N_TP).reshape(N_TP, 2, 128, KEYW)
    other = lax.ppermute(mine, "co", [(0, 1), (1, 0)])

    cos_table, sin_table = rotation(row_positions(ctx, jnp.arange(ROWS)))
    cos_table = cos_table.reshape(2, 1, HALF, ROPE // 2)
    sin_table = sin_table.reshape(2, 1, HALF, ROPE // 2)
    key_up_heads = key_up.reshape(LAT, HEADS, NOPE)
    value_up_heads = value_up.reshape(LAT, HEADS, VDIM)
    query_heads = queries.reshape(2, HALF, HEADS, NOPE + ROPE).transpose(0, 2, 1, 3)
    query_rot = rotate_pairs(query_heads[..., NOPE:].astype(f32), cos_table, sin_table)
    query_latent = jnp.einsum(
        "ghsn,lhn->ghsl", query_heads[..., :NOPE], key_up_heads, preferred_element_type=f32
    )
    q = jnp.concatenate([query_latent.astype(bf16), query_rot.astype(bf16)], axis=3)
    q = q.reshape(2, SEG, KEYW)
    g = jnp.einsum(
        "gshv,lhv->ghsl",
        grad_out.reshape(2, HALF, HEADS, VDIM),
        value_up_heads,
        preferred_element_type=f32,
    )
    g = g.astype(bf16).reshape(2, SEG, LAT)
    where = jnp.stack([ctx, core]).astype(jnp.int32)
    o, lead, tail, dmine, dother = attention(
        where, mine, other, q, q.swapaxes(1, 2), g, g.swapaxes(1, 2)
    )

    received = lax.ppermute(dother, "co", [(0, 1), (1, 0)])
    dkey = (dmine.astype(f32) + received.astype(f32)).astype(bf16)
    dkey = lax.all_to_all(dkey, TP, split_axis=0, concat_axis=0, tiled=True)
    dkey = jnp.sum(dkey.astype(f32), axis=0).astype(bf16).reshape(16, PIECE, KEYW)
    dkey = lax.all_to_all(dkey, XZ, split_axis=0, concat_axis=0, tiled=True)
    dkey = jnp.sum(dkey.astype(f32), axis=0)

    attended = jnp.einsum(
        "ghsl,lhv->gshv",
        o.reshape(2, HEADS, HALF, LAT),
        value_up_heads,
        preferred_element_type=f32,
    )
    attended = attended.astype(bf16).reshape(ROWS, HEADS * VDIM)
    grad_nope = jnp.einsum(
        "ghsl,lhn->ghsn",
        lead.reshape(2, HEADS, HALF, LAT),
        key_up_heads,
        preferred_element_type=f32,
    )
    grad_rope = unrotate(tail.reshape(2, HEADS, HALF, ROPE), cos_table, sin_table)
    grad_queries = jnp.concatenate([grad_nope, grad_rope], axis=3).astype(bf16)
    grad_queries = grad_queries.transpose(0, 2, 1, 3).reshape(ROWS, HEADS * (NOPE + ROPE))

    gained = gain_latent * dkey[:, :LAT]
    dlatent = jnp.concatenate(
        [
            inv_latent * gained
            - inv_latent**3 * leading * jnp.sum(gained * leading, axis=1, keepdims=True) / LAT,
            unrotate(dkey[:, LAT:], piece_cos, piece_sin),
        ],
        axis=1,
    )
    coef_hidden = jnp.sum(dlatent * part_hidden, axis=1, keepdims=True) * inv_hidden**3 / D
    coef_next = jnp.sum(dlatent * part_next, axis=1, keepdims=True) * inv_next**3 / D

    def in_two(c):
        high = c.astype(bf16)
        low = (c - high.astype(f32)).astype(bf16)
        width = (PIECE, (WIDE - KEYW) // 2)
        return [jnp.broadcast_to(high, width), jnp.broadcast_to(low, width)]

    packed = jnp.concatenate(
        [(inv_hidden * dlatent).astype(bf16)]
        + in_two(coef_hidden)
        + [(inv_next * dlatent).astype(bf16)]
        + in_two(coef_next),
        axis=1,
    )
    packed = gather_copies(packed, TP, N_TP).reshape(ROWS, 2 * WIDE)

    def whole(block):
        high = block[:, KEYW : KEYW + 1].astype(f32)
        return block[:, :KEYW], high + block[:, WIDE - 1 :].astype(f32)

    dpart_hidden, coef_hidden = whole(packed[:, :WIDE])
    grad_hidden = (
        gain_hidden
        * jnp.einsum("rc,dc->rd", dpart_hidden, proj_hidden, preferred_element_type=f32)
        - coef_hidden * hidden_wide
    ).astype(bf16)

    nexts = packed[:, WIDE:]
    after, before = edge_exchange(nexts[ROWS - 1 :], nexts[HALF - 1 : HALF])
    before_late = jnp.where(last, nexts[HALF - 1 : HALF], after)
    shifted = jnp.concatenate(
        [before, nexts[: HALF - 1], before_late, nexts[HALF : ROWS - 1]], axis=0
    )
    dpart_next, coef_next = whole(shifted)
    grad_embed = (
        gain_embed
        * jnp.einsum("rc,dc->rd", dpart_next, proj_embed, preferred_element_type=f32)
        - coef_next * embed.astype(f32)
    ).astype(bf16)
    return (attended, grad_queries, grad_hidden, grad_embed)


def solution(mesh):
    axes = ("xh", "z", "co", "xl", "y")
    fine = Mesh(mesh.devices.reshape(2, 8, 2, 2, 4), axes)
    both = P(CTX, TP)
    placed = (
        both,
        both,
        P(TP),
        P(TP),
        P(TP, None),
        P(TP, None),
        P(),
        P(None, TP),
        P(None, TP),
        both,
        both,
    )
    return jax.shard_map(
        on_device,
        mesh=fine,
        in_specs=placed,
        out_specs=(both, both, both, both),
        check_vma=False,
    )
```

time: 730 us -> 246 us (0.34); the launches traced: 718 us -> 245 us
  waiting for transfers between devices: 293 us -> 59.7 us
  matrix products: 179 us -> 8.89 us
  other arithmetic: 96.3 us -> 14.8 us
  local copies, waits for them, and re-layouts: 107 us -> 45 us
  blocking collectives: 0 us -> 45 us
  Pallas kernels: 0 us -> 31.5 us
  between operations: 15 us -> 1.24 us
  starting transfers between devices: 25.8 us -> 38.5 us
    dot_general x129 -> x7, matrix products: 179 us -> 7.21 us  [the longest x1 1.67 us: on_device(): jnp.einsum('ghsl,lhv->gshv', o.reshape(2, HEADS, HALF, LAT), value_up_hea...]
    reduce_scatter x1 -> x0, waiting for transfers between devices: 156 us -> none  [sent_together(): lax.psum_scatter(both, axis, scatter_dimension=dim, tiled=True)]
    all_gather x1 -> x0, waiting for transfers between devices: 73.7 us -> none  [side_by_side(): lax.all_gather(both, axis, axis=dim, tiled=True)]
    all_to_all x0 -> x2, blocking collectives: none -> 45 us  [gather_copies(): return lax.all_to_all(copies, axes, split_axis=0, concat_axis=0, tiled=True)]
    dynamic_update_slice x17 -> x0, other arithmetic: 34.2 us -> none  [grad_step(): lax.dynamic_update_slice_in_dim(grad_keys, update, first_key, 0)]
    slice x31 -> x4, local copies, waits for them, and re-layouts: 34.9 us -> 1.92 us  [the longest x1 1.03 us: on_device(): embed[1:HALF]]
    pallas_call x0 -> x1, Pallas kernels: none -> 31.5 us  [attention(): pl.pallas_call(attention_kernel, in_specs=[pl.BlockSpec(memory_space=pltp...]
    reduce_sum x10 -> x8, other arithmetic: 27.7 us -> 3.51 us  [the longest x1 1.13 us: on_device(): jnp.sum(dkey.astype(f32), axis=0).astype(bf16).reshape(16, PIECE, KEYW)]
  transfers between devices with their start and end apart: 8 -> 10, of which waited for: 7 -> 8; matrix products, arithmetic and copies ran while one was open for 7% -> 14% of each run, Pallas kernels for 0% -> 0%
where the time goes in v1:
time: 246 us; the launch traced here: 245 us
  waiting for transfers between devices  59.7 us (24%)
  local copies, waits for them, and re-layouts  45 us (18%)
  blocking collectives  45 us (18%)
  starting transfers between devices  38.5 us (16%)
  Pallas kernels  31.5 us (13%)
  other arithmetic  14.8 us (6%)
  matrix products  8.89 us (4%)
    all_to_all x2, blocking collectives, gather_copies(): return lax.all_to_all(copies, axes, split_axis=0, concat_axis=0, tiled=True)  45 us
    pallas_call x1, Pallas kernels, attention(): pl.pallas_call(attention_kernel, in_specs=[pl.BlockSpec(memory_space=pltp...  31.5 us
    all_to_all x1, waiting for transfers between devices, on_device(): dkey = lax.all_to_all(dkey, TP, split_axis=0, concat_axis=0, tiled=True)  27.1 us
    ppermute x2, waiting for transfers between devices, edge_exchange(): lax.ppermute(second_row, CTX, up)  10.1 us
    ppermute x2, starting transfers between devices, edge_exchange(): lax.ppermute(first_row, CTX, down)  9.27 us
    all_to_all x1, starting transfers between devices, on_device(): dkey = lax.all_to_all(dkey, XZ, split_axis=0, concat_axis=0, tiled=True)  9.1 us
    all_to_all x1, waiting for transfers between devices, on_device(): lax.all_to_all(parts, TP, split_axis=0, concat_axis=0, tiled=True)  8.76 us
    all_to_all x1, waiting for transfers between devices, on_device(): dkey = lax.all_to_all(dkey, XZ, split_axis=0, concat_axis=0, tiled=True)  7.03 us
  transfers between devices with their start and end apart: 10, of which 8 were waited for; matrix products, arithmetic and copies ran while one was open for 14% of the time, Pallas kernels for 0%

profile of v1, /device:TPU:4, one launch (start us, length us, event | category | flops | bytes accessed | tf_op | source)
XLA Modules:
  0.0 244.7 jit_solution(12151064761799762045)
XLA Ops:
  0.7 0.9 slice.85
  1.5 7.1 %collective-permute-start = (bf16[1,896]{1,0:T(2,128)(2,1)S(1)}, bf16[1,896]{1,0:T(2,128)(2,1)S(1)}, u32[]{:S(2)}, u32[]{:S(2)}) collective-permute-start(bf16[1,896]{1,0:T(2,128)(2,1)S(1)} %slice.85), channel_id=1, source_target_pairs={{8,0},{16,8},{24,16},{32,24},{40,32},{48,40},{56,48},{64,56},{72,6... | collective-permute-start | bytes 5384 | tf_op jit(solution)/shard_map/ppermute | solution.py:72
  8.7 1.4 fusion.20
  10.1 1.0 fusion.60
  11.1 0.7 broadcast_select_fusion
  11.9 1.9 collective-permute-start.1
  13.8 1.1 fusion.18
  14.8 5.6 %collective-permute-done.1 = bf16[1,896]{1,0:T(2,128)(2,1)S(1)} collective-permute-done((bf16[1,896]{1,0:T(2,128)(2,1)S(1)}, bf16[1,896]{1,0:T(2,128)(2,1)S(1)}, u32[]{:S(2)}, u32[]{:S(2)}) %collective-permute-start.1) | collective-permute-done | bytes 1824 | tf_op jit(solution)/shard_map/ppermute | solution.py:72
  20.6 0.4 fusion.22
  21.2 1.1 copy.141
  22.2 6.0 %all-to-all-start = ((f32[8,16,1280]{2,1,0:T(8,128)}), f32[8,16,1280]{2,1,0:T(8,128)S(1)}, u32[]{:S(2)}, u32[]{:S(2)}) async-start(f32[8,16,1280]{2,1,0:T(8,128)} %bitcast.2), calls=%async_computation | async-start | bytes 1310720 | tf_op jit(solution)/shard_map/all_to_all | solution.py:278
  28.3 8.8 %all-to-all-done = f32[8,16,1280]{2,1,0:T(8,128)S(1)} async-done(((f32[8,16,1280]{2,1,0:T(8,128)}), f32[8,16,1280]{2,1,0:T(8,128)S(1)}, u32[]{:S(2)}, u32[]{:S(2)}) %all-to-all-start) | async-done | bytes 655392 | tf_op jit(solution)/shard_map/all_to_all | solution.py:278
  37.5 0.6 multiply_multiply_fusion.2
  38.4 13.8 %all_to_all.30 = bf16[16,16,576]{2,1,0:T(8,128)(2,1)S(1)} all-to-all(bf16[16,16,576]{2,1,0:T(8,128)(2,1)S(1)} %broadcast_in_dim.34), channel_id=1, replica_groups=mesh['xh'=2,'z'=8,'co'=2,'xl'=2,'y'=4] {'xh','z'}, dimensions={0} | all-to-all | bytes 589824 | tf_op jit(solution)/shard_map/all_to_all | solution.py:66
  52.4 0.5 broadcast_in_dim.36
  52.9 31.2 %all_to_all.31 = bf16[8,2,128,576]{2,3,1,0:T(8,128)(2,1)S(1)} all-to-all(bf16[8,2,128,576]{2,3,1,0:T(8,128)(2,1)S(1)} %broadcast_in_dim.36), channel_id=1, replica_groups=mesh['xh'=2,'z'=8,'co'=2,'xl'=2,'y'=4] {'xl','y'}, dimensions={0} | all-to-all | bytes 4718592 | tf_op jit(solution)/shard_map/all_to_all | solution.py:66
  84.1 2.2 reshape.133
  86.4 1.1 copy.203
  87.5 1.5 copy.179
  89.0 0.3 multiply_cosine_fusion
  89.4 0.3 subtract_convert_fusion.1
  89.7 0.5 fusion
  90.2 0.2 pad_maximum_fusion
  90.5 1.2 copy.145
  91.7 2.4 copy.146
  94.1 1.0 copy.180
  95.1 1.7 fusion.7
  96.9 1.0 copy.149
  98.0 2.3 copy.150
  100.3 0.6 pad_add_fusion.where_ref
  100.9 2.6 %copy.151.mine_ref = bf16[8,2,128,576]{3,2,1,0:T(8,128)(2,1)} copy(bf16[8,2,128,576]{2,3,1,0:T(8,128)(2,1)S(1)} %all_to_all.31) | data formatting | bytes 4718592 | tf_op jit(solution)/shard_map/all_to_all | solution.py:66
  103.4 4.3 %copy.152.other_ref = bf16[8,2,128,576]{3,2,1,0:T(8,128)(2,1)} copy(bf16[8,2,128,576]{2,3,1,0:T(8,128)(2,1)} %collective-permute-done.2) | data formatting | bytes 4718592 | tf_op jit(solution)/shard_map/ppermute | solution.py:296
  107.8 31.5 %attention.1 = (bf16[2,512,512]{2,1,0:T(8,128)(2,1)}, bf16[2,512,512]{2,1,0:T(8,128)(2,1)}, f32[2,512,64]{2,1,0:T(8,128)}, bf16[8,2,128,576]{3,2,1,0:T(8,128)(2,1)}, bf16[8,2,128,576]{3,2,1,0:T(8,128)(2,1)}) custom-call(s32[2]{0:T(128)} %pad_add_fusion.where_ref, bf16[8,2,128,576]{3,2,1,0:T(8,128)(2,1)} %copy.151.mine_ref, ...), custom_call_target="tpu_custom_call" | custom-call | flops 14000000000 | bytes 20000000 | tf_op jit(solution)/shard_map/attention/pallas_call | solution.py:206
  139.3 3.2 %copy.161 = bf16[8,2,128,576]{2,3,1,0:T(8,128)(2,1)S(1)} copy(bf16[8,2,128,576]{3,2,1,0:T(8,128)(2,1)} %get-tuple-element.13) | data formatting | bytes 4718592 | tf_op jit(solution)/shard_map/attention/pallas_call | solution.py:206
  142.5 0.8 collective-permute-start.3
  143.2 4.3 %collective-permute-done.3 = bf16[8,2,128,576]{2,3,1,0:T(8,128)(2,1)} collective-permute-done((bf16[8,2,128,576]{2,3,1,0:T(8,128)(2,1)S(1)}, bf16[8,2,128,576]{2,3,1,0:T(8,128)(2,1)}, u32[]{:S(2)}, u32[]{:S(2)}) %collective-permute-start.3) | collective-permute-done | bytes 2359328 | tf_op jit(solution)/shard_map/ppermute | solution.py:322
  147.5 4.3 %copy.162 = bf16[8,2,128,576]{3,2,1,0:T(8,128)(2,1)} copy(bf16[8,2,128,576]{2,3,1,0:T(8,128)(2,1)} %collective-permute-done.3) | data formatting | bytes 4718592 | tf_op jit(solution)/shard_map/ppermute | solution.py:322
  151.9 4.8 %add_convert_fusion = bf16[8,2,128,576]{3,2,1,0:T(8,128)(2,1)} fusion(bf16[8,2,128,576]{3,2,1,0:T(8,128)(2,1)} %copy.162, bf16[8,2,128,576]{3,2,1,0:T(8,128)(2,1)} %get-tuple-element.12), kind=kLoop, calls=%fused_computation | loop fusion | flops 4718592 | bytes 7077888 | tf_op jit(solution)/shard_map/convert_element_type | solution.py:323
  156.7 4.4 %copy.163 = bf16[8,2,128,576]{2,3,1,0:T(8,128)(2,1)} copy(bf16[8,2,128,576]{3,2,1,0:T(8,128)(2,1)} %add_convert_fusion) | data formatting | bytes 4718592 | tf_op jit(solution)/shard_map/convert_element_type | solution.py:323
  161.1 3.6 %all-to-all-start.3 = ((bf16[8,2,128,576]{2,3,1,0:T(8,128)(2,1)}), bf16[8,2,128,576]{2,3,1,0:T(8,128)(2,1)S(1)}, u32[]{:S(2)}, u32[]{:S(2)}) async-start(bf16[8,2,128,576]{2,3,1,0:T(8,128)(2,1)} %copy.163), calls=%async_computation.3 | async-start | bytes 4718592 | tf_op jit(solution)/shard_map/all_to_all | solution.py:324
  164.7 2.5 %copy.181 = bf16[64,8,8,128]{3,2,1,0:T(8,128)(2,1)} copy(bf16[64,8,8,128]{3,1,2,0:T(8,128)(2,1)} %bitcast.66) | data formatting | bytes 2097152
  167.2 27.1 %all-to-all-done.3 = bf16[8,2,128,576]{2,3,1,0:T(8,128)(2,1)S(1)} async-done(((bf16[8,2,128,576]{2,3,1,0:T(8,128)(2,1)}), bf16[8,2,128,576]{2,3,1,0:T(8,128)(2,1)S(1)}, u32[]{:S(2)}, u32[]{:S(2)}) %all-to-all-start.3) | async-done | bytes 2359328 | tf_op jit(solution)/shard_map/all_to_all | solution.py:324
  194.3 1.1 reduce_sum.88
  195.4 1.9 copy.164
  197.3 9.1 %all-to-all-start.4 = ((bf16[16,16,576]{2,1,0:T(8,128)(2,1)}), bf16[16,16,576]{2,1,0:T(8,128)(2,1)S(1)}, u32[]{:S(2)}, u32[]{:S(2)}) async-start(bf16[16,16,576]{2,1,0:T(8,128)(2,1)} %bitcast.23), calls=%async_computation.4 | async-start | bytes 655360 | tf_op jit(solution)/shard_map/all_to_all | solution.py:326
  206.4 1.5 fusion.57
  208.0 0.9 add_convert_fusion.1
  208.8 1.2 fusion.6
  210.0 7.0 %all-to-all-done.4 = bf16[16,16,576]{2,1,0:T(8,128)(2,1)S(1)} async-done(((bf16[16,16,576]{2,1,0:T(8,128)(2,1)}), bf16[16,16,576]{2,1,0:T(8,128)(2,1)S(1)}, u32[]{:S(2)}, u32[]{:S(2)}) %all-to-all-start.4) | async-done | bytes 294944 | tf_op jit(solution)/shard_map/all_to_all | solution.py:326
  217.5 0.9 multiply_reduce_fusion
  218.5 0.2 fusion.53
  219.1 0.7 broadcast_in_dim.92
  219.9 3.9 %all-to-all-start.5 = ((bf16[8,16,1280]{2,1,0:T(8,128)(2,1)}), bf16[8,16,1280]{2,1,0:T(8,128)(2,1)S(1)}, u32[]{:S(2)}, u32[]{:S(2)}) async-start(bf16[8,16,1280]{2,1,0:T(8,128)(2,1)} %broadcast_in_dim.92), calls=%async_computation.5 | async-start | bytes 655360 | tf_op jit(solution)/shard_map/all_to_all | solution.py:66
  223.7 1.2 maximum_bitcast_fusion
  224.9 0.3 copy.160
  225.2 1.2 reshape.142
  226.4 1.7 fusion.5
  228.3 0.8 copy.204
  229.1 2.1 all-to-all-done.5
  231.4 2.1 collective-permute-start.5
  233.6 1.1 fusion.4
  234.8 4.0 %collective-permute-start.4 = (bf16[1,640]{1,0:T(2,128)(2,1)S(1)}, bf16[1,640]{1,0:T(2,128)(2,1)S(1)}, u32[]{:S(2)}, u32[]{:S(2)}) collective-permute-start(bf16[1,640]{1,0:T(2,128)(2,1)S(1)} %get-tuple-element.30), channel_id=1, source_target_pairs={{0,8},{8,16},{16,24},{24,32},{32,40},{40,48},{48,56},{56,64},{64,7... | collective-permute-start | bytes 3848 | tf_op jit(solution)/shard_map/ppermute | solution.py:72
  238.9 4.5 %collective-permute-done.4 = bf16[1,640]{1,0:T(2,128)(2,1)S(1)} collective-permute-done((bf16[1,640]{1,0:T(2,128)(2,1)S(1)}, bf16[1,640]{1,0:T(2,128)(2,1)S(1)}, u32[]{:S(2)}, u32[]{:S(2)}) %collective-permute-start.4) | collective-permute-done | bytes 1312 | tf_op jit(solution)/shard_map/ppermute | solution.py:72
  243.6 1.0 fusion.3
  (91 shorter events, 3.3 us)
Async XLA Ops:
  0.6 8.0 %copy-start = (bf16[896,576]{0,1:T(8,128)(2,1)S(1)}, bf16[896,576]{0,1:T(8,128)(2,1)}, u32[]{:S(2)}) copy-start(bf16[896,576]{0,1:T(8,128)(2,1)} %param.15) | copy-start | bytes 3096580
  0.6 20.0 %copy-start.19 = (f32[896]{0:T(1024)S(1)}, f32[896]{0:T(1024)}, u32[]{:S(2)}) copy-start(f32[896]{0:T(1024)} %param.14) | copy-start | bytes 10756
  0.7 20.0 %copy-start.5 = (bf16[896,576]{0,1:T(8,128)(2,1)S(1)}, bf16[896,576]{0,1:T(8,128)(2,1)}, u32[]{:S(2)}) copy-start(bf16[896,576]{0,1:T(8,128)(2,1)} %param.16) | copy-start | bytes 3096580
  1.5 9.6 %collective-permute-start = (bf16[1,896]{1,0:T(2,128)(2,1)S(1)}, bf16[1,896]{1,0:T(2,128)(2,1)S(1)}, u32[]{:S(2)}, u32[]{:S(2)}) collective-permute-start(bf16[1,896]{1,0:T(2,128)(2,1)S(1)} %slice.85), channel_id=1, source_target_pairs={{8,0},{16,8},{24,16},{32,24},{40,32},{48,40},{56,48},{64,56},{72,6... | collective-permute-start | bytes 5384 | tf_op jit(solution)/shard_map/ppermute | solution.py:72
  11.9 8.6 %collective-permute-start.1 = (bf16[1,896]{1,0:T(2,128)(2,1)S(1)}, bf16[1,896]{1,0:T(2,128)(2,1)S(1)}, u32[]{:S(2)}, u32[]{:S(2)}) collective-permute-start(bf16[1,896]{1,0:T(2,128)(2,1)S(1)} %get-tuple-element.37), channel_id=1, source_target_pairs={{0,8},{8,16},{16,24},{24,32},{32,40},{40,48},{48,56},{56,64},{64,7... | collective-permute-start | bytes 5384 | tf_op jit(solution)/shard_map/ppermute | solution.py:72
  21.1 17.0 %copy-start.12 = (f32[512]{0:T(512)S(1)}, f32[512]{0:T(512)}, u32[]{:S(2)}) copy-start(f32[512]{0:T(512)} %param.17) | copy-start | bytes 6148
  22.2 14.8 %all-to-all-start = ((f32[8,16,1280]{2,1,0:T(8,128)}), f32[8,16,1280]{2,1,0:T(8,128)S(1)}, u32[]{:S(2)}, u32[]{:S(2)}) async-start(f32[8,16,1280]{2,1,0:T(8,128)} %bitcast.2), calls=%async_computation | async-start | bytes 1310720 | tf_op jit(solution)/shard_map/all_to_all | solution.py:278
  28.3 60.8 %copy-start.15 = (f32[32]{0:T(128)}, f32[32]{0:T(128)S(1)}, u32[]{:S(2)}) copy-start(f32[32]{0:T(128)S(1)} %multiply_power_fusion) | copy-start | bytes 388
  28.3 24.6 %copy-start.17 = (f32[16]{0:T(128)}, f32[16]{0:T(128)S(1)}, u32[]{:S(2)}) copy-start(f32[16]{0:T(128)S(1)} %fusion.55) | copy-start | bytes 196
  37.3 0.8 copy-start.14
  38.1 46.0 %copy-start.21 = (f32[16]{0:T(128)}, f32[16]{0:T(128)S(1)}, u32[]{:S(2)}) copy-start(f32[16]{0:T(128)S(1)} %get-tuple-element.47) | copy-start | bytes 196
  84.1 19.3 %collective-permute-start.2 = (bf16[8,2,128,576]{2,3,1,0:T(8,128)(2,1)S(1)}, bf16[8,2,128,576]{2,3,1,0:T(8,128)(2,1)}, u32[]{:S(2)}, u32[]{:S(2)}) collective-permute-start(bf16[8,2,128,576]{2,3,1,0:T(8,128)(2,1)S(1)} %all_to_all.31), channel_id=1, source_target_pairs={{0,8},{8,0},{1,9},{9,1},{2,10},{10,2},{3,11},{11,3},{4,12},{12,4},... | collective-permute-start | bytes 7077896 | tf_op jit(solution)/shard_map/ppermute | solution.py:296
  89.0 1.2 copy-start.1
  89.4 0.8 copy-start.8
  89.4 0.8 copy-start.10
  142.5 5.1 %collective-permute-start.3 = (bf16[8,2,128,576]{2,3,1,0:T(8,128)(2,1)S(1)}, bf16[8,2,128,576]{2,3,1,0:T(8,128)(2,1)}, u32[]{:S(2)}, u32[]{:S(2)}) collective-permute-start(bf16[8,2,128,576]{2,3,1,0:T(8,128)(2,1)S(1)} %copy.161), channel_id=1, source_target_pairs={{0,8},{8,0},{1,9},{9,1},{2,10},{10,2},{3,11},{11,3},{4,12},{12,4},... | collective-permute-start | bytes 7077896 | tf_op jit(solution)/shard_map/ppermute | solution.py:322
  161.1 33.2 %all-to-all-start.3 = ((bf16[8,2,128,576]{2,3,1,0:T(8,128)(2,1)}), bf16[8,2,128,576]{2,3,1,0:T(8,128)(2,1)S(1)}, u32[]{:S(2)}, u32[]{:S(2)}) async-start(bf16[8,2,128,576]{2,3,1,0:T(8,128)(2,1)} %copy.163), calls=%async_computation.3 | async-start | bytes 4718592 | tf_op jit(solution)/shard_map/all_to_all | solution.py:324
  195.4 12.5 %copy-start.9 = (f32[2,64,32]{2,1,0:T(8,128)S(1)}, f32[2,64,32]{2,1,0:T(8,128)}, u32[]{:S(2)}) copy-start(f32[2,64,32]{2,1,0:T(8,128)} %copy-done.8) | copy-start | bytes 49156
  195.4 12.5 %copy-start.11 = (f32[2,64,32]{2,1,0:T(8,128)S(1)}, f32[2,64,32]{2,1,0:T(8,128)}, u32[]{:S(2)}) copy-start(f32[2,64,32]{2,1,0:T(8,128)} %copy-done.10) | copy-start | bytes 49156
  197.3 11.5 %copy-start.2 = (bf16[64,8,8,128]{3,2,1,0:T(8,128)(2,1)S(1)}, bf16[64,8,8,128]{3,2,1,0:T(8,128)(2,1)}, u32[]{:S(2)}) copy-start(bf16[64,8,8,128]{3,2,1,0:T(8,128)(2,1)} %copy-done.1) | copy-start | bytes 3145732
  197.3 19.7 %all-to-all-start.4 = ((bf16[16,16,576]{2,1,0:T(8,128)(2,1)}), bf16[16,16,576]{2,1,0:T(8,128)(2,1)S(1)}, u32[]{:S(2)}, u32[]{:S(2)}) async-start(bf16[16,16,576]{2,1,0:T(8,128)(2,1)} %bitcast.23), calls=%async_computation.4 | async-start | bytes 655360 | tf_op jit(solution)/shard_map/all_to_all | solution.py:326
  206.4 2.4 copy-start.24
  207.9 9.3 %copy-start.16 = (f32[32]{0:T(128)S(1)}, f32[32]{0:T(128)}, u32[]{:S(2)}) copy-start(f32[32]{0:T(128)} %copy-done.15) | copy-start | bytes 388
  208.0 9.3 %copy-start.18 = (f32[16]{0:T(128)S(1)}, f32[16]{0:T(128)}, u32[]{:S(2)}) copy-start(f32[16]{0:T(128)} %copy-done.17) | copy-start | bytes 196
  208.0 9.4 %copy-start.22 = (f32[16]{0:T(128)S(1)}, f32[16]{0:T(128)}, u32[]{:S(2)}) copy-start(f32[16]{0:T(128)} %copy-done.21) | copy-start | bytes 196
  208.0 9.4 %copy-start.23 = (f32[16]{0:T(128)S(1)}, f32[16]{0:T(128)}, u32[]{:S(2)}) copy-start(f32[16]{0:T(128)} %get-tuple-element.46) | copy-start | bytes 196
  217.5 9.0 %copy-start.4 = (bf16[64,8,8,128]{3,2,1,0:T(8,128)(2,1)S(1)}, bf16[64,8,8,128]{3,2,1,0:T(8,128)(2,1)}, u32[]{:S(2)}) copy-start(bf16[64,8,8,128]{3,2,1,0:T(8,128)(2,1)} %copy.181) | copy-start | bytes 3145732
  219.9 11.3 %all-to-all-start.5 = ((bf16[8,16,1280]{2,1,0:T(8,128)(2,1)}), bf16[8,16,1280]{2,1,0:T(8,128)(2,1)S(1)}, u32[]{:S(2)}, u32[]{:S(2)}) async-start(bf16[8,16,1280]{2,1,0:T(8,128)(2,1)} %broadcast_in_dim.92), calls=%async_computation.5 | async-start | bytes 655360 | tf_op jit(solution)/shard_map/all_to_all | solution.py:66
  225.2 8.3 %copy-start.3 = (bf16[128,896]{1,0:T(8,128)(2,1)S(1)}, bf16[128,896]{1,0:T(8,128)(2,1)}, u32[]{:S(2)}) copy-start(bf16[128,896]{1,0:T(8,128)(2,1)} %param.11) | copy-start | bytes 688132
  225.2 8.3 %copy-start.13 = (f32[896]{0:T(1024)S(1)}, f32[896]{0:T(1024)}, u32[]{:S(2)}) copy-start(f32[896]{0:T(1024)} %param.13) | copy-start | bytes 10756
  228.1 15.5 %copy-start.6 = (bf16[896,576]{0,1:T(8,128)(2,1)S(1)}, bf16[896,576]{0,1:T(8,128)(2,1)}, u32[]{:S(2)}) copy-start(bf16[896,576]{0,1:T(8,128)(2,1)} %param.16) | copy-start | bytes 3096580
  228.1 15.5 %copy-start.7 = (bf16[128,896]{1,0:T(8,128)(2,1)S(1)}, bf16[128,896]{1,0:T(8,128)(2,1)}, u32[]{:S(2)}) copy-start(bf16[128,896]{1,0:T(8,128)(2,1)} %param.12) | copy-start | bytes 688132
  228.1 15.5 %copy-start.20 = (f32[896]{0:T(1024)S(1)}, f32[896]{0:T(1024)}, u32[]{:S(2)}) copy-start(f32[896]{0:T(1024)} %param.14) | copy-start | bytes 10756
  231.4 3.4 %collective-permute-start.5 = (bf16[1,640]{1,0:T(2,128)(2,1)S(1)}, bf16[1,640]{1,0:T(2,128)(2,1)S(1)}, u32[]{:S(2)}, u32[]{:S(2)}) collective-permute-start(bf16[1,640]{1,0:T(2,128)(2,1)S(1)} %slice.118), channel_id=1, source_target_pairs={{8,0},{16,8},{24,16},{32,24},{40,32},{48,40},{56,48},{64,56},{72,6... | collective-permute-start | bytes 3848 | tf_op jit(solution)/shard_map/ppermute | solution.py:72
  234.8 8.5 %collective-permute-start.4 = (bf16[1,640]{1,0:T(2,128)(2,1)S(1)}, bf16[1,640]{1,0:T(2,128)(2,1)S(1)}, u32[]{:S(2)}, u32[]{:S(2)}) collective-permute-start(bf16[1,640]{1,0:T(2,128)(2,1)S(1)} %get-tuple-element.30), channel_id=1, source_target_pairs={{0,8},{8,16},{16,24},{24,32},{32,40},{40,48},{48,56},{56,64},{64,7... | collective-permute-start | bytes 3848 | tf_op jit(solution)/shard_map/ppermute | solution.py:72

commit v2 on v1

--- a/solution.py
+++ b/solution.py
@@ -72,20 +72,36 @@
     return lax.ppermute(first_row, CTX, down), lax.ppermute(second_row, CTX, up)
 
 
+def pack_keys(rows):
+    lead = rows[..., :LAT].reshape(2, 128, 4, 128).transpose(0, 2, 1, 3).reshape(8, 128, 128)
+    rope = jnp.concatenate([rows[0, :, LAT:KEYW], rows[1, :, LAT:KEYW]], axis=1)
+    return jnp.concatenate([lead, rope[None]], axis=0)
+
+
+def unpack_keys(tiles):
+    lead = tiles[:8].reshape(2, 4, 128, 128).transpose(0, 2, 1, 3).reshape(2, 128, LAT)
+    rope = jnp.stack([tiles[8, :, :ROPE], tiles[8, :, ROPE:]], axis=0)
+    return jnp.concatenate([lead, rope, jnp.zeros_like(rope)], axis=2)
+
+
 def attention_kernel(
     where_ref,
     mine_ref,
     other_ref,
+    q_hbm,
+    qt_hbm,
+    g_hbm,
+    gt_hbm,
+    ot_hbm,
+    leadt_hbm,
+    tailt_hbm,
+    dmine_ref,
+    dother_ref,
+    keys,
     q_ref,
     qt_ref,
     g_ref,
     gt_ref,
-    o_ref,
-    lead_ref,
-    tail_ref,
-    dmine_ref,
-    dother_ref,
-    keys,
     s_buf,
     dp_buf,
     m_buf,
@@ -93,14 +109,27 @@
     a_buf,
     ot_buf,
     dqt_buf,
+    ot_out,
+    lead_out,
     dk_buf,
+    dk_out,
     sems,
+    out_sems,
 ):
     ctx = where_ref[0]
     core = where_ref[1]
     copies = [
-        pltpu.make_async_copy(mine_ref, keys.at[core], sems.at[0]),
-        pltpu.make_async_copy(other_ref, keys.at[1 - core], sems.at[1]),
+        pltpu.make_async_copy(source, target, sems.at[n])
+        for n, (source, target) in enumerate(
+            [
+                (mine_ref, keys.at[core]),
+                (qt_hbm, qt_ref),
+                (gt_hbm, gt_ref),
+                (other_ref, keys.at[1 - core]),
+                (q_hbm, q_ref),
+                (g_hbm, g_ref),
+            ]
+        )
     ]
     for copy in copies:
         copy.start()
@@ -109,8 +138,14 @@
     a_buf[...] = jnp.zeros_like(a_buf)
     ot_buf[...] = jnp.zeros_like(ot_buf)
     dqt_buf[...] = jnp.zeros_like(dqt_buf)
-    dk_buf[...] = jnp.zeros_like(dk_buf)
-    for copy in copies:
+
+    def clear(t, carry):
+        dk_buf[0, t] = jnp.zeros((9, 128, 128), f32)
+        dk_buf[1, t] = jnp.zeros((9, 128, 128), f32)
+        return carry
+
+    lax.fori_loop(0, N_TP, clear, 0)
+    for copy in copies[:4]:
         copy.wait()
 
     group = ctx // 8
@@ -126,14 +161,20 @@
     def slab(half, block):
         xh = block // 2
         at = pl.multiple_of((block % 2) * 64, 64)
-        return jnp.concatenate(
-            [
-                keys[co, half * 4 + y, xh, pl.ds(at, 64), :]
-                for co in range(2)
-                for y in range(4)
-            ],
-            axis=0,
-        )
+
+        def tile(part):
+            return jnp.concatenate(
+                [
+                    keys[co, half * 4 + y, part, pl.ds(at, 64), :]
+                    for co in range(2)
+                    for y in range(4)
+                ],
+                axis=0,
+            )
+
+        rope = tile(8)
+        rope = jnp.where(xh == 0, rope[:, :ROPE], rope[:, ROPE:])
+        return jnp.concatenate([tile(xh * 4 + c) for c in range(4)] + [rope], axis=1)
 
     def nn(a, b):
         return jnp.dot(a, b, preferred_element_type=f32)
@@ -162,6 +203,8 @@
         return carry
 
     lax.fori_loop(0, STEPS, first, 0)
+    for copy in copies[4:]:
+        copy.wait()
 
     def second(i, carry):
         seg, half, block = locate(i)
@@ -177,45 +220,64 @@
         tail = nn(ds, q_ref[seg, :, LAT:])
         xh = block // 2
         at = pl.multiple_of((block % 2) * 64, 64)
+        lane = lax.broadcasted_iota(jnp.int32, (1, 128), 1)
+        tail = jnp.where(lane // ROPE == xh, jnp.concatenate([tail, tail], axis=1), 0.0)
         for co in range(2):
             for y in range(4):
                 j = (co * 4 + y) * 64
-                dk_buf[co, half * 4 + y, xh, pl.ds(at, 64), :LAT] += lead[j : j + 64]
-                dk_buf[co, half * 4 + y, xh, pl.ds(at, 64), LAT:] += tail[j : j + 64]
+                own = half * 4 + y
+                for c in range(4):
+                    dk_buf[co, own, xh * 4 + c, pl.ds(at, 64), :] += lead[
+                        j : j + 64, c * 128 : c * 128 + 128
+                    ]
+                dk_buf[co, own, 8, pl.ds(at, 64), :] += tail[j : j + 64]
         return carry
 
     lax.fori_loop(0, STEPS, second, 0)
 
+    sends = []
+
+    def send(source, target):
+        copy = pltpu.make_async_copy(source, target, out_sems.at[len(sends)])
+        copy.start()
+        sends.append(copy)
+
+    send(dqt_buf.at[:, pl.ds(LAT, ROPE)], tailt_hbm)
+    for t in range(N_TP):
+        dk_out[0, t] = dk_buf[1 - core, t].astype(bf16)
+        send(dk_out.at[0, t], dother_ref.at[t])
+    for t in range(N_TP):
+        dk_out[1, t] = dk_buf[core, t].astype(bf16)
+        send(dk_out.at[1, t], dmine_ref.at[t])
     for seg in range(2):
-        o_ref[seg] = ot_buf[seg].astype(bf16).T
-        lead_ref[seg] = dqt_buf[seg, :LAT].astype(bf16).T
-        tail_ref[seg] = dqt_buf[seg, LAT:].T
-
-    def put(t, carry):
-        dmine_ref[t] = dk_buf[core, t].astype(bf16)
-        dother_ref[t] = dk_buf[1 - core, t].astype(bf16)
-        return carry
-
-    lax.fori_loop(0, N_TP, put, 0)
+        ot_out[seg] = ot_buf[seg].astype(bf16)
+        send(ot_out.at[seg], ot_hbm.at[seg])
+        lead_out[seg] = dqt_buf[seg, :LAT].astype(bf16)
+        send(lead_out.at[seg], leadt_hbm.at[seg])
+    for copy in sends:
+        copy.wait()
 
 
 def attention(where, mine, other, q, qt, g, gt):
-    vmem = pl.BlockSpec(memory_space=pltpu.VMEM)
     hbm = pl.BlockSpec(memory_space=pl.ANY)
-    half_keys = (N_TP, 2, 128, KEYW)
+    half_keys = (N_TP, 9, 128, 128)
     return pl.pallas_call(
         attention_kernel,
-        in_specs=[pl.BlockSpec(memory_space=pltpu.SMEM), hbm, hbm, vmem, vmem, vmem, vmem],
-        out_specs=[vmem] * 5,
+        in_specs=[pl.BlockSpec(memory_space=pltpu.SMEM)] + [hbm] * 6,
+        out_specs=[hbm] * 5,
         out_shape=[
-            jax.ShapeDtypeStruct((2, SEG, LAT), bf16),
-            jax.ShapeDtypeStruct((2, SEG, LAT), bf16),
-            jax.ShapeDtypeStruct((2, SEG, ROPE), f32),
+            jax.ShapeDtypeStruct((2, LAT, SEG), bf16),
+            jax.ShapeDtypeStruct((2, LAT, SEG), bf16),
+            jax.ShapeDtypeStruct((2, ROPE, SEG), f32),
             jax.ShapeDtypeStruct(half_keys, bf16),
             jax.ShapeDtypeStruct(half_keys, bf16),
         ],
         scratch_shapes=[
             pltpu.VMEM((2,) + half_keys, bf16),
+            pltpu.VMEM((2, SEG, KEYW), bf16),
+            pltpu.VMEM((2, KEYW, SEG), bf16),
+            pltpu.VMEM((2, SEG, LAT), bf16),
+            pltpu.VMEM((2, LAT, SEG), bf16),
             pltpu.VMEM((STEPS, BLOCK, SEG), f32),
             pltpu.VMEM((STEPS, BLOCK, SEG), f32),
             pltpu.VMEM((2, 1, SEG), f32),
@@ -223,10 +285,14 @@
             pltpu.VMEM((2, 1, SEG), f32),
             pltpu.VMEM((2, LAT, SEG), f32),
             pltpu.VMEM((2, KEYW, SEG), f32),
+            pltpu.VMEM((2, LAT, SEG), bf16),
+            pltpu.VMEM((2, LAT, SEG), bf16),
             pltpu.VMEM((2,) + half_keys, f32),
-            pltpu.SemaphoreType.DMA((2,)),
+            pltpu.VMEM((2,) + half_keys, bf16),
+            pltpu.SemaphoreType.DMA((6,)),
+            pltpu.SemaphoreType.DMA((21,)),
         ],
-        compiler_params=pltpu.CompilerParams(vmem_limit_bytes=62 * 1024 * 1024),
+        compiler_params=pltpu.CompilerParams(vmem_limit_bytes=58 * 1024 * 1024),
         cost_estimate=pl.CostEstimate(
             flops=14_000_000_000, bytes_accessed=20_000_000, transcendentals=4_000_000
         ),
@@ -275,8 +341,31 @@
         ],
         axis=1,
     ).reshape(N_TP, PIECE, 2 * WIDE)
-    parts = jnp.sum(lax.all_to_all(parts, TP, split_axis=0, concat_axis=0, tiled=True), axis=0)
-
+    parts = lax.all_to_all(parts, TP, split_axis=0, concat_axis=0, tiled=True)
+
+    cos_table, sin_table = rotation(row_positions(ctx, jnp.arange(ROWS)))
+    cos_table = cos_table.reshape(2, 1, HALF, ROPE // 2)
+    sin_table = sin_table.reshape(2, 1, HALF, ROPE // 2)
+    key_up_heads = key_up.reshape(LAT, HEADS, NOPE)
+    value_up_heads = value_up.reshape(LAT, HEADS, VDIM)
+    query_heads = queries.reshape(2, HALF, HEADS, NOPE + ROPE).transpose(0, 2, 1, 3)
+    query_rot = rotate_pairs(query_heads[..., NOPE:].astype(f32), cos_table, sin_table)
+    query_latent = jnp.einsum(
+        "ghsn,lhn->ghsl", query_heads[..., :NOPE], key_up_heads, preferred_element_type=f32
+    )
+    q = jnp.concatenate([query_latent.astype(bf16), query_rot.astype(bf16)], axis=3)
+    q = q.reshape(2, SEG, KEYW)
+    g = jnp.einsum(
+        "gshv,lhv->ghsl",
+        grad_out.reshape(2, HALF, HEADS, VDIM),
+        value_up_heads,
+        preferred_element_type=f32,
+    )
+    g = g.astype(bf16).reshape(2, SEG, LAT)
+    qt, gt = q.swapaxes(1, 2), g.swapaxes(1, 2)
+
+    parts, q, qt, g, gt = lax.optimization_barrier((parts, q, qt, g, gt))
+    parts = jnp.sum(parts, axis=0)
     part_hidden, part_next = parts[:, :KEYW], parts[:, WIDE : WIDE + KEYW]
     inv_hidden = lax.rsqrt(parts[:, KEYW : KEYW + 1] / D + EPSILON)
     inv_next = lax.rsqrt(parts[:, WIDE + KEYW : WIDE + KEYW + 1] / D + EPSILON)
@@ -288,58 +377,42 @@
         [
             (leading * inv_latent * gain_latent).astype(bf16),
             rotate_pairs(latent[:, LAT:], piece_cos, piece_sin).astype(bf16),
+            jnp.zeros((PIECE, WIDE - KEYW), bf16),
         ],
         axis=1,
     )
-    same = gather_copies(key_piece, XZ, 16).reshape(2, 128, KEYW)
-    mine = gather_copies(same, TP, N_TP).reshape(N_TP, 2, 128, KEYW)
+    same = pack_keys(gather_copies(key_piece, XZ, 16).reshape(2, 128, WIDE))
+    mine = gather_copies(same, TP, N_TP)
     other = lax.ppermute(mine, "co", [(0, 1), (1, 0)])
 
-    cos_table, sin_table = rotation(row_positions(ctx, jnp.arange(ROWS)))
-    cos_table = cos_table.reshape(2, 1, HALF, ROPE // 2)
-    sin_table = sin_table.reshape(2, 1, HALF, ROPE // 2)
-    key_up_heads = key_up.reshape(LAT, HEADS, NOPE)
-    value_up_heads = value_up.reshape(LAT, HEADS, VDIM)
-    query_heads = queries.reshape(2, HALF, HEADS, NOPE + ROPE).transpose(0, 2, 1, 3)
-    query_rot = rotate_pairs(query_heads[..., NOPE:].astype(f32), cos_table, sin_table)
-    query_latent = jnp.einsum(
-        "ghsn,lhn->ghsl", query_heads[..., :NOPE], key_up_heads, preferred_element_type=f32
-    )
-    q = jnp.concatenate([query_latent.astype(bf16), query_rot.astype(bf16)], axis=3)
-    q = q.reshape(2, SEG, KEYW)
-    g = jnp.einsum(
-        "gshv,lhv->ghsl",
-        grad_out.reshape(2, HALF, HEADS, VDIM),
-        value_up_heads,
-        preferred_element_type=f32,
-    )
-    g = g.astype(bf16).reshape(2, SEG, LAT)
     where = jnp.stack([ctx, core]).astype(jnp.int32)
-    o, lead, tail, dmine, dother = attention(
-        where, mine, other, q, q.swapaxes(1, 2), g, g.swapaxes(1, 2)
+    ot, leadt, tailt, dmine, dother = attention(
+        where, mine, other, q, qt, g, gt
     )
 
     received = lax.ppermute(dother, "co", [(0, 1), (1, 0)])
     dkey = (dmine.astype(f32) + received.astype(f32)).astype(bf16)
     dkey = lax.all_to_all(dkey, TP, split_axis=0, concat_axis=0, tiled=True)
-    dkey = jnp.sum(dkey.astype(f32), axis=0).astype(bf16).reshape(16, PIECE, KEYW)
+    dkey = unpack_keys(jnp.sum(dkey.astype(f32), axis=0).astype(bf16)).reshape(16, PIECE, WIDE)
     dkey = lax.all_to_all(dkey, XZ, split_axis=0, concat_axis=0, tiled=True)
-    dkey = jnp.sum(dkey.astype(f32), axis=0)
+    dkey = jnp.sum(dkey.astype(f32), axis=0)[:, :KEYW]
 
     attended = jnp.einsum(
-        "ghsl,lhv->gshv",
-        o.reshape(2, HEADS, HALF, LAT),
+        "glhs,lhv->gshv",
+        ot.reshape(2, LAT, HEADS, HALF),
         value_up_heads,
         preferred_element_type=f32,
     )
     attended = attended.astype(bf16).reshape(ROWS, HEADS * VDIM)
     grad_nope = jnp.einsum(
-        "ghsl,lhn->ghsn",
-        lead.reshape(2, HEADS, HALF, LAT),
+        "glhs,lhn->ghsn",
+        leadt.reshape(2, LAT, HEADS, HALF),
         key_up_heads,
         preferred_element_type=f32,
     )
-    grad_rope = unrotate(tail.reshape(2, HEADS, HALF, ROPE), cos_table, sin_table)
+    grad_rope = unrotate(
+        tailt.reshape(2, ROPE, HEADS, HALF).transpose(0, 2, 3, 1), cos_table, sin_table
+    )
     grad_queries = jnp.concatenate([grad_nope, grad_rope], axis=3).astype(bf16)
     grad_queries = grad_queries.transpose(0, 2, 1, 3).reshape(ROWS, HEADS * (NOPE + ROPE))
 

time: 246 us -> 227 us (0.923)
  blocking collectives: 45 us -> 81.2 us
  waiting for transfers between devices: 59.7 us -> 23.9 us
  local copies, waits for them, and re-layouts: 45 us -> 26.5 us
  starting transfers between devices: 38.5 us -> 35.2 us
  other arithmetic: 14.8 us -> 18 us
    all_to_all x0 -> x1, blocking collectives: none -> 32.7 us  [on_device(): dkey = lax.all_to_all(dkey, TP, split_axis=0, concat_axis=0, tiled=True)]
    all_to_all x2 -> x1, waiting for transfers between devices: 35.9 us -> 6.78 us  [on_device(): parts = lax.all_to_all(parts, TP, split_axis=0, concat_axis=0, tiled=True)]
    ppermute x2 -> x0, local copies, waits for them, and re-layouts: 8.7 us -> none  [the longest x1 4.35 us: on_device(): received = lax.ppermute(dother, 'co', [(0, 1), (1, 0)])]
    all_to_all x1, waiting for transfers between devices: 7.03 us -> 0.8 us  [on_device(): dkey = lax.all_to_all(dkey, XZ, split_axis=0, concat_axis=0, tiled=True)]
    convert_element_type x1 -> x0, local copies, waits for them, and re-layouts: 4.36 us -> none  [on_device(): dkey = (dmine.astype(f32) + received.astype(f32)).astype(bf16)]
    ppermute x2, waiting for transfers between devices: 10.1 us -> 6.13 us  [edge_exchange(): lax.ppermute(second_row, CTX, up)]
    ppermute x1, waiting for transfers between devices: 0.01 us -> 3.87 us  [on_device(): other = lax.ppermute(mine, 'co', [(0, 1), (1, 0)])]
    all_to_all x2 -> x1, starting transfers between devices: 9.62 us -> 6 us  [on_device(): parts = lax.all_to_all(parts, TP, split_axis=0, concat_axis=0, tiled=True)]
  transfers between devices with their start and end apart: 10 -> 9, of which waited for: 8 -> 8; matrix products, arithmetic and copies ran while one was open for 14% -> 13% of each run, Pallas kernels for 0% -> 0%
where the time goes in v2:
time: 227 us; the launch traced here: 226 us
  blocking collectives  81.2 us (36%)
  starting transfers between devices  35.2 us (16%)
  Pallas kernels  29.8 us (13%)
  local copies, waits for them, and re-layouts  26.5 us (12%)
  waiting for transfers between devices  23.9 us (11%)
  other arithmetic  18 us (8%)
  matrix products  9.59 us (4%)
    all_to_all x2, blocking collectives, gather_copies(): return lax.all_to_all(copies, axes, split_axis=0, concat_axis=0, tiled=True)  48.5 us
    all_to_all x1, blocking collectives, on_device(): dkey = lax.all_to_all(dkey, TP, split_axis=0, concat_axis=0, tiled=True)  32.7 us
    pallas_call x1, Pallas kernels, attention(): pl.pallas_call(attention_kernel, in_specs=[pl.BlockSpec(memory_space=pltp...  29.8 us
    all_to_all x1, starting transfers between devices, on_device(): dkey = lax.all_to_all(dkey, XZ, split_axis=0, concat_axis=0, tiled=True)  9.16 us
    ppermute x2, starting transfers between devices, edge_exchange(): lax.ppermute(first_row, CTX, down)  9.06 us
    all_to_all x1, waiting for transfers between devices, on_device(): parts = lax.all_to_all(parts, TP, split_axis=0, concat_axis=0, tiled=True)  6.78 us
    ppermute x2, waiting for transfers between devices, edge_exchange(): lax.ppermute(second_row, CTX, up)  6.13 us
    ppermute x2, starting transfers between devices, edge_exchange(): lax.ppermute(second_row, CTX, up)  6.06 us
  transfers between devices with their start and end apart: 9, of which 8 were waited for; matrix products, arithmetic and copies ran while one was open for 13% of the time, Pallas kernels for 0%

profile of v2, /device:TPU:4, one launch (start us, length us, event | category | flops | bytes accessed | tf_op | source)
XLA Modules:
  0.0 225.6 jit_solution(1214470491661790771)
XLA Ops:
  0.7 0.9 slice.120
  1.5 7.1 %collective-permute-start = (bf16[1,896]{1,0:T(2,128)(2,1)S(1)}, bf16[1,896]{1,0:T(2,128)(2,1)S(1)}, u32[]{:S(2)}, u32[]{:S(2)}) collective-permute-start(bf16[1,896]{1,0:T(2,128)(2,1)S(1)} %slice.120), channel_id=1, source_target_pairs={{8,0},{16,8},{24,16},{32,24},{40,32},{48,40},{56,48},{64,56},{72,6... | collective-permute-start | bytes 5384 | tf_op jit(solution)/shard_map/ppermute | solution.py:72
  8.7 1.7 fusion.61
  10.4 1.4 reshape.146
  12.0 0.3 copy.121
  12.3 0.5 fusion
  12.8 0.3 multiply_cosine_fusion
  13.4 1.1 fusion.20
  14.6 1.3 pad_maximum_fusion
  15.9 0.7 broadcast_select_fusion
  16.6 1.9 collective-permute-start.1
  18.7 1.4 copy.93
  20.2 1.4 copy.94
  21.6 1.0 copy.122
  22.6 0.8 copy.96
  23.4 1.8 collective-permute-done.1
  25.2 1.0 fusion.16
  26.2 1.3 fusion.22
  27.7 1.1 copy.90
  28.8 6.0 %all-to-all-start = ((f32[8,16,1280]{2,1,0:T(8,128)}), f32[8,16,1280]{2,1,0:T(8,128)}, u32[]{:S(2)}, u32[]{:S(2)}) async-start(f32[8,16,1280]{2,1,0:T(8,128)} %bitcast.2), calls=%async_computation | async-start | bytes 1310720 | tf_op jit(solution)/shard_map/all_to_all | solution.py:344
  34.8 0.4 fusion.7
  35.5 1.3 copy.98
  36.9 6.8 %all-to-all-done = f32[8,16,1280]{2,1,0:T(8,128)} async-done(((f32[8,16,1280]{2,1,0:T(8,128)}), f32[8,16,1280]{2,1,0:T(8,128)}, u32[]{:S(2)}, u32[]{:S(2)}) %all-to-all-start) | async-done | bytes 655392 | tf_op jit(solution)/shard_map/all_to_all | solution.py:344
  43.7 1.1 reduce_sum.86
  45.2 0.6 multiply_multiply_fusion.2
  46.1 17.7 %all_to_all.30 = bf16[16,16,640]{2,1,0:T(8,128)(2,1)S(1)} all-to-all(bf16[16,16,640]{2,1,0:T(8,128)(2,1)S(1)} %broadcast_in_dim.39), channel_id=1, replica_groups=mesh['xh'=2,'z'=8,'co'=2,'xl'=2,'y'=4] {'xh','z'}, dimensions={0} | all-to-all | bytes 655360 | tf_op jit(solution)/shard_map/all_to_all | solution.py:66
  64.0 0.6 broadcast_in_dim.41
  64.6 30.8 %all_to_all.31.mine_ref = bf16[8,9,128,128]{3,2,1,0:T(8,128)(2,1)S(1)} all-to-all(bf16[8,9,128,128]{3,2,1,0:T(8,128)(2,1)S(1)} %broadcast_in_dim.41), channel_id=1, replica_groups=mesh['xh'=2,'z'=8,'co'=2,'xl'=2,'y'=4] {'xl','y'}, dimensions={0} | all-to-all | bytes 4718592 | tf_op jit(solution)/shard_map/all_to_all | solution.py:66
  95.5 0.7 pad_add_fusion.where_ref
  96.1 3.9 %collective-permute-done.2.other_ref = bf16[8,9,128,128]{3,2,1,0:T(8,128)(2,1)S(1)} collective-permute-done((bf16[8,9,128,128]{3,2,1,0:T(8,128)(2,1)S(1)}, bf16[8,9,128,128]{3,2,1,0:T(8,128)(2,1)S(1)}, u32[]{:S(2)}, u32[]{:S(2)}) %collective-permute-start.2) | collective-permute-done | bytes 2359328 | tf_op jit(solution)/shard_map/ppermute | solution.py:386
  100.0 1.4 copy-done.34
  101.4 29.8 %attention.1 = (bf16[2,512,512]{2,1,0:T(8,128)(2,1)}, bf16[2,512,512]{2,1,0:T(8,128)(2,1)}, f32[2,64,512]{2,1,0:T(8,128)}, bf16[8,9,128,128]{3,2,1,0:T(8,128)(2,1)}, bf16[8,9,128,128]{3,2,1,0:T(8,128)(2,1)}) custom-call(s32[2]{0:T(128)} %pad_add_fusion.where_ref, bf16[8,9,128,128]{3,2,1,0:T(8,128)(2,1)} %copy-done.7, bf16[8,9,128,128]{3,2,1,0:T(8,128)(2,1)} %copy-done.34, ...), custom_call_target="tpu_custom_call" | custom-call | flops 14000000000 | bytes 20000000 | tf_op jit(solution)/shard_map/attention/pallas_call | solution.py:264
  131.5 4.6 %collective-permute-done.3 = bf16[8,9,128,128]{3,2,1,0:T(8,128)(2,1)S(1)} collective-permute-done((bf16[8,9,128,128]{3,2,1,0:T(8,128)(2,1)}, bf16[8,9,128,128]{3,2,1,0:T(8,128)(2,1)S(1)}, u32[]{:S(2)}, u32[]{:S(2)}) %collective-permute-start.3) | collective-permute-done | bytes 2359328 | tf_op jit(solution)/shard_map/ppermute | solution.py:393
  136.1 2.9 %add_convert_fusion = bf16[8,9,128,128]{3,2,1,0:T(8,128)(2,1)S(1)} fusion(bf16[8,9,128,128]{3,2,1,0:T(8,128)(2,1)S(1)} %collective-permute-done.3, bf16[8,9,128,128]{3,2,1,0:T(8,128)(2,1)} %get-tuple-element.22), kind=kLoop, calls=%fused_computation | loop fusion | flops 4718592 | bytes 7077888 | tf_op jit(solution)/shard_map/convert_element_type | solution.py:394
  139.0 32.7 %all_to_all.32 = bf16[8,9,128,128]{3,2,1,0:T(8,128)(2,1)S(1)} all-to-all(bf16[8,9,128,128]{3,2,1,0:T(8,128)(2,1)S(1)} %add_convert_fusion), channel_id=1, replica_groups=mesh['xh'=2,'z'=8,'co'=2,'xl'=2,'y'=4] {'xl','y'}, dimensions={0} | all-to-all | bytes 4718592 | tf_op jit(solution)/shard_map/all_to_all | solution.py:395
  171.7 1.2 reduce_sum.88
  172.9 1.1 slice.162
  174.0 1.5 fusion.60
  175.5 0.9 copy.108
  176.4 1.1 concatenate.56
  177.5 0.8 pad_maximum_fusion.6
  178.3 0.8 maximum_maximum_fusion
  179.1 9.2 %all-to-all-start.4 = ((bf16[16,16,640]{2,1,0:T(8,128)(2,1)}), bf16[16,16,640]{2,1,0:T(8,128)(2,1)S(1)}, u32[]{:S(2)}, u32[]{:S(2)}) async-start(bf16[16,16,640]{2,1,0:T(8,128)(2,1)} %maximum_maximum_fusion), calls=%async_computation.4 | async-start | bytes 655360 | tf_op jit(solution)/shard_map/all_to_all | solution.py:397
  188.2 1.2 copy.123
  189.5 1.3 copy.103
  190.8 1.1 reshape.156
  192.2 1.9 add_convert_fusion.1
  194.1 2.4 %fusion.6 = bf16[2,8,64,128]{3,2,0,1:T(8,128)(2,1)} fusion(bf16[2,512,8,64]{1,3,2,0:T(8,128)(2,1)} %bitcast.95, bf16[512,8,128,1]{2,1,0,3:T(8,128)(2,1)S(1)} %bitcast.79), kind=kOutput, calls=%fused_computation.13 | convolution fusion | flops 134348800 | bytes 2359296 | tf_op jit(solution)/shard_map/glhs,lhn->ghsn/dot_general | solution.py:407
  196.5 0.8 all-to-all-done.4
  197.7 0.9 multiply_reduce_fusion
  199.4 0.8 broadcast_in_dim.102
  200.2 4.7 %all-to-all-start.5 = ((bf16[8,16,1280]{2,1,0:T(8,128)(2,1)}), bf16[8,16,1280]{2,1,0:T(8,128)(2,1)S(1)}, u32[]{:S(2)}, u32[]{:S(2)}) async-start(bf16[8,16,1280]{2,1,0:T(8,128)(2,1)} %broadcast_in_dim.102), calls=%async_computation.5 | async-start | bytes 655360 | tf_op jit(solution)/shard_map/all_to_all | solution.py:66
  204.9 1.3 maximum_bitcast_fusion
  206.1 0.3 copy.107
  206.4 1.2 reshape.157
  207.6 0.5 copy.99
  208.2 1.7 fusion.5
  210.1 0.8 copy.142
  210.9 1.5 all-to-all-done.5
  212.5 1.9 collective-permute-start.5
  214.5 1.1 fusion.4
  215.8 4.1 %collective-permute-start.4 = (bf16[1,640]{1,0:T(2,128)(2,1)S(1)}, bf16[1,640]{1,0:T(2,128)(2,1)S(1)}, u32[]{:S(2)}, u32[]{:S(2)}) collective-permute-start(bf16[1,640]{1,0:T(2,128)(2,1)S(1)} %get-tuple-element.38), channel_id=1, source_target_pairs={{0,8},{8,16},{16,24},{24,32},{32,40},{40,48},{48,56},{56,64},{64,7... | collective-permute-start | bytes 3848 | tf_op jit(solution)/shard_map/ppermute | solution.py:72
  220.0 4.3 %collective-permute-done.4 = bf16[1,640]{1,0:T(2,128)(2,1)S(1)} collective-permute-done((bf16[1,640]{1,0:T(2,128)(2,1)S(1)}, bf16[1,640]{1,0:T(2,128)(2,1)S(1)}, u32[]{:S(2)}, u32[]{:S(2)}) %collective-permute-start.4) | collective-permute-done | bytes 1312 | tf_op jit(solution)/shard_map/ppermute | solution.py:72
  224.6 1.1 fusion.3
  (119 shorter events, 4.5 us)
Async XLA Ops:
  0.6 12.8 %copy-start = (bf16[896,576]{0,1:T(8,128)(2,1)S(1)}, bf16[896,576]{0,1:T(8,128)(2,1)}, u32[]{:S(2)}) copy-start(bf16[896,576]{0,1:T(8,128)(2,1)} %param.15) | copy-start | bytes 3096580
  0.6 11.3 %copy-start.11 = (bf16[512,1024]{1,0:T(8,128)(2,1)S(1)}, bf16[512,1024]{1,0:T(8,128)(2,1)}, u32[]{:S(2)}) copy-start(bf16[512,1024]{1,0:T(8,128)(2,1)} %param.18) | copy-start | bytes 3145732
  1.5 14.4 %collective-permute-start = (bf16[1,896]{1,0:T(2,128)(2,1)S(1)}, bf16[1,896]{1,0:T(2,128)(2,1)S(1)}, u32[]{:S(2)}, u32[]{:S(2)}) collective-permute-start(bf16[1,896]{1,0:T(2,128)(2,1)S(1)} %slice.120), channel_id=1, source_target_pairs={{8,0},{16,8},{24,16},{32,24},{40,32},{48,40},{56,48},{64,56},{72,6... | collective-permute-start | bytes 5384 | tf_op jit(solution)/shard_map/ppermute | solution.py:72
  12.3 2.3 %copy-start.4 = (bf16[64,8,8,128]{3,2,1,0:T(8,128)(2,1)}, bf16[64,8,8,128]{3,2,1,0:T(8,128)(2,1)S(1)}, u32[]{:S(2)}) copy-start(bf16[64,8,8,128]{3,2,1,0:T(8,128)(2,1)S(1)} %copy.121) | copy-start | bytes 3145732
  12.3 1.2 copy-start.8
  12.3 1.2 copy-start.23
  13.1 1.5 copy-start.20
  13.1 1.5 copy-start.21
  16.6 8.5 %collective-permute-start.1 = (bf16[1,896]{1,0:T(2,128)(2,1)S(1)}, bf16[1,896]{1,0:T(2,128)(2,1)S(1)}, u32[]{:S(2)}, u32[]{:S(2)}) collective-permute-start(bf16[1,896]{1,0:T(2,128)(2,1)S(1)} %get-tuple-element.53), channel_id=1, source_target_pairs={{0,8},{8,16},{16,24},{24,32},{32,40},{40,48},{48,56},{56,64},{64,7... | collective-permute-start | bytes 5384 | tf_op jit(solution)/shard_map/ppermute | solution.py:72
  20.1 7.4 %copy-start.1 = (bf16[2,8,64,576]{3,2,1,0:T(8,128)(2,1)}, bf16[2,8,64,576]{3,2,1,0:T(8,128)(2,1)S(1)}, u32[]{:S(2)}) copy-start(bf16[2,8,64,576]{3,2,1,0:T(8,128)(2,1)S(1)} %copy.93) | copy-start | bytes 3538948
  20.1 6.1 %copy-start.15 = (bf16[896,576]{0,1:T(8,128)(2,1)S(1)}, bf16[896,576]{0,1:T(8,128)(2,1)}, u32[]{:S(2)}) copy-start(bf16[896,576]{0,1:T(8,128)(2,1)} %param.16) | copy-start | bytes 3096580
  20.2 6.1 %copy-start.29 = (f32[896]{0:T(1024)S(1)}, f32[896]{0:T(1024)}, u32[]{:S(2)}) copy-start(f32[896]{0:T(1024)} %param.14) | copy-start | bytes 10756
  21.6 6.1 %copy-start.10 = (f32[128,576]{0,1:T(8,128)S(1)}, f32[128,576]{0,1:T(8,128)}, u32[]{:S(2)}) copy-start(f32[128,576]{0,1:T(8,128)} %fusion.20) | copy-start | bytes 884740
  27.6 7.2 %copy-start.2 = (bf16[512,1024]{1,0:T(8,128)(2,1)S(1)}, bf16[512,1024]{1,0:T(8,128)(2,1)}, u32[]{:S(2)}) copy-start(bf16[512,1024]{1,0:T(8,128)(2,1)} %param.19) | copy-start | bytes 3145732
  27.6 7.2 %copy-start.14 = (bf16[2,64,8,128]{3,1,0,2:T(8,128)(2,1)S(1)}, bf16[2,64,8,128]{3,1,0,2:T(8,128)(2,1)}, u32[]{:S(2)}) copy-start(bf16[2,64,8,128]{3,1,0,2:T(8,128)(2,1)} %copy.96) | copy-start | bytes 786436
  28.8 14.9 %all-to-all-start = ((f32[8,16,1280]{2,1,0:T(8,128)}), f32[8,16,1280]{2,1,0:T(8,128)}, u32[]{:S(2)}, u32[]{:S(2)}) async-start(f32[8,16,1280]{2,1,0:T(8,128)} %bitcast.2), calls=%async_computation | async-start | bytes 1310720 | tf_op jit(solution)/shard_map/all_to_all | solution.py:344
  35.4 10.5 %copy-start.22 = (f32[512]{0:T(512)S(1)}, f32[512]{0:T(512)}, u32[]{:S(2)}) copy-start(f32[512]{0:T(512)} %param.17) | copy-start | bytes 6148
  35.5 28.4 %copy-start.6 = (bf16[2,8,64,512]{3,2,1,0:T(8,128)(2,1)}, bf16[2,8,64,512]{3,2,1,0:T(8,128)(2,1)S(1)}, u32[]{:S(2)}) copy-start(bf16[2,8,64,512]{3,2,1,0:T(8,128)(2,1)S(1)} %copy.97) | copy-start | bytes 3145732
  36.9 9.0 %copy-start.27 = (f32[16]{0:T(128)}, f32[16]{0:T(128)S(1)}, u32[]{:S(2)}) copy-start(f32[16]{0:T(128)S(1)} %fusion.55) | copy-start | bytes 196
  45.0 0.9 copy-start.24
  45.0 0.9 copy-start.26
  45.1 19.5 %copy-start.18 = (f32[16,576]{1,0:T(8,128)}, f32[16,576]{1,0:T(8,128)S(1)}, u32[]{:S(2)}) copy-start(f32[16,576]{1,0:T(8,128)S(1)} %multiply_add_fusion) | copy-start | bytes 110596
  45.8 18.0 %copy-start.31 = (f32[16]{0:T(128)}, f32[16]{0:T(128)S(1)}, u32[]{:S(2)}) copy-start(f32[16]{0:T(128)S(1)} %get-tuple-element.63) | copy-start | bytes 196
  95.5 4.5 %copy-start.7 = (bf16[8,9,128,128]{3,2,1,0:T(8,128)(2,1)}, bf16[8,9,128,128]{3,2,1,0:T(8,128)(2,1)S(1)}, u32[]{:S(2)}) copy-start(bf16[8,9,128,128]{3,2,1,0:T(8,128)(2,1)S(1)} %all_to_all.31.mine_ref) | copy-start | bytes 7077892
  95.5 4.5 %collective-permute-start.2 = (bf16[8,9,128,128]{3,2,1,0:T(8,128)(2,1)S(1)}, bf16[8,9,128,128]{3,2,1,0:T(8,128)(2,1)S(1)}, u32[]{:S(2)}, u32[]{:S(2)}) collective-permute-start(bf16[8,9,128,128]{3,2,1,0:T(8,128)(2,1)S(1)} %all_to_all.31.mine_ref), channel_id=1, source_target_pairs={{0,8},{8,0},{1,9},{9,1},{2,10},{10,2},{3,11},{11,3},{4,12},{12,4},... | collective-permute-start | bytes 7077896 | tf_op jit(solution)/shard_map/ppermute | solution.py:386
  100.0 1.4 copy-start.34
  131.3 4.8 %collective-permute-start.3 = (bf16[8,9,128,128]{3,2,1,0:T(8,128)(2,1)}, bf16[8,9,128,128]{3,2,1,0:T(8,128)(2,1)S(1)}, u32[]{:S(2)}, u32[]{:S(2)}) collective-permute-start(bf16[8,9,128,128]{3,2,1,0:T(8,128)(2,1)} %get-tuple-element.23), channel_id=1, source_target_pairs={{0,8},{8,0},{1,9},{9,1},{2,10},{10,2},{3,11},{11,3},{4,12},{12,4},... | collective-permute-start | bytes 7077896 | tf_op jit(solution)/shard_map/ppermute | solution.py:393
  172.9 15.3 %copy-start.3 = (bf16[512,1024]{1,0:T(8,128)(2,1)S(1)}, bf16[512,1024]{1,0:T(8,128)(2,1)}, u32[]{:S(2)}) copy-start(bf16[512,1024]{1,0:T(8,128)(2,1)} %param.19) | copy-start | bytes 3145732
  174.0 15.5 %copy-start.13 = (bf16[2,512,512]{2,1,0:T(8,128)(2,1)S(1)}, bf16[2,512,512]{2,1,0:T(8,128)(2,1)}, u32[]{:S(2)}) copy-start(bf16[2,512,512]{2,1,0:T(8,128)(2,1)} %get-tuple-element.20) | copy-start | bytes 3145732
  179.1 18.2 %all-to-all-start.4 = ((bf16[16,16,640]{2,1,0:T(8,128)(2,1)}), bf16[16,16,640]{2,1,0:T(8,128)(2,1)S(1)}, u32[]{:S(2)}, u32[]{:S(2)}) async-start(bf16[16,16,640]{2,1,0:T(8,128)(2,1)} %maximum_maximum_fusion), calls=%async_computation.4 | async-start | bytes 655360 | tf_op jit(solution)/shard_map/all_to_all | solution.py:397
  189.5 4.6 %copy-start.5 = (bf16[64,8,8,128]{3,2,1,0:T(8,128)(2,1)S(1)}, bf16[64,8,8,128]{3,2,1,0:T(8,128)(2,1)}, u32[]{:S(2)}) copy-start(bf16[64,8,8,128]{3,2,1,0:T(8,128)(2,1)} %copy-done.4) | copy-start | bytes 3145732
  192.1 5.2 %copy-start.19 = (f32[16,576]{1,0:T(8,128)S(1)}, f32[16,576]{1,0:T(8,128)}, u32[]{:S(2)}) copy-start(f32[16,576]{1,0:T(8,128)} %copy-done.18) | copy-start | bytes 110596
  192.2 5.3 %copy-start.28 = (f32[16]{0:T(128)S(1)}, f32[16]{0:T(128)}, u32[]{:S(2)}) copy-start(f32[16]{0:T(128)} %copy-done.27) | copy-start | bytes 196
  192.2 5.4 %copy-start.32 = (f32[16]{0:T(128)S(1)}, f32[16]{0:T(128)}, u32[]{:S(2)}) copy-start(f32[16]{0:T(128)} %copy-done.31) | copy-start | bytes 196
  192.2 5.4 %copy-start.33 = (f32[16]{0:T(128)S(1)}, f32[16]{0:T(128)}, u32[]{:S(2)}) copy-start(f32[16]{0:T(128)} %get-tuple-element.62) | copy-start | bytes 196
  192.2 5.5 %copy-start.25 = (f32[16]{0:T(128)S(1)}, f32[16]{0:T(128)}, u32[]{:S(2)}) copy-start(f32[16]{0:T(128)} %copy-done.24) | copy-start | bytes 196
  197.7 9.9 %copy-start.12 = (bf16[2,512,512]{2,1,0:T(8,128)(2,1)S(1)}, bf16[2,512,512]{2,1,0:T(8,128)(2,1)}, u32[]{:S(2)}) copy-start(bf16[2,512,512]{2,1,0:T(8,128)(2,1)} %get-tuple-element.19) | copy-start | bytes 3145732
  200.2 12.2 %all-to-all-start.5 = ((bf16[8,16,1280]{2,1,0:T(8,128)(2,1)}), bf16[8,16,1280]{2,1,0:T(8,128)(2,1)S(1)}, u32[]{:S(2)}, u32[]{:S(2)}) async-start(bf16[8,16,1280]{2,1,0:T(8,128)(2,1)} %broadcast_in_dim.102), calls=%async_computation.5 | async-start | bytes 655360 | tf_op jit(solution)/shard_map/all_to_all | solution.py:66
  208.1 6.3 %copy-start.9 = (bf16[128,896]{1,0:T(8,128)(2,1)S(1)}, bf16[128,896]{1,0:T(8,128)(2,1)}, u32[]{:S(2)}) copy-start(bf16[128,896]{1,0:T(8,128)(2,1)} %param.11) | copy-start | bytes 688132
  209.9 14.7 %copy-start.16 = (bf16[896,576]{0,1:T(8,128)(2,1)S(1)}, bf16[896,576]{0,1:T(8,128)(2,1)}, u32[]{:S(2)}) copy-start(bf16[896,576]{0,1:T(8,128)(2,1)} %param.16) | copy-start | bytes 3096580
  209.9 14.6 %copy-start.17 = (bf16[128,896]{1,0:T(8,128)(2,1)S(1)}, bf16[128,896]{1,0:T(8,128)(2,1)}, u32[]{:S(2)}) copy-start(bf16[128,896]{1,0:T(8,128)(2,1)} %param.12) | copy-start | bytes 688132
  209.9 14.6 %copy-start.30 = (f32[896]{0:T(1024)S(1)}, f32[896]{0:T(1024)}, u32[]{:S(2)}) copy-start(f32[896]{0:T(1024)} %param.14) | copy-start | bytes 10756
  212.5 3.2 %collective-permute-start.5 = (bf16[1,640]{1,0:T(2,128)(2,1)S(1)}, bf16[1,640]{1,0:T(2,128)(2,1)S(1)}, u32[]{:S(2)}, u32[]{:S(2)}) collective-permute-start(bf16[1,640]{1,0:T(2,128)(2,1)S(1)} %slice.171), channel_id=1, source_target_pairs={{8,0},{16,8},{24,16},{32,24},{40,32},{48,40},{56,48},{64,56},{72,6... | collective-permute-start | bytes 3848 | tf_op jit(solution)/shard_map/ppermute | solution.py:72
  215.8 8.5 %collective-permute-start.4 = (bf16[1,640]{1,0:T(2,128)(2,1)S(1)}, bf16[1,640]{1,0:T(2,128)(2,1)S(1)}, u32[]{:S(2)}, u32[]{:S(2)}) collective-permute-start(bf16[1,640]{1,0:T(2,128)(2,1)S(1)} %get-tuple-element.38), channel_id=1, source_target_pairs={{0,8},{8,16},{16,24},{24,32},{32,40},{40,48},{48,56},{56,64},{64,7... | collective-permute-start | bytes 3848 | tf_op jit(solution)/shard_map/ppermute | solution.py:72

commit v3 on v2

--- a/solution.py
+++ b/solution.py
@@ -18,6 +18,7 @@
 EPSILON = 1e-06
 ROTARY_BASE = 10000.0
 SCALE = (NOPE + ROPE) ** (-0.5)
+LOG2E = 1.4426950408889634
 
 CTX = ("xh", "z", "co")
 TP = ("xl", "y")
@@ -78,10 +79,30 @@
     return jnp.concatenate([lead, rope[None]], axis=0)
 
 
-def unpack_keys(tiles):
-    lead = tiles[:8].reshape(2, 4, 128, 128).transpose(0, 2, 1, 3).reshape(2, 128, LAT)
-    rope = jnp.stack([tiles[8, :, :ROPE], tiles[8, :, ROPE:]], axis=0)
-    return jnp.concatenate([lead, rope, jnp.zeros_like(rope)], axis=2)
+def merge_kernel(in_ref, out_ref):
+    total = in_ref[0].astype(f32)
+    for t in range(1, N_TP):
+        total = total + in_ref[t].astype(f32)
+    total = total.astype(bf16)
+    for xh in range(2):
+        rope = total[8, :, xh * ROPE : (xh + 1) * ROPE]
+        row = jnp.concatenate(
+            [total[xh * 4 + c] for c in range(4)] + [rope, jnp.zeros_like(rope)], axis=1
+        )
+        for z in range(8):
+            out_ref[xh * 8 + z] = row[z * PIECE : (z + 1) * PIECE]
+
+
+def merge(arrived):
+    return pl.pallas_call(
+        merge_kernel,
+        out_shape=jax.ShapeDtypeStruct((16, PIECE, WIDE), bf16),
+        compiler_params=pltpu.CompilerParams(vmem_limit_bytes=16 * 1024 * 1024),
+        cost_estimate=pl.CostEstimate(
+            flops=1_200_000, bytes_accessed=2_700_000, transcendentals=0
+        ),
+        name="merge",
+    )(arrived)
 
 
 def attention_kernel(
@@ -182,42 +203,53 @@
     def first(i, carry):
         seg, half, block = locate(i)
         k = slab(half, block)
-        s = nn(k, qt_ref[seg]) * SCALE
         idx = lax.broadcasted_iota(jnp.int32, (BLOCK, 1), 0)
         owner = block * 8 + ((idx // 16) % 4) * 2 + idx // 256
         within = ((idx // 64) % 4) * 16 + idx % 16
         key_pos = jnp.where(half == 0, owner, 63 - owner) * 64 + within
-        row = lax.broadcasted_iota(jnp.int32, (1, SEG), 1)
+        wide = SEG // 1
+        row = lax.broadcasted_iota(jnp.int32, (1, wide), 1)
         q_pos = jnp.where(seg == 0, ctx, 63 - ctx) * 64 + row % 64
-        s = jnp.where(key_pos <= q_pos, s, -jnp.inf)
-        s_buf[i] = s
-        dp = nn(k[:, :LAT], gt_ref[seg])
-        dp_buf[i] = dp
-        m_old = m_buf[seg]
-        m_new = jnp.maximum(m_old, jnp.max(s, axis=0, keepdims=True))
-        alpha = jnp.exp(m_old - m_new)
-        e = jnp.exp(s - m_new)
-        m_buf[seg] = m_new
-        l_buf[seg] = l_buf[seg] * alpha + jnp.sum(e, axis=0, keepdims=True)
-        a_buf[seg] = a_buf[seg] * alpha + jnp.sum(e * dp, axis=0, keepdims=True)
+        for at in range(0, SEG, wide):
+            part = slice(at, at + wide)
+            s = nn(k, qt_ref[seg, :, part]) * (SCALE * LOG2E)
+            s = jnp.where(key_pos <= q_pos, s, -jnp.inf)
+            s_buf[i, :, part] = s
+            dp = nn(k[:, :LAT], gt_ref[seg, :, part])
+            dp_buf[i, :, part] = dp
+            m_old = m_buf[seg, :, part]
+            m_new = jnp.maximum(m_old, jnp.max(s, axis=0, keepdims=True))
+            alpha = jnp.exp2(m_old - m_new)
+            e = jnp.exp2(s - m_new)
+            m_buf[seg, :, part] = m_new
+            l_buf[seg, :, part] = l_buf[seg, :, part] * alpha + jnp.sum(e, axis=0, keepdims=True)
+            a_buf[seg, :, part] = a_buf[seg, :, part] * alpha + jnp.sum(
+                e * dp, axis=0, keepdims=True
+            )
         return carry
 
     lax.fori_loop(0, STEPS, first, 0)
     for copy in copies[4:]:
         copy.wait()
+    a_buf[...] = a_buf[...] / l_buf[...]
+    m_buf[...] = m_buf[...] + jnp.log2(l_buf[...])
 
     def second(i, carry):
         seg, half, block = locate(i)
         k = slab(half, block)
-        inv = 1.0 / l_buf[seg]
-        delta = a_buf[seg] * inv
-        p = (jnp.exp(s_buf[i] - m_buf[seg]) * inv).astype(bf16)
-        ds = (p.astype(f32) * (dp_buf[i] - delta) * SCALE).astype(bf16)
         kt = k.T
-        ot_buf[seg] += nn(kt[:LAT], p)
-        dqt_buf[seg] += nn(kt, ds)
-        lead = nn(ds, q_ref[seg, :, :LAT]) + nn(p, g_ref[seg])
-        tail = nn(ds, q_ref[seg, :, LAT:])
+        wide = SEG // 1
+        lead = None
+        for at in range(0, SEG, wide):
+            part = slice(at, at + wide)
+            p = jnp.exp2(s_buf[i, :, part] - m_buf[seg, :, part]).astype(bf16)
+            ds = (p.astype(f32) * ((dp_buf[i, :, part] - a_buf[seg, :, part]) * SCALE)).astype(bf16)
+            ot_buf[seg, :, part] += nn(kt[:LAT], p)
+            dqt_buf[seg, :, part] += nn(kt, ds)
+            more = nn(ds, q_ref[seg, part, :LAT]) + nn(p, g_ref[seg, part, :])
+            rest = nn(ds, q_ref[seg, part, LAT:])
+            lead = more if lead is None else lead + more
+            tail = rest if at == 0 else tail + rest
         xh = block // 2
         at = pl.multiple_of((block % 2) * 64, 64)
         lane = lax.broadcasted_iota(jnp.int32, (1, 128), 1)
@@ -343,28 +375,7 @@
     ).reshape(N_TP, PIECE, 2 * WIDE)
     parts = lax.all_to_all(parts, TP, split_axis=0, concat_axis=0, tiled=True)
 
-    cos_table, sin_table = rotation(row_positions(ctx, jnp.arange(ROWS)))
-    cos_table = cos_table.reshape(2, 1, HALF, ROPE // 2)
-    sin_table = sin_table.reshape(2, 1, HALF, ROPE // 2)
-    key_up_heads = key_up.reshape(LAT, HEADS, NOPE)
-    value_up_heads = value_up.reshape(LAT, HEADS, VDIM)
-    query_heads = queries.reshape(2, HALF, HEADS, NOPE + ROPE).transpose(0, 2, 1, 3)
-    query_rot = rotate_pairs(query_heads[..., NOPE:].astype(f32), cos_table, sin_table)
-    query_latent = jnp.einsum(
-        "ghsn,lhn->ghsl", query_heads[..., :NOPE], key_up_heads, preferred_element_type=f32
-    )
-    q = jnp.concatenate([query_latent.astype(bf16), query_rot.astype(bf16)], axis=3)
-    q = q.reshape(2, SEG, KEYW)
-    g = jnp.einsum(
-        "gshv,lhv->ghsl",
-        grad_out.reshape(2, HALF, HEADS, VDIM),
-        value_up_heads,
-        preferred_element_type=f32,
-    )
-    g = g.astype(bf16).reshape(2, SEG, LAT)
-    qt, gt = q.swapaxes(1, 2), g.swapaxes(1, 2)
-
-    parts, q, qt, g, gt = lax.optimization_barrier((parts, q, qt, g, gt))
+    parts, queries, grad_out = lax.optimization_barrier((parts, queries, grad_out))
     parts = jnp.sum(parts, axis=0)
     part_hidden, part_next = parts[:, :KEYW], parts[:, WIDE : WIDE + KEYW]
     inv_hidden = lax.rsqrt(parts[:, KEYW : KEYW + 1] / D + EPSILON)
@@ -383,6 +394,28 @@
     )
     same = pack_keys(gather_copies(key_piece, XZ, 16).reshape(2, 128, WIDE))
     mine = gather_copies(same, TP, N_TP)
+
+    cos_table, sin_table = rotation(row_positions(ctx, jnp.arange(ROWS)))
+    cos_table = cos_table.reshape(2, 1, HALF, ROPE // 2)
+    sin_table = sin_table.reshape(2, 1, HALF, ROPE // 2)
+    key_up_heads = key_up.reshape(LAT, HEADS, NOPE)
+    value_up_heads = value_up.reshape(LAT, HEADS, VDIM)
+    query_heads = queries.reshape(2, HALF, HEADS, NOPE + ROPE).transpose(0, 2, 1, 3)
+    query_rot = rotate_pairs(query_heads[..., NOPE:].astype(f32), cos_table, sin_table)
+    query_latent = jnp.einsum(
+        "ghsn,lhn->ghsl", query_heads[..., :NOPE], key_up_heads, preferred_element_type=f32
+    )
+    q = jnp.concatenate([query_latent.astype(bf16), query_rot.astype(bf16)], axis=3)
+    q = q.reshape(2, SEG, KEYW)
+    g = jnp.einsum(
+        "gshv,lhv->ghsl",
+        grad_out.reshape(2, HALF, HEADS, VDIM),
+        value_up_heads,
+        preferred_element_type=f32,
+    )
+    g = g.astype(bf16).reshape(2, SEG, LAT)
+    qt, gt = q.swapaxes(1, 2), g.swapaxes(1, 2)
+    mine, q, qt, g, gt = lax.optimization_barrier((mine, q, qt, g, gt))
     other = lax.ppermute(mine, "co", [(0, 1), (1, 0)])
 
     where = jnp.stack([ctx, core]).astype(jnp.int32)
@@ -393,9 +426,6 @@
     received = lax.ppermute(dother, "co", [(0, 1), (1, 0)])
     dkey = (dmine.astype(f32) + received.astype(f32)).astype(bf16)
     dkey = lax.all_to_all(dkey, TP, split_axis=0, concat_axis=0, tiled=True)
-    dkey = unpack_keys(jnp.sum(dkey.astype(f32), axis=0).astype(bf16)).reshape(16, PIECE, WIDE)
-    dkey = lax.all_to_all(dkey, XZ, split_axis=0, concat_axis=0, tiled=True)
-    dkey = jnp.sum(dkey.astype(f32), axis=0)[:, :KEYW]
 
     attended = jnp.einsum(
         "glhs,lhv->gshv",
@@ -415,6 +445,10 @@
     )
     grad_queries = jnp.concatenate([grad_nope, grad_rope], axis=3).astype(bf16)
     grad_queries = grad_queries.transpose(0, 2, 1, 3).reshape(ROWS, HEADS * (NOPE + ROPE))
+    dkey, attended, grad_queries = lax.optimization_barrier((dkey, attended, grad_queries))
+
+    dkey = lax.all_to_all(merge(dkey), XZ, split_axis=0, concat_axis=0, tiled=True)
+    dkey = jnp.sum(dkey.astype(f32), axis=0)[:, :KEYW]
 
     gained = gain_latent * dkey[:, :LAT]
     dlatent = jnp.concatenate(

time: 227 us -> 210 us (0.925)
  blocking collectives: 81.2 us -> 44.9 us
  waiting for transfers between devices: 23.9 us -> 51.9 us
  starting transfers between devices: 35.2 us -> 29.7 us
  other arithmetic: 18 us -> 13 us
  local copies, waits for them, and re-layouts: 26.5 us -> 29.1 us
    all_to_all x2, blocking collectives: 48.5 us -> 25.3 us  [gather_copies(): return lax.all_to_all(copies, axes, split_axis=0, concat_axis=0, tiled=True)]
    all_to_all x1, blocking collectives: 32.7 us -> 19.7 us  [on_device(): lax.all_to_all(merge(dkey), XZ, split_axis=0, concat_axis=0, tiled=True)]
    all_to_all x1, waiting for transfers between devices: 1.49 us -> 13.5 us  [gather_copies(): return lax.all_to_all(copies, axes, split_axis=0, concat_axis=0, tiled=True)]
    all_to_all x1, waiting for transfers between devices: 0.8 us -> 10.7 us  [on_device(): dkey = lax.all_to_all(dkey, TP, split_axis=0, concat_axis=0, tiled=True)]
    all_to_all x1, starting transfers between devices: 9.16 us -> 3.8 us  [on_device(): dkey = lax.all_to_all(dkey, TP, split_axis=0, concat_axis=0, tiled=True)]
    ppermute x2, waiting for transfers between devices: 6.13 us -> 10.1 us  [edge_exchange(): lax.ppermute(second_row, CTX, up)]
    pallas_call x2, local copies, waits for them, and re-layouts: 1.86 us -> 4.58 us  [attention(): pl.pallas_call(attention_kernel, in_specs=[pl.BlockSpec(memory_space=pltp...]
    reshape x2, local copies, waits for them, and re-layouts: 1.31 us -> 3.94 us  [on_device(): tailt.reshape(2, ROPE, HEADS, HALF).transpose(0, 2, 3, 1)]
  transfers between devices with their start and end apart: 9 -> 9, of which waited for: 8 -> 8; matrix products, arithmetic and copies ran while one was open for 13% -> 17% of each run, Pallas kernels for 0% -> 0%
where the time goes in v3:
time: 210 us; the launch traced here: 209 us
  waiting for transfers between devices  51.9 us (25%)
  blocking collectives  44.9 us (21%)
  Pallas kernels  29.8 us (14%)
  starting transfers between devices  29.7 us (14%)
  local copies, waits for them, and re-layouts  29.1 us (14%)
  other arithmetic  13 us (6%)
  matrix products  8.85 us (4%)
    pallas_call x1, Pallas kernels, attention(): pl.pallas_call(attention_kernel, in_specs=[pl.BlockSpec(memory_space=pltp...  29.4 us
    all_to_all x2, blocking collectives, gather_copies(): return lax.all_to_all(copies, axes, split_axis=0, concat_axis=0, tiled=True)  25.3 us
    all_to_all x1, blocking collectives, on_device(): lax.all_to_all(merge(dkey), XZ, split_axis=0, concat_axis=0, tiled=True)  19.7 us
    all_to_all x1, waiting for transfers between devices, gather_copies(): return lax.all_to_all(copies, axes, split_axis=0, concat_axis=0, tiled=True)  13.5 us
    all_to_all x1, waiting for transfers between devices, on_device(): dkey = lax.all_to_all(dkey, TP, split_axis=0, concat_axis=0, tiled=True)  10.7 us
    ppermute x2, waiting for transfers between devices, edge_exchange(): lax.ppermute(second_row, CTX, up)  10.1 us
    ppermute x2, starting transfers between devices, edge_exchange(): lax.ppermute(first_row, CTX, down)  9.25 us
    all_to_all x1, waiting for transfers between devices, on_device(): parts = lax.all_to_all(parts, TP, split_axis=0, concat_axis=0, tiled=True)  8.71 us
  transfers between devices with their start and end apart: 9, of which 8 were waited for; matrix products, arithmetic and copies ran while one was open for 17% of the time, Pallas kernels for 0%

profile of v3, /device:TPU:4, one launch (start us, length us, event | category | flops | bytes accessed | tf_op | source)
XLA Modules:
  0.0 208.6 jit_solution(14686187477046916348)
XLA Ops:
  0.7 0.9 slice.111
  1.5 7.1 %collective-permute-start = (bf16[1,896]{1,0:T(2,128)(2,1)S(1)}, bf16[1,896]{1,0:T(2,128)(2,1)S(1)}, u32[]{:S(2)}, u32[]{:S(2)}) collective-permute-start(bf16[1,896]{1,0:T(2,128)(2,1)S(1)} %slice.111), channel_id=1, source_target_pairs={{8,0},{16,8},{24,16},{32,24},{40,32},{48,40},{56,48},{64,56},{72,6... | collective-permute-start | bytes 5384 | tf_op jit(solution)/shard_map/ppermute | solution.py:73
  8.7 1.4 fusion.20
  10.1 1.0 fusion.60
  11.1 0.7 broadcast_select_fusion
  11.9 1.9 collective-permute-start.1
  13.8 1.1 fusion.17
  14.8 5.6 %collective-permute-done.1 = bf16[1,896]{1,0:T(2,128)(2,1)S(1)} collective-permute-done((bf16[1,896]{1,0:T(2,128)(2,1)S(1)}, bf16[1,896]{1,0:T(2,128)(2,1)S(1)}, u32[]{:S(2)}, u32[]{:S(2)}) %collective-permute-start.1) | collective-permute-done | bytes 1824 | tf_op jit(solution)/shard_map/ppermute | solution.py:73
  20.6 0.4 fusion.22
  21.2 1.1 copy.88
  22.2 6.0 %all-to-all-start = ((f32[8,16,1280]{2,1,0:T(8,128)}), f32[8,16,1280]{2,1,0:T(8,128)S(1)}, u32[]{:S(2)}, u32[]{:S(2)}) async-start(f32[8,16,1280]{2,1,0:T(8,128)} %bitcast.2), calls=%async_computation | async-start | bytes 1310720 | tf_op jit(solution)/shard_map/all_to_all | solution.py:376
  28.3 8.7 %all-to-all-done = f32[8,16,1280]{2,1,0:T(8,128)S(1)} async-done(((f32[8,16,1280]{2,1,0:T(8,128)}), f32[8,16,1280]{2,1,0:T(8,128)S(1)}, u32[]{:S(2)}, u32[]{:S(2)}) %all-to-all-start) | async-done | bytes 655392 | tf_op jit(solution)/shard_map/all_to_all | solution.py:376
  37.1 0.2 fusion.50
  37.8 13.8 %all_to_all.30 = bf16[16,16,640]{2,1,0:T(8,128)(2,1)S(1)} all-to-all(bf16[16,16,640]{2,1,0:T(8,128)(2,1)S(1)} %broadcast_in_dim.37), channel_id=1, replica_groups=mesh['xh'=2,'z'=8,'co'=2,'xl'=2,'y'=4] {'xh','z'}, dimensions={0} | all-to-all | bytes 655360 | tf_op jit(solution)/shard_map/all_to_all | solution.py:67
  51.8 2.0 broadcast_in_dim.39
  53.8 4.5 %all-to-all-start.2 = ((bf16[8,9,128,128]{3,2,1,0:T(8,128)(2,1)}), bf16[8,9,128,128]{3,2,1,0:T(8,128)(2,1)}, u32[]{:S(2)}, u32[]{:S(2)}) async-start(bf16[8,9,128,128]{3,2,1,0:T(8,128)(2,1)} %broadcast_in_dim.39), calls=%async_computation.2 | async-start | bytes 4718592 | tf_op jit(solution)/shard_map/all_to_all | solution.py:67
  58.3 0.3 copy.120
  58.6 0.9 copy-done.8
  59.5 0.3 copy.122
  59.8 1.0 multiply_cosine_fusion
  60.8 0.8 copy.121
  61.6 2.3 %reshape.138 = bf16[2,64,8,192]{3,2,1,0:T(8,128)(2,1)} reshape(bf16[128,1536]{1,0:T(8,128)(2,1)} %param.20) | data formatting | bytes 786432 | tf_op jit(solution)/shard_map/reshape | solution.py:403
  63.8 1.1 copy.140
  65.0 1.1 subtract_convert_fusion.1
  66.1 0.5 fusion
  66.6 0.2 pad_maximum_fusion
  67.0 0.5 copy-done.6
  67.6 0.5 fusion.1
  68.1 1.3 copy.96
  69.5 1.4 copy.92
  70.9 13.5 %all-to-all-done.2.mine_ref = bf16[8,9,128,128]{3,2,1,0:T(8,128)(2,1)} async-done(((bf16[8,9,128,128]{3,2,1,0:T(8,128)(2,1)}), bf16[8,9,128,128]{3,2,1,0:T(8,128)(2,1)}, u32[]{:S(2)}, u32[]{:S(2)}) %all-to-all-start.2) | async-done | bytes 2359328 | tf_op jit(solution)/shard_map/all_to_all | solution.py:67
  84.4 0.7 pad_add_fusion.where_ref
  85.0 4.1 %collective-permute-done.2.other_ref = bf16[8,9,128,128]{3,2,1,0:T(8,128)(2,1)S(1)} collective-permute-done((bf16[8,9,128,128]{3,2,1,0:T(8,128)(2,1)}, bf16[8,9,128,128]{3,2,1,0:T(8,128)(2,1)S(1)}, u32[]{:S(2)}, u32[]{:S(2)}) %collective-permute-start.2) | collective-permute-done | bytes 2359328 | tf_op jit(solution)/shard_map/ppermute | solution.py:419
  89.1 1.4 copy-done.16
  90.6 29.4 %attention.1 = (bf16[2,512,512]{2,1,0:T(8,128)(2,1)}, bf16[2,512,512]{2,1,0:T(8,128)(2,1)}, f32[2,64,512]{2,1,0:T(8,128)}, bf16[8,9,128,128]{3,2,1,0:T(8,128)(2,1)}, bf16[8,9,128,128]{3,2,1,0:T(8,128)(2,1)}) custom-call(s32[2]{0:T(128)} %pad_add_fusion.where_ref, bf16[8,9,128,128]{3,2,1,0:T(8,128)(2,1)} %all-to-all-done.2.mine_ref, ...), custom_call_target="tpu_custom_call" | custom-call | flops 14000000000 | bytes 20000000 | tf_op jit(solution)/shard_map/attention/pallas_call | solution.py:296
  119.9 0.2 collective-permute-start.3
  120.2 4.6 %collective-permute-done.3 = bf16[8,9,128,128]{3,2,1,0:T(8,128)(2,1)S(1)} collective-permute-done((bf16[8,9,128,128]{3,2,1,0:T(8,128)(2,1)}, bf16[8,9,128,128]{3,2,1,0:T(8,128)(2,1)S(1)}, u32[]{:S(2)}, u32[]{:S(2)}) %collective-permute-start.3) | collective-permute-done | bytes 2359328 | tf_op jit(solution)/shard_map/ppermute | solution.py:426
  124.8 4.3 %add_convert_fusion = bf16[8,9,128,128]{3,2,1,0:T(8,128)(2,1)} fusion(bf16[8,9,128,128]{3,2,1,0:T(8,128)(2,1)S(1)} %collective-permute-done.3, bf16[8,9,128,128]{3,2,1,0:T(8,128)(2,1)} %get-tuple-element.28), kind=kLoop, calls=%fused_computation | loop fusion | flops 4718592 | bytes 7077888 | tf_op jit(solution)/shard_map/convert_element_type | solution.py:427
  129.1 3.8 %all-to-all-start.3 = ((bf16[8,9,128,128]{3,2,1,0:T(8,128)(2,1)}), bf16[8,9,128,128]{3,2,1,0:T(8,128)(2,1)S(1)}, u32[]{:S(2)}, u32[]{:S(2)}) async-start(bf16[8,9,128,128]{3,2,1,0:T(8,128)(2,1)} %add_convert_fusion), calls=%async_computation.3 | async-start | bytes 4718592 | tf_op jit(solution)/shard_map/all_to_all | solution.py:428
  132.9 1.9 reshape.147
  134.8 2.0 copy.104
  136.8 2.3 %copy.97 = bf16[2,512,512]{1,2,0:T(8,128)(2,1)} copy(bf16[2,512,512]{2,1,0:T(8,128)(2,1)} %get-tuple-element.30) | data formatting | bytes 2097152 | tf_op jit(solution)/shard_map/attention/pallas_call | solution.py:296
  139.1 2.0 fusion.6
  141.1 0.2 copy.100
  141.3 0.8 copy.141
  142.1 2.3 %copy.101 = bf16[2,512,512]{1,2,0:T(8,128)(2,1)} copy(bf16[2,512,512]{2,1,0:T(8,128)(2,1)} %get-tuple-element.31) | data formatting | bytes 2097152 | tf_op jit(solution)/shard_map/attention/pallas_call | solution.py:296
  144.4 1.4 add_convert_fusion.1
  145.8 2.0 fusion.7
  148.0 1.1 copy.105
  149.1 2.3 %reshape.148 = bf16[128,1536]{1,0:T(8,128)(2,1)} reshape(bf16[2,64,8,192]{3,2,1,0:T(8,128)(2,1)} %copy.105) | data formatting | bytes 786432 | tf_op jit(solution)/shard_map/reshape | solution.py:447
  151.4 10.7 %all-to-all-done.3.in_ref = bf16[8,9,128,128]{3,2,1,0:T(8,128)(2,1)S(1)} async-done(((bf16[8,9,128,128]{3,2,1,0:T(8,128)(2,1)}), bf16[8,9,128,128]{3,2,1,0:T(8,128)(2,1)S(1)}, u32[]{:S(2)}, u32[]{:S(2)}) %all-to-all-start.3) | async-done | bytes 2359328 | tf_op jit(solution)/shard_map/all_to_all | solution.py:428
  162.1 0.5 merge.1
  162.5 19.7 %all_to_all.31 = bf16[16,16,640]{2,1,0:T(8,128)(2,1)S(1)} all-to-all(bf16[16,16,640]{2,1,0:T(8,128)(2,1)S(1)} %merge.1), channel_id=1, replica_groups=mesh['xh'=2,'z'=8,'co'=2,'xl'=2,'y'=4] {'xh','z'}, dimensions={0} | all-to-all | bytes 655360 | tf_op jit(solution)/shard_map/all_to_all | solution.py:450
  182.6 0.2 multiply_reduce_fusion
  183.0 0.2 fusion.53
  183.6 11.5 %all_to_all.32 = bf16[8,16,1280]{2,1,0:T(8,128)(2,1)S(1)} all-to-all(bf16[8,16,1280]{2,1,0:T(8,128)(2,1)S(1)} %broadcast_in_dim.98), channel_id=1, replica_groups=mesh['xh'=2,'z'=8,'co'=2,'xl'=2,'y'=4] {'xl','y'}, dimensions={0} | all-to-all | bytes 655360 | tf_op jit(solution)/shard_map/all_to_all | solution.py:67
  195.1 0.2 add_reduce_fusion.1
  195.3 2.1 %collective-permute-start.5 = (bf16[1,640]{1,0:T(2,128)(2,1)S(1)}, bf16[1,640]{1,0:T(2,128)(2,1)S(1)}, u32[]{:S(2)}, u32[]{:S(2)}) collective-permute-start(bf16[1,640]{1,0:T(2,128)(2,1)S(1)} %slice.156), channel_id=1, source_target_pairs={{8,0},{16,8},{24,16},{32,24},{40,32},{48,40},{56,48},{64,56},{72,6... | collective-permute-start | bytes 3848 | tf_op jit(solution)/shard_map/ppermute | solution.py:73
  197.4 1.1 fusion.5
  198.5 0.2 collective-permute-done.5
  198.7 4.0 %collective-permute-start.4 = (bf16[1,640]{1,0:T(2,128)(2,1)S(1)}, bf16[1,640]{1,0:T(2,128)(2,1)S(1)}, u32[]{:S(2)}, u32[]{:S(2)}) collective-permute-start(bf16[1,640]{1,0:T(2,128)(2,1)S(1)} %get-tuple-element.50), channel_id=1, source_target_pairs={{0,8},{8,16},{16,24},{24,32},{32,40},{40,48},{48,56},{56,64},{64,7... | collective-permute-start | bytes 3848 | tf_op jit(solution)/shard_map/ppermute | solution.py:73
  202.8 4.5 %collective-permute-done.4 = bf16[1,640]{1,0:T(2,128)(2,1)S(1)} collective-permute-done((bf16[1,640]{1,0:T(2,128)(2,1)S(1)}, bf16[1,640]{1,0:T(2,128)(2,1)S(1)}, u32[]{:S(2)}, u32[]{:S(2)}) %collective-permute-start.4) | collective-permute-done | bytes 1312 | tf_op jit(solution)/shard_map/ppermute | solution.py:73
  207.2 0.2 add_reduce_fusion
  207.5 1.0 fusion.4
  (75 shorter events, 2.6 us)
Async XLA Ops:
  0.6 8.0 %copy-start = (bf16[896,576]{0,1:T(8,128)(2,1)S(1)}, bf16[896,576]{0,1:T(8,128)(2,1)}, u32[]{:S(2)}) copy-start(bf16[896,576]{0,1:T(8,128)(2,1)} %param.15) | copy-start | bytes 3096580
  0.6 20.0 %copy-start.9 = (bf16[896,576]{0,1:T(8,128)(2,1)S(1)}, bf16[896,576]{0,1:T(8,128)(2,1)}, u32[]{:S(2)}) copy-start(bf16[896,576]{0,1:T(8,128)(2,1)} %param.16) | copy-start | bytes 3096580
  0.7 20.0 %copy-start.15 = (f32[896]{0:T(1024)S(1)}, f32[896]{0:T(1024)}, u32[]{:S(2)}) copy-start(f32[896]{0:T(1024)} %param.14) | copy-start | bytes 10756
  1.5 9.6 %collective-permute-start = (bf16[1,896]{1,0:T(2,128)(2,1)S(1)}, bf16[1,896]{1,0:T(2,128)(2,1)S(1)}, u32[]{:S(2)}, u32[]{:S(2)}) collective-permute-start(bf16[1,896]{1,0:T(2,128)(2,1)S(1)} %slice.111), channel_id=1, source_target_pairs={{8,0},{16,8},{24,16},{32,24},{40,32},{48,40},{56,48},{64,56},{72,6... | collective-permute-start | bytes 5384 | tf_op jit(solution)/shard_map/ppermute | solution.py:73
  11.9 8.6 %collective-permute-start.1 = (bf16[1,896]{1,0:T(2,128)(2,1)S(1)}, bf16[1,896]{1,0:T(2,128)(2,1)S(1)}, u32[]{:S(2)}, u32[]{:S(2)}) collective-permute-start(bf16[1,896]{1,0:T(2,128)(2,1)S(1)} %get-tuple-element.63), channel_id=1, source_target_pairs={{0,8},{8,16},{16,24},{24,32},{32,40},{40,48},{48,56},{56,64},{64,7... | collective-permute-start | bytes 5384 | tf_op jit(solution)/shard_map/ppermute | solution.py:73
  21.1 16.5 %copy-start.13 = (f32[512]{0:T(512)S(1)}, f32[512]{0:T(512)}, u32[]{:S(2)}) copy-start(f32[512]{0:T(512)} %param.17) | copy-start | bytes 6148
  22.2 14.8 %all-to-all-start = ((f32[8,16,1280]{2,1,0:T(8,128)}), f32[8,16,1280]{2,1,0:T(8,128)S(1)}, u32[]{:S(2)}, u32[]{:S(2)}) async-start(f32[8,16,1280]{2,1,0:T(8,128)} %bitcast.2), calls=%async_computation | async-start | bytes 1310720 | tf_op jit(solution)/shard_map/all_to_all | solution.py:376
  53.8 4.5 %copy-start.7 = (bf16[512,1024]{1,0:T(8,128)(2,1)S(1)}, bf16[512,1024]{1,0:T(8,128)(2,1)}, u32[]{:S(2)}) copy-start(bf16[512,1024]{1,0:T(8,128)(2,1)} %param.18) | copy-start | bytes 3145732
  53.8 30.6 %all-to-all-start.2 = ((bf16[8,9,128,128]{3,2,1,0:T(8,128)(2,1)}), bf16[8,9,128,128]{3,2,1,0:T(8,128)(2,1)}, u32[]{:S(2)}, u32[]{:S(2)}) async-start(bf16[8,9,128,128]{3,2,1,0:T(8,128)(2,1)} %broadcast_in_dim.39), calls=%async_computation.2 | async-start | bytes 4718592 | tf_op jit(solution)/shard_map/all_to_all | solution.py:67
  58.3 1.2 copy-start.8
  58.3 2.5 %copy-start.12 = (bf16[128,1024]{1,0:T(8,128)(2,1)S(1)}, bf16[128,1024]{1,0:T(8,128)(2,1)}, u32[]{:S(2)}) copy-start(bf16[128,1024]{1,0:T(8,128)(2,1)} %param.21) | copy-start | bytes 786436
  58.6 7.5 %copy-start.2 = (bf16[64,8,8,128]{3,2,1,0:T(8,128)(2,1)}, bf16[64,8,8,128]{3,2,1,0:T(8,128)(2,1)S(1)}, u32[]{:S(2)}) copy-start(bf16[64,8,8,128]{3,2,1,0:T(8,128)(2,1)S(1)} %copy.120) | copy-start | bytes 3145732
  59.8 7.2 %copy-start.3 = (bf16[64,8,8,128]{3,2,1,0:T(8,128)(2,1)}, bf16[64,8,8,128]{3,2,1,0:T(8,128)(2,1)S(1)}, u32[]{:S(2)}) copy-start(bf16[64,8,8,128]{3,2,1,0:T(8,128)(2,1)S(1)} %copy.122) | copy-start | bytes 3145732
  66.6 1.0 copy-start.6
  67.0 2.4 %copy-start.1 = (bf16[2,8,64,576]{3,2,1,0:T(8,128)(2,1)}, bf16[2,8,64,576]{3,2,1,0:T(8,128)(2,1)S(1)}, u32[]{:S(2)}) copy-start(bf16[2,8,64,576]{3,2,1,0:T(8,128)(2,1)S(1)} %copy.91) | copy-start | bytes 3538948
  68.1 21.0 %copy-start.4 = (bf16[2,8,64,512]{3,2,1,0:T(8,128)(2,1)}, bf16[2,8,64,512]{3,2,1,0:T(8,128)(2,1)S(1)}, u32[]{:S(2)}) copy-start(bf16[2,8,64,512]{3,2,1,0:T(8,128)(2,1)S(1)} %copy.95) | copy-start | bytes 3145732
  84.4 4.7 %collective-permute-start.2 = (bf16[8,9,128,128]{3,2,1,0:T(8,128)(2,1)}, bf16[8,9,128,128]{3,2,1,0:T(8,128)(2,1)S(1)}, u32[]{:S(2)}, u32[]{:S(2)}) collective-permute-start(bf16[8,9,128,128]{3,2,1,0:T(8,128)(2,1)} %all-to-all-done.2.mine_ref), channel_id=1, source_target_pairs={{0,8},{8,0},{1,9},{9,1},{2,10},{10,2},{3,11},{11,3},{4,12},{12,4},... | collective-permute-start | bytes 7077896 | tf_op jit(solution)/shard_map/ppermute | solution.py:419
  89.1 1.4 copy-start.16
  119.9 4.8 %collective-permute-start.3 = (bf16[8,9,128,128]{3,2,1,0:T(8,128)(2,1)}, bf16[8,9,128,128]{3,2,1,0:T(8,128)(2,1)S(1)}, u32[]{:S(2)}, u32[]{:S(2)}) collective-permute-start(bf16[8,9,128,128]{3,2,1,0:T(8,128)(2,1)} %get-tuple-element.29), channel_id=1, source_target_pairs={{0,8},{8,0},{1,9},{9,1},{2,10},{10,2},{3,11},{11,3},{4,12},{12,4},... | collective-permute-start | bytes 7077896 | tf_op jit(solution)/shard_map/ppermute | solution.py:426
  129.1 33.0 %all-to-all-start.3 = ((bf16[8,9,128,128]{3,2,1,0:T(8,128)(2,1)}), bf16[8,9,128,128]{3,2,1,0:T(8,128)(2,1)S(1)}, u32[]{:S(2)}, u32[]{:S(2)}) async-start(bf16[8,9,128,128]{3,2,1,0:T(8,128)(2,1)} %add_convert_fusion), calls=%async_computation.3 | async-start | bytes 4718592 | tf_op jit(solution)/shard_map/all_to_all | solution.py:428
  162.1 35.4 %copy-start.14 = (f32[896]{0:T(1024)S(1)}, f32[896]{0:T(1024)}, u32[]{:S(2)}) copy-start(f32[896]{0:T(1024)} %param.13) | copy-start | bytes 10756
  162.5 34.9 %copy-start.5 = (bf16[128,896]{1,0:T(8,128)(2,1)S(1)}, bf16[128,896]{1,0:T(8,128)(2,1)}, u32[]{:S(2)}) copy-start(bf16[128,896]{1,0:T(8,128)(2,1)} %param.11) | copy-start | bytes 688132
  182.2 25.3 %copy-start.10 = (bf16[896,576]{0,1:T(8,128)(2,1)S(1)}, bf16[896,576]{0,1:T(8,128)(2,1)}, u32[]{:S(2)}) copy-start(bf16[896,576]{0,1:T(8,128)(2,1)} %param.16) | copy-start | bytes 3096580
  182.2 25.3 %copy-start.11 = (bf16[128,896]{1,0:T(8,128)(2,1)S(1)}, bf16[128,896]{1,0:T(8,128)(2,1)}, u32[]{:S(2)}) copy-start(bf16[128,896]{1,0:T(8,128)(2,1)} %param.12) | copy-start | bytes 688132
  195.3 3.4 %collective-permute-start.5 = (bf16[1,640]{1,0:T(2,128)(2,1)S(1)}, bf16[1,640]{1,0:T(2,128)(2,1)S(1)}, u32[]{:S(2)}, u32[]{:S(2)}) collective-permute-start(bf16[1,640]{1,0:T(2,128)(2,1)S(1)} %slice.156), channel_id=1, source_target_pairs={{8,0},{16,8},{24,16},{32,24},{40,32},{48,40},{56,48},{64,56},{72,6... | collective-permute-start | bytes 3848 | tf_op jit(solution)/shard_map/ppermute | solution.py:73
  198.7 8.5 %collective-permute-start.4 = (bf16[1,640]{1,0:T(2,128)(2,1)S(1)}, bf16[1,640]{1,0:T(2,128)(2,1)S(1)}, u32[]{:S(2)}, u32[]{:S(2)}) collective-permute-start(bf16[1,640]{1,0:T(2,128)(2,1)S(1)} %get-tuple-element.50), channel_id=1, source_target_pairs={{0,8},{8,16},{16,24},{24,32},{32,40},{40,48},{48,56},{56,64},{64,7... | collective-permute-start | bytes 3848 | tf_op jit(solution)/shard_map/ppermute | solution.py:73

commit v4 on v3

--- a/solution.py
+++ b/solution.py
@@ -22,9 +22,11 @@
 
 CTX = ("xh", "z", "co")
 TP = ("xl", "y")
-XZ = ("xh", "z")
+XY = ("xh", "xl", "y")
 N_CTX = 32
 N_TP = 8
+N_Z = 8
+N_XY = 16
 HEADS = 8
 HALF = 64
 ROWS = 128
@@ -33,6 +35,11 @@
 BLOCK = 512
 STEPS = 9
 
+ALL = CTX + TP
+ORDER = [c * N_TP + t for c in range(N_CTX) for t in range(N_TP // 2)] + [
+    c * N_TP + t for c in reversed(range(N_CTX)) for t in range(N_TP // 2, N_TP)
+]
+
 bf16 = jnp.bfloat16
 f32 = jnp.float32
 
@@ -67,42 +74,55 @@
     return lax.all_to_all(copies, axes, split_axis=0, concat_axis=0, tiled=True)
 
 
-def edge_exchange(first_row, second_row):
-    down = [(i + 1, i) for i in range(N_CTX - 1)]
-    up = [(i, i + 1) for i in range(N_CTX - 1)]
-    return lax.ppermute(first_row, CTX, down), lax.ppermute(second_row, CTX, up)
-
-
 def pack_keys(rows):
-    lead = rows[..., :LAT].reshape(2, 128, 4, 128).transpose(0, 2, 1, 3).reshape(8, 128, 128)
-    rope = jnp.concatenate([rows[0, :, LAT:KEYW], rows[1, :, LAT:KEYW]], axis=1)
+    lead = rows[:, :LAT].reshape(2, 64, 4, 128).transpose(0, 2, 1, 3).reshape(8, 64, 128)
+    rope = jnp.concatenate([rows[:64, LAT:KEYW], rows[64:, LAT:KEYW]], axis=1)
     return jnp.concatenate([lead, rope[None]], axis=0)
 
 
 def merge_kernel(in_ref, out_ref):
     total = in_ref[0].astype(f32)
-    for t in range(1, N_TP):
+    for t in range(1, N_XY):
         total = total + in_ref[t].astype(f32)
     total = total.astype(bf16)
-    for xh in range(2):
-        rope = total[8, :, xh * ROPE : (xh + 1) * ROPE]
+    for zh in range(2):
+        rope = total[8, :, zh * ROPE : (zh + 1) * ROPE]
         row = jnp.concatenate(
-            [total[xh * 4 + c] for c in range(4)] + [rope, jnp.zeros_like(rope)], axis=1
+            [total[zh * 4 + c] for c in range(4)] + [rope, jnp.zeros_like(rope)], axis=1
         )
-        for z in range(8):
-            out_ref[xh * 8 + z] = row[z * PIECE : (z + 1) * PIECE]
+        for z in range(4):
+            out_ref[zh * 4 + z] = row[z * PIECE : (z + 1) * PIECE]
 
 
 def merge(arrived):
     return pl.pallas_call(
         merge_kernel,
-        out_shape=jax.ShapeDtypeStruct((16, PIECE, WIDE), bf16),
+        out_shape=jax.ShapeDtypeStruct((N_Z, PIECE, WIDE), bf16),
         compiler_params=pltpu.CompilerParams(vmem_limit_bytes=16 * 1024 * 1024),
         cost_estimate=pl.CostEstimate(
-            flops=1_200_000, bytes_accessed=2_700_000, transcendentals=0
+            flops=1_200_000, bytes_accessed=2_500_000, transcendentals=0
         ),
         name="merge",
     )(arrived)
+
+
+def add_kernel(a_ref, b_ref, out_ref):
+    out_ref[...] = (a_ref[...].astype(f32) + b_ref[...].astype(f32)).astype(bf16)
+
+
+def add_cores(mine, received):
+    block = pl.BlockSpec((2, 9, 64, 128), lambda i: (i, 0, 0, 0))
+    return pl.pallas_call(
+        add_kernel,
+        grid=(N_XY // 2,),
+        in_specs=[block, block],
+        out_specs=block,
+        out_shape=jax.ShapeDtypeStruct(mine.shape, bf16),
+        cost_estimate=pl.CostEstimate(
+            flops=1_200_000, bytes_accessed=7_100_000, transcendentals=0
+        ),
+        name="add_cores",
+    )(mine, received)
 
 
 def attention_kernel(
@@ -161,11 +181,11 @@
     dqt_buf[...] = jnp.zeros_like(dqt_buf)
 
     def clear(t, carry):
-        dk_buf[0, t] = jnp.zeros((9, 128, 128), f32)
-        dk_buf[1, t] = jnp.zeros((9, 128, 128), f32)
+        dk_buf[0, t] = jnp.zeros((9, 64, 128), f32)
+        dk_buf[1, t] = jnp.zeros((9, 64, 128), f32)
         return carry
 
-    lax.fori_loop(0, N_TP, clear, 0)
+    lax.fori_loop(0, N_XY, clear, 0)
     for copy in copies[:4]:
         copy.wait()
 
@@ -180,22 +200,17 @@
         return late.astype(jnp.int32), half, block
 
     def slab(half, block):
-        xh = block // 2
-        at = pl.multiple_of((block % 2) * 64, 64)
+        x4 = (block // 2 * 2 + half) * 4
+        zh = block % 2
 
         def tile(part):
             return jnp.concatenate(
-                [
-                    keys[co, half * 4 + y, part, pl.ds(at, 64), :]
-                    for co in range(2)
-                    for y in range(4)
-                ],
-                axis=0,
+                [keys[co, x4 + y, part] for co in range(2) for y in range(4)], axis=0
             )
 
         rope = tile(8)
-        rope = jnp.where(xh == 0, rope[:, :ROPE], rope[:, ROPE:])
-        return jnp.concatenate([tile(xh * 4 + c) for c in range(4)] + [rope], axis=1)
+        rope = jnp.where(zh == 0, rope[:, :ROPE], rope[:, ROPE:])
+        return jnp.concatenate([tile(zh * 4 + c) for c in range(4)] + [rope], axis=1)
 
     def nn(a, b):
         return jnp.dot(a, b, preferred_element_type=f32)
@@ -250,19 +265,16 @@
             rest = nn(ds, q_ref[seg, part, LAT:])
             lead = more if lead is None else lead + more
             tail = rest if at == 0 else tail + rest
-        xh = block // 2
-        at = pl.multiple_of((block % 2) * 64, 64)
+        x4 = (block // 2 * 2 + half) * 4
+        zh = block % 2
         lane = lax.broadcasted_iota(jnp.int32, (1, 128), 1)
-        tail = jnp.where(lane // ROPE == xh, jnp.concatenate([tail, tail], axis=1), 0.0)
+        tail = jnp.where(lane // ROPE == zh, jnp.concatenate([tail, tail], axis=1), 0.0)
         for co in range(2):
             for y in range(4):
                 j = (co * 4 + y) * 64
-                own = half * 4 + y
                 for c in range(4):
-                    dk_buf[co, own, xh * 4 + c, pl.ds(at, 64), :] += lead[
-                        j : j + 64, c * 128 : c * 128 + 128
-                    ]
-                dk_buf[co, own, 8, pl.ds(at, 64), :] += tail[j : j + 64]
+                    dk_buf[co, x4 + y, zh * 4 + c] += lead[j : j + 64, c * 128 : c * 128 + 128]
+                dk_buf[co, x4 + y, 8] += tail[j : j + 64]
         return carry
 
     lax.fori_loop(0, STEPS, second, 0)
@@ -275,12 +287,12 @@
         sends.append(copy)
 
     send(dqt_buf.at[:, pl.ds(LAT, ROPE)], tailt_hbm)
-    for t in range(N_TP):
-        dk_out[0, t] = dk_buf[1 - core, t].astype(bf16)
-        send(dk_out.at[0, t], dother_ref.at[t])
-    for t in range(N_TP):
-        dk_out[1, t] = dk_buf[core, t].astype(bf16)
-        send(dk_out.at[1, t], dmine_ref.at[t])
+    for t in range(0, N_XY, 2):
+        dk_out[0, t : t + 2] = dk_buf[1 - core, t : t + 2].astype(bf16)
+        send(dk_out.at[0, pl.ds(t, 2)], dother_ref.at[pl.ds(t, 2)])
+    for t in range(0, N_XY, 2):
+        dk_out[1, t : t + 2] = dk_buf[core, t : t + 2].astype(bf16)
+        send(dk_out.at[1, pl.ds(t, 2)], dmine_ref.at[pl.ds(t, 2)])
     for seg in range(2):
         ot_out[seg] = ot_buf[seg].astype(bf16)
         send(ot_out.at[seg], ot_hbm.at[seg])
@@ -292,7 +304,7 @@
 
 def attention(where, mine, other, q, qt, g, gt):
     hbm = pl.BlockSpec(memory_space=pl.ANY)
-    half_keys = (N_TP, 9, 128, 128)
+    half_keys = (N_XY, 9, 64, 128)
     return pl.pallas_call(
         attention_kernel,
         in_specs=[pl.BlockSpec(memory_space=pltpu.SMEM)] + [hbm] * 6,
@@ -324,7 +336,7 @@
             pltpu.SemaphoreType.DMA((6,)),
             pltpu.SemaphoreType.DMA((21,)),
         ],
-        compiler_params=pltpu.CompilerParams(vmem_limit_bytes=58 * 1024 * 1024),
+        compiler_params=pltpu.CompilerParams(vmem_limit_bytes=60 * 1024 * 1024),
         cost_estimate=pl.CostEstimate(
             flops=14_000_000_000, bytes_accessed=20_000_000, transcendentals=4_000_000
         ),
@@ -348,28 +360,22 @@
     ctx = lax.axis_index(CTX)
     core = lax.axis_index("co")
     tp = lax.axis_index(TP)
-    last = ctx == N_CTX - 1
-
-    after, before = edge_exchange(embed[0:1], embed[HALF : HALF + 1])
-    after_early = jnp.where(last, embed[HALF : HALF + 1], after)
-    next_embed = jnp.concatenate(
-        [embed[1:HALF], after_early, embed[HALF + 1 :], before], axis=0
-    )
+
     hidden_wide = hidden.astype(f32)
-    next_wide = next_embed.astype(f32)
+    embed_wide = embed.astype(f32)
     part_hidden = jnp.dot(
         (hidden_wide * gain_hidden).astype(bf16), proj_hidden, preferred_element_type=f32
     )
-    part_next = jnp.dot(
-        (next_wide * gain_embed).astype(bf16), proj_embed, preferred_element_type=f32
+    part_embed = jnp.dot(
+        (embed_wide * gain_embed).astype(bf16), proj_embed, preferred_element_type=f32
     )
     spread = (ROWS, WIDE - KEYW)
     parts = jnp.concatenate(
         [
             part_hidden,
             jnp.broadcast_to(jnp.sum(hidden_wide * hidden_wide, axis=1, keepdims=True), spread),
-            part_next,
-            jnp.broadcast_to(jnp.sum(next_wide * next_wide, axis=1, keepdims=True), spread),
+            part_embed,
+            jnp.broadcast_to(jnp.sum(embed_wide * embed_wide, axis=1, keepdims=True), spread),
         ],
         axis=1,
     ).reshape(N_TP, PIECE, 2 * WIDE)
@@ -377,9 +383,12 @@
 
     parts, queries, grad_out = lax.optimization_barrier((parts, queries, grad_out))
     parts = jnp.sum(parts, axis=0)
-    part_hidden, part_next = parts[:, :KEYW], parts[:, WIDE : WIDE + KEYW]
+    nexts = parts[:, WIDE:]
+    after = lax.ppermute(nexts[:1], ALL, [(b, a) for a, b in zip(ORDER[:-1], ORDER[1:])])
+    nexts = jnp.concatenate([nexts[1:], after], axis=0)
+    part_hidden, part_next = parts[:, :KEYW], nexts[:, :KEYW]
     inv_hidden = lax.rsqrt(parts[:, KEYW : KEYW + 1] / D + EPSILON)
-    inv_next = lax.rsqrt(parts[:, WIDE + KEYW : WIDE + KEYW + 1] / D + EPSILON)
+    inv_next = lax.rsqrt(nexts[:, KEYW : KEYW + 1] / D + EPSILON)
     latent = inv_hidden * part_hidden + inv_next * part_next
     leading = latent[:, :LAT]
     inv_latent = lax.rsqrt(jnp.mean(leading * leading, axis=1, keepdims=True) + EPSILON)
@@ -392,8 +401,8 @@
         ],
         axis=1,
     )
-    same = pack_keys(gather_copies(key_piece, XZ, 16).reshape(2, 128, WIDE))
-    mine = gather_copies(same, TP, N_TP)
+    same = pack_keys(gather_copies(key_piece, "z", N_Z).reshape(128, WIDE))
+    mine = gather_copies(same, XY, N_XY)
 
     cos_table, sin_table = rotation(row_positions(ctx, jnp.arange(ROWS)))
     cos_table = cos_table.reshape(2, 1, HALF, ROPE // 2)
@@ -424,8 +433,8 @@
     )
 
     received = lax.ppermute(dother, "co", [(0, 1), (1, 0)])
-    dkey = (dmine.astype(f32) + received.astype(f32)).astype(bf16)
-    dkey = lax.all_to_all(dkey, TP, split_axis=0, concat_axis=0, tiled=True)
+    dkey = add_cores(dmine, received)
+    dkey = lax.all_to_all(dkey, XY, split_axis=0, concat_axis=0, tiled=True)
 
     attended = jnp.einsum(
         "glhs,lhv->gshv",
@@ -447,7 +456,7 @@
     grad_queries = grad_queries.transpose(0, 2, 1, 3).reshape(ROWS, HEADS * (NOPE + ROPE))
     dkey, attended, grad_queries = lax.optimization_barrier((dkey, attended, grad_queries))
 
-    dkey = lax.all_to_all(merge(dkey), XZ, split_axis=0, concat_axis=0, tiled=True)
+    dkey = lax.all_to_all(merge(dkey), "z", split_axis=0, concat_axis=0, tiled=True)
     dkey = jnp.sum(dkey.astype(f32), axis=0)[:, :KEYW]
 
     gained = gain_latent * dkey[:, :LAT]
@@ -468,12 +477,15 @@
         width = (PIECE, (WIDE - KEYW) // 2)
         return [jnp.broadcast_to(high, width), jnp.broadcast_to(low, width)]
 
+    packed_hidden = jnp.concatenate(
+        [(inv_hidden * dlatent).astype(bf16)] + in_two(coef_hidden), axis=1
+    )
+    packed_next = jnp.concatenate(
+        [(inv_next * dlatent).astype(bf16)] + in_two(coef_next), axis=1
+    )
+    before = lax.ppermute(packed_next[-1:], ALL, list(zip(ORDER[:-1], ORDER[1:])))
     packed = jnp.concatenate(
-        [(inv_hidden * dlatent).astype(bf16)]
-        + in_two(coef_hidden)
-        + [(inv_next * dlatent).astype(bf16)]
-        + in_two(coef_next),
-        axis=1,
+        [packed_hidden, jnp.concatenate([before, packed_next[:-1]], axis=0)], axis=1
     )
     packed = gather_copies(packed, TP, N_TP).reshape(ROWS, 2 * WIDE)
 
@@ -488,17 +500,11 @@
         - coef_hidden * hidden_wide
     ).astype(bf16)
 
-    nexts = packed[:, WIDE:]
-    after, before = edge_exchange(nexts[ROWS - 1 :], nexts[HALF - 1 : HALF])
-    before_late = jnp.where(last, nexts[HALF - 1 : HALF], after)
-    shifted = jnp.concatenate(
-        [before, nexts[: HALF - 1], before_late, nexts[HALF : ROWS - 1]], axis=0
-    )
-    dpart_next, coef_next = whole(shifted)
+    dpart_next, coef_next = whole(packed[:, WIDE:])
     grad_embed = (
         gain_embed
         * jnp.einsum("rc,dc->rd", dpart_next, proj_embed, preferred_element_type=f32)
-        - coef_next * embed.astype(f32)
+        - coef_next * embed_wide
     ).astype(bf16)
     return (attended, grad_queries, grad_hidden, grad_embed)
 

time: 210 us -> 212 us (level)
  blocking collectives: 44.9 us -> 36.6 us
  Pallas kernels: 29.8 us -> 36.1 us
  waiting for transfers between devices: 51.9 us -> 55.8 us
    all_to_all x1, blocking collectives: 19.7 us -> 11.9 us  [on_device(): lax.all_to_all(merge(dkey), 'z', split_axis=0, concat_axis=0, tiled=True)]
    pallas_call x1 -> x2, Pallas kernels: 0.47 us -> 6.79 us  [the longest x1 6.38 us: add_cores(): pl.pallas_call(add_kernel, grid=(N_XY // 2,), in_specs=[block, block], ou...]
    ppermute x4 -> x2, starting transfers between devices: 15.2 us -> 9.88 us  [the longest x1 7.41 us: on_device(): lax.ppermute(nexts[:1], ALL, [(b, a) for a, b in zip(ORDER[:-1], ORDER[1:...]
    all_to_all x1, starting transfers between devices: 3.8 us -> 7.91 us  [on_device(): dkey = lax.all_to_all(dkey, XY, split_axis=0, concat_axis=0, tiled=True)]
    all_to_all x1, starting transfers between devices: 4.5 us -> 8.53 us  [gather_copies(): return lax.all_to_all(copies, axes, split_axis=0, concat_axis=0, tiled=True)]
    convert_element_type x1, other arithmetic: 4.34 us -> 0.81 us  [in_two(): high = c.astype(bf16)]
    ppermute x4 -> x2, waiting for transfers between devices: 10.3 us -> 9.03 us  [the longest x1 7.95 us: on_device(): lax.ppermute(packed_next[-1:], ALL, list(zip(ORDER[:-1], ORDER[1:])))]
    unnamed x38 -> x64, local copies, waits for them, and re-layouts: 5.01 us -> 5.63 us
  transfers between devices with their start and end apart: 9 -> 7, of which waited for: 8 -> 7; matrix products, arithmetic and copies ran while one was open for 17% -> 14% of each run, Pallas kernels for 0% -> 0%
where the time goes in v4:
time: 212 us; the launch traced here: 211 us
  waiting for transfers between devices  55.8 us (26%)
  blocking collectives  36.6 us (17%)
  Pallas kernels  36.1 us (17%)
  starting transfers between devices  31.7 us (15%)
  local copies, waits for them, and re-layouts  27.8 us (13%)
  other arithmetic  11 us (5%)
  matrix products  10.9 us (5%)
    pallas_call x1, Pallas kernels, attention(): pl.pallas_call(attention_kernel, in_specs=[pl.BlockSpec(memory_space=pltp...  29.3 us
    all_to_all x2, blocking collectives, gather_copies(): return lax.all_to_all(copies, axes, split_axis=0, concat_axis=0, tiled=True)  24.6 us
    all_to_all x1, waiting for transfers between devices, gather_copies(): return lax.all_to_all(copies, axes, split_axis=0, concat_axis=0, tiled=True)  14.7 us
    all_to_all x1, waiting for transfers between devices, on_device(): dkey = lax.all_to_all(dkey, XY, split_axis=0, concat_axis=0, tiled=True)  12.8 us
    all_to_all x1, blocking collectives, on_device(): lax.all_to_all(merge(dkey), 'z', split_axis=0, concat_axis=0, tiled=True)  11.9 us
    all_to_all x1, waiting for transfers between devices, on_device(): parts = lax.all_to_all(parts, TP, split_axis=0, concat_axis=0, tiled=True)  10.5 us
    all_to_all x1, starting transfers between devices, gather_copies(): return lax.all_to_all(copies, axes, split_axis=0, concat_axis=0, tiled=True)  8.53 us
    ppermute x1, waiting for transfers between devices, on_device(): lax.ppermute(packed_next[-1:], ALL, list(zip(ORDER[:-1], ORDER[1:])))  7.95 us
  transfers between devices with their start and end apart: 7, of which 7 were waited for; matrix products, arithmetic and copies ran while one was open for 14% of the time, Pallas kernels for 0%

profile of v4, /device:TPU:4, one launch (start us, length us, event | category | flops | bytes accessed | tf_op | source)
XLA Modules:
  0.0 211.0 jit_solution(12411331803729489014)
XLA Ops:
  0.6 1.2 fusion.15
  1.8 1.1 fusion.17
  2.9 1.8 fusion.22
  4.7 1.4 fusion.20
  6.2 1.1 copy.92
  7.2 5.1 %all-to-all-start = ((f32[8,16,1280]{2,1,0:T(8,128)}), f32[8,16,1280]{2,1,0:T(8,128)S(1)}, u32[]{:S(2)}, u32[]{:S(2)}) async-start(f32[8,16,1280]{2,1,0:T(8,128)} %bitcast.2), calls=%async_computation | async-start | bytes 1310720 | tf_op jit(solution)/shard_map/all_to_all | solution.py:382
  12.5 10.5 %all-to-all-done = f32[8,16,1280]{2,1,0:T(8,128)S(1)} async-done(((f32[8,16,1280]{2,1,0:T(8,128)}), f32[8,16,1280]{2,1,0:T(8,128)S(1)}, u32[]{:S(2)}, u32[]{:S(2)}) %all-to-all-start) | async-done | bytes 655392 | tf_op jit(solution)/shard_map/all_to_all | solution.py:382
  23.0 7.4 %collective-permute-start = (f32[1,640]{1,0:T(1,128)S(1)}, f32[1,640]{1,0:T(1,128)S(1)}, u32[]{:S(2)}, u32[]{:S(2)}) collective-permute-start(f32[1,640]{1,0:T(1,128)S(1)} %slice.107), channel_id=1, source_target_pairs={{1,0},{2,1},{3,2},{8,3},{9,8},{10,9},{11,10},{16,11},{17,16},{18,1... | collective-permute-start | bytes 7688 | tf_op jit(solution)/shard_map/ppermute | solution.py:387
  30.5 0.2 fusion.51
  30.7 1.1 collective-permute-done
  31.7 0.8 fusion.58
  32.7 0.3 copy-done.18
  33.1 0.6 multiply_multiply_fusion.2
  33.9 0.3 copy-done.27
  34.3 14.5 %all_to_all.30 = bf16[8,16,640]{2,1,0:T(8,128)(2,1)S(1)} all-to-all(bf16[8,16,640]{2,1,0:T(8,128)(2,1)S(1)} %broadcast_in_dim.37), channel_id=1, replica_groups=mesh['xh'=2,'z'=8,'co'=2,'xl'=2,'y'=4] {'z'}, dimensions={0} | all-to-all | bytes 327680 | tf_op jit(solution)/shard_map/all_to_all | solution.py:74
  48.9 2.0 broadcast_in_dim.39
  50.9 8.5 %all-to-all-start.2 = ((bf16[16,9,64,128]{3,2,1,0:T(8,128)(2,1)}), bf16[16,9,64,128]{3,2,1,0:T(8,128)(2,1)}, u32[]{:S(2)}, u32[]{:S(2)}) async-start(bf16[16,9,64,128]{3,2,1,0:T(8,128)(2,1)} %broadcast_in_dim.39), calls=%async_computation.2 | async-start | bytes 4718592 | tf_op jit(solution)/shard_map/all_to_all | solution.py:74
  59.5 0.3 copy.125
  59.8 0.9 copy-done.11
  60.7 0.3 copy.127
  61.0 1.0 multiply_cosine_fusion
  62.0 0.8 copy.126
  62.7 2.3 %reshape.141 = bf16[2,64,8,192]{3,2,1,0:T(8,128)(2,1)} reshape(bf16[128,1536]{1,0:T(8,128)(2,1)} %param.20) | data formatting | bytes 786432 | tf_op jit(solution)/shard_map/reshape | solution.py:412
  65.0 1.1 copy.145
  66.2 1.1 subtract_convert_fusion.1
  67.3 0.5 fusion
  67.8 0.2 pad_maximum_fusion
  68.2 0.5 copy-done.9
  68.7 0.5 fusion.1
  69.3 1.3 copy.101
  70.6 1.4 copy.97
  72.0 14.7 %all-to-all-done.2.mine_ref = bf16[16,9,64,128]{3,2,1,0:T(8,128)(2,1)} async-done(((bf16[16,9,64,128]{3,2,1,0:T(8,128)(2,1)}), bf16[16,9,64,128]{3,2,1,0:T(8,128)(2,1)}, u32[]{:S(2)}, u32[]{:S(2)}) %all-to-all-start.2) | async-done | bytes 2359328 | tf_op jit(solution)/shard_map/all_to_all | solution.py:74
  86.7 0.7 pad_add_fusion.where_ref
  87.3 4.2 %collective-permute-done.1.other_ref = bf16[16,9,64,128]{3,2,1,0:T(8,128)(2,1)} collective-permute-done((bf16[16,9,64,128]{3,2,1,0:T(8,128)(2,1)}, bf16[16,9,64,128]{3,2,1,0:T(8,128)(2,1)}, u32[]{:S(2)}, u32[]{:S(2)}) %collective-permute-start.1) | collective-permute-done | bytes 2359328 | tf_op jit(solution)/shard_map/ppermute | solution.py:428
  91.6 29.3 %attention.1 = (bf16[2,512,512]{2,1,0:T(8,128)(2,1)}, bf16[2,512,512]{2,1,0:T(8,128)(2,1)}, f32[2,64,512]{2,1,0:T(8,128)}, bf16[16,9,64,128]{3,2,1,0:T(8,128)(2,1)}, bf16[16,9,64,128]{3,2,1,0:T(8,128)(2,1)}) custom-call(s32[2]{0:T(128)} %pad_add_fusion.where_ref, bf16[16,9,64,128]{3,2,1,0:T(8,128)(2,1)} %all-to-all-done.2.mine_ref, ...), custom_call_target="tpu_custom_call" | custom-call | flops 14000000000 | bytes 20000000 | tf_op jit(solution)/shard_map/attention/pallas_call | solution.py:308
  120.8 0.2 collective-permute-start.2
  121.1 4.6 %collective-permute-done.2.b_ref = bf16[16,9,64,128]{3,2,1,0:T(8,128)(2,1)S(1)} collective-permute-done((bf16[16,9,64,128]{3,2,1,0:T(8,128)(2,1)}, bf16[16,9,64,128]{3,2,1,0:T(8,128)(2,1)S(1)}, u32[]{:S(2)}, u32[]{:S(2)}) %collective-permute-start.2) | collective-permute-done | bytes 2359328 | tf_op jit(solution)/shard_map/ppermute | solution.py:435
  125.7 1.4 copy-done.6
  127.1 6.4 %add_cores.1 = bf16[16,9,64,128]{3,2,1,0:T(8,128)(2,1)} custom-call(bf16[16,9,64,128]{3,2,1,0:T(8,128)(2,1)} %get-tuple-element.28.a_ref, bf16[16,9,64,128]{3,2,1,0:T(8,128)(2,1)} %copy-done.6), custom_call_target="tpu_custom_call" | custom-call | flops 1200000 | bytes 7100000 | tf_op jit(solution)/shard_map/add_cores/pallas_call | solution.py:115
  133.5 7.9 %all-to-all-start.3 = ((bf16[16,9,64,128]{3,2,1,0:T(8,128)(2,1)}), bf16[16,9,64,128]{3,2,1,0:T(8,128)(2,1)S(1)}, u32[]{:S(2)}, u32[]{:S(2)}) async-start(bf16[16,9,64,128]{3,2,1,0:T(8,128)(2,1)} %add_cores.1), calls=%async_computation.3 | async-start | bytes 4718592 | tf_op jit(solution)/shard_map/all_to_all | solution.py:437
  141.4 1.9 reshape.150
  143.3 2.0 copy.109
  145.3 2.3 %copy.102 = bf16[2,512,512]{1,2,0:T(8,128)(2,1)} copy(bf16[2,512,512]{2,1,0:T(8,128)(2,1)} %get-tuple-element.30) | data formatting | bytes 2097152 | tf_op jit(solution)/shard_map/attention/pallas_call | solution.py:308
  147.6 2.0 fusion.6
  149.6 0.2 copy.105
  149.8 0.8 copy.146
  150.5 2.3 %copy.106 = bf16[2,512,512]{1,2,0:T(8,128)(2,1)} copy(bf16[2,512,512]{2,1,0:T(8,128)(2,1)} %get-tuple-element.31) | data formatting | bytes 2097152 | tf_op jit(solution)/shard_map/attention/pallas_call | solution.py:308
  152.8 1.4 add_convert_fusion
  154.2 2.0 fusion.7
  156.3 0.2 maximum_bitcast_fusion
  156.4 1.1 copy.110
  157.5 2.3 %reshape.151 = bf16[128,1536]{1,0:T(8,128)(2,1)} reshape(bf16[2,64,8,192]{3,2,1,0:T(8,128)(2,1)} %copy.110) | data formatting | bytes 786432 | tf_op jit(solution)/shard_map/reshape | solution.py:456
  159.8 12.8 %all-to-all-done.3.in_ref = bf16[16,9,64,128]{3,2,1,0:T(8,128)(2,1)S(1)} async-done(((bf16[16,9,64,128]{3,2,1,0:T(8,128)(2,1)}), bf16[16,9,64,128]{3,2,1,0:T(8,128)(2,1)S(1)}, u32[]{:S(2)}, u32[]{:S(2)}) %all-to-all-start.3) | async-done | bytes 2359328 | tf_op jit(solution)/shard_map/all_to_all | solution.py:437
  172.6 0.4 merge.1
  173.1 11.9 %all_to_all.31 = bf16[8,16,640]{2,1,0:T(8,128)(2,1)S(1)} all-to-all(bf16[8,16,640]{2,1,0:T(8,128)(2,1)S(1)} %merge.1), channel_id=1, replica_groups=mesh['xh'=2,'z'=8,'co'=2,'xl'=2,'y'=4] {'z'}, dimensions={0} | all-to-all | bytes 327680 | tf_op jit(solution)/shard_map/all_to_all | solution.py:459
  185.4 0.2 multiply_reduce_fusion
  185.8 0.8 fusion.55
  186.8 2.5 %collective-permute-start.3 = (bf16[1,640]{1,0:T(2,128)(2,1)S(1)}, bf16[1,640]{1,0:T(2,128)(2,1)S(1)}, u32[]{:S(2)}, u32[]{:S(2)}) collective-permute-start(bf16[1,640]{1,0:T(2,128)(2,1)S(1)} %pad_maximum_fusion.7), channel_id=1, source_target_pairs={{0,1},{1,2},{2,3},{3,8},{8,9},{9,10},{10,11},{11,16},{16,17},{17,1... | collective-permute-start | bytes 3848 | tf_op jit(solution)/shard_map/ppermute | solution.py:486
  189.3 0.2 fusion.52
  189.5 8.0 %collective-permute-done.3 = bf16[1,640]{1,0:T(2,128)(2,1)S(1)} collective-permute-done((bf16[1,640]{1,0:T(2,128)(2,1)S(1)}, bf16[1,640]{1,0:T(2,128)(2,1)S(1)}, u32[]{:S(2)}, u32[]{:S(2)}) %collective-permute-start.3) | collective-permute-done | bytes 1312 | tf_op jit(solution)/shard_map/ppermute | solution.py:486
  197.8 10.1 %all_to_all.32 = bf16[8,16,1280]{2,1,0:T(8,128)(2,1)S(1)} all-to-all(bf16[8,16,1280]{2,1,0:T(8,128)(2,1)S(1)} %broadcast_in_dim.98), channel_id=1, replica_groups=mesh['xh'=2,'z'=8,'co'=2,'xl'=2,'y'=4] {'xl','y'}, dimensions={0} | all-to-all | bytes 655360 | tf_op jit(solution)/shard_map/all_to_all | solution.py:74
  208.0 0.2 add_reduce_fusion
  208.1 1.7 fusion.4
  209.9 1.1 fusion.5
  (96 shorter events, 2.3 us)
Async XLA Ops:
  0.6 4.0 %copy-start = (bf16[896,576]{0,1:T(8,128)(2,1)S(1)}, bf16[896,576]{0,1:T(8,128)(2,1)}, u32[]{:S(2)}) copy-start(bf16[896,576]{0,1:T(8,128)(2,1)} %param.16) | copy-start | bytes 3096580
  6.1 27.7 %copy-start.15 = (f32[512]{0:T(512)S(1)}, f32[512]{0:T(512)}, u32[]{:S(2)}) copy-start(f32[512]{0:T(512)} %param.17) | copy-start | bytes 6148
  7.2 15.8 %all-to-all-start = ((f32[8,16,1280]{2,1,0:T(8,128)}), f32[8,16,1280]{2,1,0:T(8,128)S(1)}, u32[]{:S(2)}, u32[]{:S(2)}) async-start(f32[8,16,1280]{2,1,0:T(8,128)} %bitcast.2), calls=%async_computation | async-start | bytes 1310720 | tf_op jit(solution)/shard_map/all_to_all | solution.py:382
  12.4 38.5 %copy-start.20 = (f32[32]{0:T(128)}, f32[32]{0:T(128)S(1)}, u32[]{:S(2)}) copy-start(f32[32]{0:T(128)S(1)} %multiply_power_fusion) | copy-start | bytes 388
  12.4 38.5 %copy-start.25 = (f32[16]{0:T(128)}, f32[16]{0:T(128)S(1)}, u32[]{:S(2)}) copy-start(f32[16]{0:T(128)S(1)} %fusion.57) | copy-start | bytes 196
  23.0 8.7 %collective-permute-start = (f32[1,640]{1,0:T(1,128)S(1)}, f32[1,640]{1,0:T(1,128)S(1)}, u32[]{:S(2)}, u32[]{:S(2)}) collective-permute-start(f32[1,640]{1,0:T(1,128)S(1)} %slice.107), channel_id=1, source_target_pairs={{1,0},{2,1},{3,2},{8,3},{9,8},{10,9},{11,10},{16,11},{17,16},{18,1... | collective-permute-start | bytes 7688 | tf_op jit(solution)/shard_map/ppermute | solution.py:387
  30.6 2.1 copy-start.23
  31.7 2.1 %copy-start.13 = (f32[1,640]{1,0:T(1,128)}, f32[1,640]{1,0:T(1,128)S(1)}, u32[]{:S(2)}) copy-start(f32[1,640]{1,0:T(1,128)S(1)} %collective-permute-done) | copy-start | bytes 7684
  32.5 0.5 copy-start.18
  33.7 0.5 copy-start.27
  50.9 8.6 %copy-start.10 = (bf16[512,1024]{1,0:T(8,128)(2,1)S(1)}, bf16[512,1024]{1,0:T(8,128)(2,1)}, u32[]{:S(2)}) copy-start(bf16[512,1024]{1,0:T(8,128)(2,1)} %param.18) | copy-start | bytes 3145732
  50.9 35.8 %all-to-all-start.2 = ((bf16[16,9,64,128]{3,2,1,0:T(8,128)(2,1)}), bf16[16,9,64,128]{3,2,1,0:T(8,128)(2,1)}, u32[]{:S(2)}, u32[]{:S(2)}) async-start(bf16[16,9,64,128]{3,2,1,0:T(8,128)(2,1)} %broadcast_in_dim.39), calls=%async_computation.2 | async-start | bytes 4718592 | tf_op jit(solution)/shard_map/all_to_all | solution.py:74
  59.5 1.2 copy-start.11
  59.5 1.5 copy-start.21
  59.5 2.5 %copy-start.12 = (bf16[128,1024]{1,0:T(8,128)(2,1)S(1)}, bf16[128,1024]{1,0:T(8,128)(2,1)}, u32[]{:S(2)}) copy-start(bf16[128,1024]{1,0:T(8,128)(2,1)} %param.21) | copy-start | bytes 786436
  59.8 7.5 %copy-start.2 = (bf16[64,8,8,128]{3,2,1,0:T(8,128)(2,1)}, bf16[64,8,8,128]{3,2,1,0:T(8,128)(2,1)S(1)}, u32[]{:S(2)}) copy-start(bf16[64,8,8,128]{3,2,1,0:T(8,128)(2,1)S(1)} %copy.125) | copy-start | bytes 3145732
  61.0 7.2 %copy-start.3 = (bf16[64,8,8,128]{3,2,1,0:T(8,128)(2,1)}, bf16[64,8,8,128]{3,2,1,0:T(8,128)(2,1)S(1)}, u32[]{:S(2)}) copy-start(bf16[64,8,8,128]{3,2,1,0:T(8,128)(2,1)S(1)} %copy.127) | copy-start | bytes 3145732
  67.8 1.0 copy-start.9
  68.2 2.5 %copy-start.1 = (bf16[2,8,64,576]{3,2,1,0:T(8,128)(2,1)}, bf16[2,8,64,576]{3,2,1,0:T(8,128)(2,1)S(1)}, u32[]{:S(2)}) copy-start(bf16[2,8,64,576]{3,2,1,0:T(8,128)(2,1)S(1)} %copy.96) | copy-start | bytes 3538948
  69.3 22.3 %copy-start.4 = (bf16[2,8,64,512]{3,2,1,0:T(8,128)(2,1)}, bf16[2,8,64,512]{3,2,1,0:T(8,128)(2,1)S(1)}, u32[]{:S(2)}) copy-start(bf16[2,8,64,512]{3,2,1,0:T(8,128)(2,1)S(1)} %copy.100) | copy-start | bytes 3145732
  86.7 4.9 %collective-permute-start.1 = (bf16[16,9,64,128]{3,2,1,0:T(8,128)(2,1)}, bf16[16,9,64,128]{3,2,1,0:T(8,128)(2,1)}, u32[]{:S(2)}, u32[]{:S(2)}) collective-permute-start(bf16[16,9,64,128]{3,2,1,0:T(8,128)(2,1)} %all-to-all-done.2.mine_ref), channel_id=1, source_target_pairs={{0,8},{8,0},{1,9},{9,1},{2,10},{10,2},{3,11},{11,3},{4,12},{12,4},... | collective-permute-start | bytes 7077896 | tf_op jit(solution)/shard_map/ppermute | solution.py:428
  120.8 4.8 %collective-permute-start.2 = (bf16[16,9,64,128]{3,2,1,0:T(8,128)(2,1)}, bf16[16,9,64,128]{3,2,1,0:T(8,128)(2,1)S(1)}, u32[]{:S(2)}, u32[]{:S(2)}) collective-permute-start(bf16[16,9,64,128]{3,2,1,0:T(8,128)(2,1)} %get-tuple-element.29), channel_id=1, source_target_pairs={{0,8},{8,0},{1,9},{9,1},{2,10},{10,2},{3,11},{11,3},{4,12},{12,4},... | collective-permute-start | bytes 7077896 | tf_op jit(solution)/shard_map/ppermute | solution.py:435
  125.7 1.4 copy-start.6
  133.5 39.0 %all-to-all-start.3 = ((bf16[16,9,64,128]{3,2,1,0:T(8,128)(2,1)}), bf16[16,9,64,128]{3,2,1,0:T(8,128)(2,1)S(1)}, u32[]{:S(2)}, u32[]{:S(2)}) async-start(bf16[16,9,64,128]{3,2,1,0:T(8,128)(2,1)} %add_cores.1), calls=%async_computation.3 | async-start | bytes 4718592 | tf_op jit(solution)/shard_map/all_to_all | solution.py:437
  172.5 12.5 %copy-start.16 = (f32[512]{0:T(512)S(1)}, f32[512]{0:T(512)}, u32[]{:S(2)}) copy-start(f32[512]{0:T(512)} %param.17) | copy-start | bytes 6148
  172.6 12.6 %copy-start.22 = (f32[32]{0:T(128)S(1)}, f32[32]{0:T(128)}, u32[]{:S(2)}) copy-start(f32[32]{0:T(128)} %copy-done.20) | copy-start | bytes 388
  172.6 12.6 %copy-start.26 = (f32[16]{0:T(128)S(1)}, f32[16]{0:T(128)}, u32[]{:S(2)}) copy-start(f32[16]{0:T(128)} %copy-done.25) | copy-start | bytes 196
  172.6 12.7 %copy-start.28 = (f32[16]{0:T(128)S(1)}, f32[16]{0:T(128)}, u32[]{:S(2)}) copy-start(f32[16]{0:T(128)} %copy-done.27) | copy-start | bytes 196
  172.6 12.8 %copy-start.29 = (f32[16]{0:T(128)S(1)}, f32[16]{0:T(128)}, u32[]{:S(2)}) copy-start(f32[16]{0:T(128)} %get-tuple-element.60) | copy-start | bytes 196
  172.6 12.8 %copy-start.14 = (f32[1,640]{1,0:T(1,128)S(1)}, f32[1,640]{1,0:T(1,128)}, u32[]{:S(2)}) copy-start(f32[1,640]{1,0:T(1,128)} %copy-done.13) | copy-start | bytes 7684
  172.6 12.8 %copy-start.19 = (f32[16]{0:T(128)S(1)}, f32[16]{0:T(128)}, u32[]{:S(2)}) copy-start(f32[16]{0:T(128)} %copy-done.18) | copy-start | bytes 196
  172.6 12.8 %copy-start.24 = (f32[16]{0:T(128)S(1)}, f32[16]{0:T(128)}, u32[]{:S(2)}) copy-start(f32[16]{0:T(128)} %copy-done.23) | copy-start | bytes 196
  173.0 35.1 %copy-start.7 = (bf16[128,896]{1,0:T(8,128)(2,1)S(1)}, bf16[128,896]{1,0:T(8,128)(2,1)}, u32[]{:S(2)}) copy-start(bf16[128,896]{1,0:T(8,128)(2,1)} %param.12) | copy-start | bytes 688132
  173.0 36.9 %copy-start.5 = (bf16[896,576]{0,1:T(8,128)(2,1)S(1)}, bf16[896,576]{0,1:T(8,128)(2,1)}, u32[]{:S(2)}) copy-start(bf16[896,576]{0,1:T(8,128)(2,1)} %param.15) | copy-start | bytes 3096580
  173.0 36.9 %copy-start.8 = (bf16[128,896]{1,0:T(8,128)(2,1)S(1)}, bf16[128,896]{1,0:T(8,128)(2,1)}, u32[]{:S(2)}) copy-start(bf16[128,896]{1,0:T(8,128)(2,1)} %param.11) | copy-start | bytes 688132
  173.0 36.9 %copy-start.17 = (f32[896]{0:T(1024)S(1)}, f32[896]{0:T(1024)}, u32[]{:S(2)}) copy-start(f32[896]{0:T(1024)} %param.13) | copy-start | bytes 10756
  186.8 10.6 %collective-permute-start.3 = (bf16[1,640]{1,0:T(2,128)(2,1)S(1)}, bf16[1,640]{1,0:T(2,128)(2,1)S(1)}, u32[]{:S(2)}, u32[]{:S(2)}) collective-permute-start(bf16[1,640]{1,0:T(2,128)(2,1)S(1)} %pad_maximum_fusion.7), channel_id=1, source_target_pairs={{0,1},{1,2},{2,3},{3,8},{8,9},{9,10},{10,11},{11,16},{16,17},{17,1... | collective-permute-start | bytes 3848 | tf_op jit(solution)/shard_map/ppermute | solution.py:486

commit v5 on v4

--- a/solution.py
+++ b/solution.py
@@ -22,6 +22,7 @@
 
 CTX = ("xh", "z", "co")
 TP = ("xl", "y")
+XZ = ("xh", "z")
 XY = ("xh", "xl", "y")
 N_CTX = 32
 N_TP = 8
@@ -74,9 +75,15 @@
     return lax.all_to_all(copies, axes, split_axis=0, concat_axis=0, tiled=True)
 
 
+def edge_exchange(first_row, second_row):
+    down = [(i + 1, i) for i in range(N_CTX - 1)]
+    up = [(i, i + 1) for i in range(N_CTX - 1)]
+    return lax.ppermute(first_row, CTX, down), lax.ppermute(second_row, CTX, up)
+
+
 def pack_keys(rows):
-    lead = rows[:, :LAT].reshape(2, 64, 4, 128).transpose(0, 2, 1, 3).reshape(8, 64, 128)
-    rope = jnp.concatenate([rows[:64, LAT:KEYW], rows[64:, LAT:KEYW]], axis=1)
+    lead = rows[..., :LAT].reshape(2, 128, 4, 128).transpose(0, 2, 1, 3).reshape(8, 128, 128)
+    rope = jnp.concatenate([rows[0, :, LAT:KEYW], rows[1, :, LAT:KEYW]], axis=1)
     return jnp.concatenate([lead, rope[None]], axis=0)
 
 
@@ -104,25 +111,6 @@
         ),
         name="merge",
     )(arrived)
-
-
-def add_kernel(a_ref, b_ref, out_ref):
-    out_ref[...] = (a_ref[...].astype(f32) + b_ref[...].astype(f32)).astype(bf16)
-
-
-def add_cores(mine, received):
-    block = pl.BlockSpec((2, 9, 64, 128), lambda i: (i, 0, 0, 0))
-    return pl.pallas_call(
-        add_kernel,
-        grid=(N_XY // 2,),
-        in_specs=[block, block],
-        out_specs=block,
-        out_shape=jax.ShapeDtypeStruct(mine.shape, bf16),
-        cost_estimate=pl.CostEstimate(
-            flops=1_200_000, bytes_accessed=7_100_000, transcendentals=0
-        ),
-        name="add_cores",
-    )(mine, received)
 
 
 def attention_kernel(
@@ -200,17 +188,22 @@
         return late.astype(jnp.int32), half, block
 
     def slab(half, block):
-        x4 = (block // 2 * 2 + half) * 4
-        zh = block % 2
+        xh = block // 2
+        at = pl.multiple_of((block % 2) * 64, 64)
 
         def tile(part):
             return jnp.concatenate(
-                [keys[co, x4 + y, part] for co in range(2) for y in range(4)], axis=0
+                [
+                    keys[co, half * 4 + y, part, pl.ds(at, 64), :]
+                    for co in range(2)
+                    for y in range(4)
+                ],
+                axis=0,
             )
 
         rope = tile(8)
-        rope = jnp.where(zh == 0, rope[:, :ROPE], rope[:, ROPE:])
-        return jnp.concatenate([tile(zh * 4 + c) for c in range(4)] + [rope], axis=1)
+        rope = jnp.where(xh == 0, rope[:, :ROPE], rope[:, ROPE:])
+        return jnp.concatenate([tile(xh * 4 + c) for c in range(4)] + [rope], axis=1)
 
     def nn(a, b):
         return jnp.dot(a, b, preferred_element_type=f32)
@@ -304,7 +297,8 @@
 
 def attention(where, mine, other, q, qt, g, gt):
     hbm = pl.BlockSpec(memory_space=pl.ANY)
-    half_keys = (N_XY, 9, 64, 128)
+    half_keys = (N_TP, 9, 128, 128)
+    half_grads = (N_XY, 9, 64, 128)
     return pl.pallas_call(
         attention_kernel,
         in_specs=[pl.BlockSpec(memory_space=pltpu.SMEM)] + [hbm] * 6,
@@ -313,8 +307,8 @@
             jax.ShapeDtypeStruct((2, LAT, SEG), bf16),
             jax.ShapeDtypeStruct((2, LAT, SEG), bf16),
             jax.ShapeDtypeStruct((2, ROPE, SEG), f32),
-            jax.ShapeDtypeStruct(half_keys, bf16),
-            jax.ShapeDtypeStruct(half_keys, bf16),
+            jax.ShapeDtypeStruct(half_grads, bf16),
+            jax.ShapeDtypeStruct(half_grads, bf16),
         ],
         scratch_shapes=[
             pltpu.VMEM((2,) + half_keys, bf16),
@@ -331,8 +325,8 @@
             pltpu.VMEM((2, KEYW, SEG), f32),
             pltpu.VMEM((2, LAT, SEG), bf16),
             pltpu.VMEM((2, LAT, SEG), bf16),
-            pltpu.VMEM((2,) + half_keys, f32),
-            pltpu.VMEM((2,) + half_keys, bf16),
+            pltpu.VMEM((2,) + half_grads, f32),
+            pltpu.VMEM((2,) + half_grads, bf16),
             pltpu.SemaphoreType.DMA((6,)),
             pltpu.SemaphoreType.DMA((21,)),
         ],
@@ -360,22 +354,28 @@
     ctx = lax.axis_index(CTX)
     core = lax.axis_index("co")
     tp = lax.axis_index(TP)
-
+    last = ctx == N_CTX - 1
+
+    after, before = edge_exchange(embed[0:1], embed[HALF : HALF + 1])
+    after_early = jnp.where(last, embed[HALF : HALF + 1], after)
+    next_embed = jnp.concatenate(
+        [embed[1:HALF], after_early, embed[HALF + 1 :], before], axis=0
+    )
     hidden_wide = hidden.astype(f32)
-    embed_wide = embed.astype(f32)
+    next_wide = next_embed.astype(f32)
     part_hidden = jnp.dot(
         (hidden_wide * gain_hidden).astype(bf16), proj_hidden, preferred_element_type=f32
     )
-    part_embed = jnp.dot(
-        (embed_wide * gain_embed).astype(bf16), proj_embed, preferred_element_type=f32
+    part_next = jnp.dot(
+        (next_wide * gain_embed).astype(bf16), proj_embed, preferred_element_type=f32
     )
     spread = (ROWS, WIDE - KEYW)
     parts = jnp.concatenate(
         [
             part_hidden,
             jnp.broadcast_to(jnp.sum(hidden_wide * hidden_wide, axis=1, keepdims=True), spread),
-            part_embed,
-            jnp.broadcast_to(jnp.sum(embed_wide * embed_wide, axis=1, keepdims=True), spread),
+            part_next,
+            jnp.broadcast_to(jnp.sum(next_wide * next_wide, axis=1, keepdims=True), spread),
         ],
         axis=1,
     ).reshape(N_TP, PIECE, 2 * WIDE)
@@ -383,12 +383,9 @@
 
     parts, queries, grad_out = lax.optimization_barrier((parts, queries, grad_out))
     parts = jnp.sum(parts, axis=0)
-    nexts = parts[:, WIDE:]
-    after = lax.ppermute(nexts[:1], ALL, [(b, a) for a, b in zip(ORDER[:-1], ORDER[1:])])
-    nexts = jnp.concatenate([nexts[1:], after], axis=0)
-    part_hidden, part_next = parts[:, :KEYW], nexts[:, :KEYW]
+    part_hidden, part_next = parts[:, :KEYW], parts[:, WIDE : WIDE + KEYW]
     inv_hidden = lax.rsqrt(parts[:, KEYW : KEYW + 1] / D + EPSILON)
-    inv_next = lax.rsqrt(nexts[:, KEYW : KEYW + 1] / D + EPSILON)
+    inv_next = lax.rsqrt(parts[:, WIDE + KEYW : WIDE + KEYW + 1] / D + EPSILON)
     latent = inv_hidden * part_hidden + inv_next * part_next
     leading = latent[:, :LAT]
     inv_latent = lax.rsqrt(jnp.mean(leading * leading, axis=1, keepdims=True) + EPSILON)
@@ -401,8 +398,8 @@
         ],
         axis=1,
     )
-    same = pack_keys(gather_copies(key_piece, "z", N_Z).reshape(128, WIDE))
-    mine = gather_copies(same, XY, N_XY)
+    same = pack_keys(gather_copies(key_piece, XZ, 16).reshape(2, 128, WIDE))
+    mine = gather_copies(same, TP, N_TP)
 
     cos_table, sin_table = rotation(row_positions(ctx, jnp.arange(ROWS)))
     cos_table = cos_table.reshape(2, 1, HALF, ROPE // 2)
@@ -433,7 +430,7 @@
     )
 
     received = lax.ppermute(dother, "co", [(0, 1), (1, 0)])
-    dkey = add_cores(dmine, received)
+    dkey = (dmine.astype(f32) + received.astype(f32)).astype(bf16)
     dkey = lax.all_to_all(dkey, XY, split_axis=0, concat_axis=0, tiled=True)
 
     attended = jnp.einsum(
@@ -472,10 +469,10 @@
     coef_next = jnp.sum(dlatent * part_next, axis=1, keepdims=True) * inv_next**3 / D
 
     def in_two(c):
-        high = c.astype(bf16)
-        low = (c - high.astype(f32)).astype(bf16)
+        high = lax.reduce_precision(c, 8, 7)
+        low = c - high
         width = (PIECE, (WIDE - KEYW) // 2)
-        return [jnp.broadcast_to(high, width), jnp.broadcast_to(low, width)]
+        return [jnp.broadcast_to(h.astype(bf16), width) for h in (high, low)]
 
     packed_hidden = jnp.concatenate(
         [(inv_hidden * dlatent).astype(bf16)] + in_two(coef_hidden), axis=1
@@ -504,7 +501,7 @@
     grad_embed = (
         gain_embed
         * jnp.einsum("rc,dc->rd", dpart_next, proj_embed, preferred_element_type=f32)
-        - coef_next * embed_wide
+        - coef_next * embed.astype(f32)
     ).astype(bf16)
     return (attended, grad_queries, grad_hidden, grad_embed)
 

time: 212 us -> 207 us (0.976)
  Pallas kernels: 36.1 us -> 29.8 us
  starting transfers between devices: 31.7 us -> 28.6 us
  waiting for transfers between devices: 55.8 us -> 58.1 us
    pallas_call x1 -> x0, Pallas kernels: 6.38 us -> none  [add_cores(): pl.pallas_call(add_kernel, grid=(N_XY // 2,), in_specs=[block, block], ou...]
    ppermute x1 -> x2, waiting for transfers between devices: 1.08 us -> 5.65 us  [the longest x1 5.64 us: edge_exchange(): lax.ppermute(second_row, CTX, up)]
    all_to_all x1, starting transfers between devices: 8.53 us -> 4.5 us  [gather_copies(): return lax.all_to_all(copies, axes, split_axis=0, concat_axis=0, tiled=True)]
    convert_element_type x2, other arithmetic: 1.01 us -> 4.39 us  [the longest x1 4.16 us: on_device(): dkey = (dmine.astype(f32) + received.astype(f32)).astype(bf16)]
    all_to_all x1, blocking collectives: 11.9 us -> 14.7 us  [on_device(): lax.all_to_all(merge(dkey), 'z', split_axis=0, concat_axis=0, tiled=True)]
    unnamed x64 -> x34, local copies, waits for them, and re-layouts: 5.63 us -> 3.56 us
    ppermute x1 -> x2, starting transfers between devices: 7.41 us -> 9.05 us  [the longest x1 7.14 us: edge_exchange(): lax.ppermute(first_row, CTX, down)]
  transfers between devices with their start and end apart: 7 -> 8, of which waited for: 7 -> 7; matrix products, arithmetic and copies ran while one was open for 14% -> 17% of each run, Pallas kernels for 0% -> 0%
where the time goes in v5:
time: 207 us; the launch traced here: 205 us
  waiting for transfers between devices  58.1 us (28%)
  blocking collectives  38.2 us (18%)
  Pallas kernels  29.8 us (14%)
  starting transfers between devices  28.6 us (14%)
  local copies, waits for them, and re-layouts  27.6 us (13%)
  other arithmetic  12.7 us (6%)
  matrix products  9.25 us (4%)
    pallas_call x1, Pallas kernels, attention(): pl.pallas_call(attention_kernel, in_specs=[pl.BlockSpec(memory_space=pltp...  29.4 us
    all_to_all x2, blocking collectives, gather_copies(): return lax.all_to_all(copies, axes, split_axis=0, concat_axis=0, tiled=True)  23.5 us
    all_to_all x1, blocking collectives, on_device(): lax.all_to_all(merge(dkey), 'z', split_axis=0, concat_axis=0, tiled=True)  14.7 us
    all_to_all x1, waiting for transfers between devices, on_device(): dkey = lax.all_to_all(dkey, XY, split_axis=0, concat_axis=0, tiled=True)  13.9 us
    all_to_all x1, waiting for transfers between devices, gather_copies(): return lax.all_to_all(copies, axes, split_axis=0, concat_axis=0, tiled=True)  12.9 us
    all_to_all x1, waiting for transfers between devices, on_device(): parts = lax.all_to_all(parts, TP, split_axis=0, concat_axis=0, tiled=True)  8.71 us
    ppermute x1, waiting for transfers between devices, on_device(): lax.ppermute(packed_next[-1:], ALL, list(zip(ORDER[:-1], ORDER[1:])))  8.12 us
    ppermute x1, starting transfers between devices, edge_exchange(): lax.ppermute(first_row, CTX, down)  7.14 us
  transfers between devices with their start and end apart: 8, of which 7 were waited for; matrix products, arithmetic and copies ran while one was open for 17% of the time, Pallas kernels for 0%

profile of v5, /device:TPU:4, one launch (start us, length us, event | category | flops | bytes accessed | tf_op | source)
XLA Modules:
  0.0 205.4 jit_solution(14244655921298321898)
XLA Ops:
  0.7 0.8 slice.103
  1.5 7.1 %collective-permute-start = (bf16[1,896]{1,0:T(2,128)(2,1)S(1)}, bf16[1,896]{1,0:T(2,128)(2,1)S(1)}, u32[]{:S(2)}, u32[]{:S(2)}) collective-permute-start(bf16[1,896]{1,0:T(2,128)(2,1)S(1)} %slice.103), channel_id=1, source_target_pairs={{8,0},{16,8},{24,16},{32,24},{40,32},{48,40},{56,48},{64,56},{72,6... | collective-permute-start | bytes 5384 | tf_op jit(solution)/shard_map/ppermute | solution.py:81
  8.6 1.8 fusion.20
  10.4 1.0 fusion.63
  11.5 0.7 broadcast_select_fusion
  12.2 1.9 collective-permute-start.1
  14.1 1.1 fusion.17
  15.2 5.6 %collective-permute-done.1 = bf16[1,896]{1,0:T(2,128)(2,1)S(1)} collective-permute-done((bf16[1,896]{1,0:T(2,128)(2,1)S(1)}, bf16[1,896]{1,0:T(2,128)(2,1)S(1)}, u32[]{:S(2)}, u32[]{:S(2)}) %collective-permute-start.1) | collective-permute-done | bytes 1824 | tf_op jit(solution)/shard_map/ppermute | solution.py:81
  20.8 0.1 fusion.15
  21.0 0.4 fusion.22
  21.5 1.1 copy.88
  22.6 6.0 %all-to-all-start = ((f32[8,16,1280]{2,1,0:T(8,128)}), f32[8,16,1280]{2,1,0:T(8,128)S(1)}, u32[]{:S(2)}, u32[]{:S(2)}) async-start(f32[8,16,1280]{2,1,0:T(8,128)} %bitcast.2), calls=%async_computation | async-start | bytes 1310720 | tf_op jit(solution)/shard_map/all_to_all | solution.py:382
  28.7 8.7 %all-to-all-done = f32[8,16,1280]{2,1,0:T(8,128)S(1)} async-done(((f32[8,16,1280]{2,1,0:T(8,128)}), f32[8,16,1280]{2,1,0:T(8,128)S(1)}, u32[]{:S(2)}, u32[]{:S(2)}) %all-to-all-start) | async-done | bytes 655392 | tf_op jit(solution)/shard_map/all_to_all | solution.py:382
  37.4 0.2 fusion.53
  37.8 0.1 fusion.38
  38.2 13.4 %all_to_all.30 = bf16[16,16,640]{2,1,0:T(8,128)(2,1)S(1)} all-to-all(bf16[16,16,640]{2,1,0:T(8,128)(2,1)S(1)} %broadcast_in_dim.37), channel_id=1, replica_groups=mesh['xh'=2,'z'=8,'co'=2,'xl'=2,'y'=4] {'xh','z'}, dimensions={0} | all-to-all | bytes 655360 | tf_op jit(solution)/shard_map/all_to_all | solution.py:75
  51.8 2.0 broadcast_in_dim.39
  53.7 4.5 %all-to-all-start.2 = ((bf16[8,9,128,128]{3,2,1,0:T(8,128)(2,1)}), bf16[8,9,128,128]{3,2,1,0:T(8,128)(2,1)}, u32[]{:S(2)}, u32[]{:S(2)}) async-start(bf16[8,9,128,128]{3,2,1,0:T(8,128)(2,1)} %broadcast_in_dim.39), calls=%async_computation.2 | async-start | bytes 4718592 | tf_op jit(solution)/shard_map/all_to_all | solution.py:75
  58.3 0.3 copy.120
  58.6 0.9 copy-done.9
  59.5 0.3 copy.122
  59.8 1.0 multiply_cosine_fusion
  60.8 0.8 copy.121
  61.5 2.3 %reshape.138 = bf16[2,64,8,192]{3,2,1,0:T(8,128)(2,1)} reshape(bf16[128,1536]{1,0:T(8,128)(2,1)} %param.20) | data formatting | bytes 786432 | tf_op jit(solution)/shard_map/reshape | solution.py:409
  63.8 1.1 copy.140
  65.0 1.1 subtract_convert_fusion.1
  66.1 0.5 fusion
  66.6 0.2 pad_maximum_fusion
  66.8 0.1 copy.91
  67.0 0.5 copy-done.7
  67.5 0.5 fusion.1
  68.1 1.3 copy.96
  69.4 1.4 copy.92
  70.8 12.9 %all-to-all-done.2.mine_ref = bf16[8,9,128,128]{3,2,1,0:T(8,128)(2,1)} async-done(((bf16[8,9,128,128]{3,2,1,0:T(8,128)(2,1)}), bf16[8,9,128,128]{3,2,1,0:T(8,128)(2,1)}, u32[]{:S(2)}, u32[]{:S(2)}) %all-to-all-start.2) | async-done | bytes 2359328 | tf_op jit(solution)/shard_map/all_to_all | solution.py:75
  83.7 0.7 pad_add_fusion.where_ref
  84.4 4.2 %collective-permute-done.2.other_ref = bf16[8,9,128,128]{3,2,1,0:T(8,128)(2,1)} collective-permute-done((bf16[8,9,128,128]{3,2,1,0:T(8,128)(2,1)}, bf16[8,9,128,128]{3,2,1,0:T(8,128)(2,1)}, u32[]{:S(2)}, u32[]{:S(2)}) %collective-permute-start.2) | collective-permute-done | bytes 2359328 | tf_op jit(solution)/shard_map/ppermute | solution.py:425
  88.6 29.4 %attention.1 = (bf16[2,512,512]{2,1,0:T(8,128)(2,1)}, bf16[2,512,512]{2,1,0:T(8,128)(2,1)}, f32[2,64,512]{2,1,0:T(8,128)}, bf16[16,9,64,128]{3,2,1,0:T(8,128)(2,1)}, bf16[16,9,64,128]{3,2,1,0:T(8,128)(2,1)}) custom-call(s32[2]{0:T(128)} %pad_add_fusion.where_ref, bf16[8,9,128,128]{3,2,1,0:T(8,128)(2,1)} %all-to-all-done.2.mine_ref, ...), custom_call_target="tpu_custom_call" | custom-call | flops 14000000000 | bytes 20000000 | tf_op jit(solution)/shard_map/attention/pallas_call | solution.py:302
  118.0 0.2 collective-permute-start.3
  118.2 4.6 %collective-permute-done.3 = bf16[16,9,64,128]{3,2,1,0:T(8,128)(2,1)S(1)} collective-permute-done((bf16[16,9,64,128]{3,2,1,0:T(8,128)(2,1)}, bf16[16,9,64,128]{3,2,1,0:T(8,128)(2,1)S(1)}, u32[]{:S(2)}, u32[]{:S(2)}) %collective-permute-start.3) | collective-permute-done | bytes 2359328 | tf_op jit(solution)/shard_map/ppermute | solution.py:432
  122.8 4.2 %add_convert_fusion = bf16[16,9,64,128]{3,2,1,0:T(8,128)(2,1)} fusion(bf16[16,9,64,128]{3,2,1,0:T(8,128)(2,1)S(1)} %collective-permute-done.3, bf16[16,9,64,128]{3,2,1,0:T(8,128)(2,1)} %get-tuple-element.28), kind=kLoop, calls=%fused_computation | loop fusion | flops 4718592 | bytes 7077888 | tf_op jit(solution)/shard_map/convert_element_type | solution.py:433
  127.0 6.3 %all-to-all-start.3 = ((bf16[16,9,64,128]{3,2,1,0:T(8,128)(2,1)}), bf16[16,9,64,128]{3,2,1,0:T(8,128)(2,1)S(1)}, u32[]{:S(2)}, u32[]{:S(2)}) async-start(bf16[16,9,64,128]{3,2,1,0:T(8,128)(2,1)} %add_convert_fusion), calls=%async_computation.3 | async-start | bytes 4718592 | tf_op jit(solution)/shard_map/all_to_all | solution.py:434
  133.3 1.9 reshape.147
  135.2 2.0 copy.104
  137.2 2.3 %copy.97 = bf16[2,512,512]{1,2,0:T(8,128)(2,1)} copy(bf16[2,512,512]{2,1,0:T(8,128)(2,1)} %get-tuple-element.30) | data formatting | bytes 2097152 | tf_op jit(solution)/shard_map/attention/pallas_call | solution.py:302
  139.5 2.0 fusion.6
  141.5 0.2 copy.100
  141.7 0.8 copy.141
  142.5 2.3 %copy.101 = bf16[2,512,512]{1,2,0:T(8,128)(2,1)} copy(bf16[2,512,512]{2,1,0:T(8,128)(2,1)} %get-tuple-element.31) | data formatting | bytes 2097152 | tf_op jit(solution)/shard_map/attention/pallas_call | solution.py:302
  144.8 1.4 add_convert_fusion.1
  146.2 2.0 fusion.7
  148.2 0.2 maximum_bitcast_fusion
  148.4 1.1 copy.105
  149.5 2.3 %reshape.148 = bf16[128,1536]{1,0:T(8,128)(2,1)} reshape(bf16[2,64,8,192]{3,2,1,0:T(8,128)(2,1)} %copy.105) | data formatting | bytes 786432 | tf_op jit(solution)/shard_map/reshape | solution.py:453
  151.8 13.9 %all-to-all-done.3.in_ref = bf16[16,9,64,128]{3,2,1,0:T(8,128)(2,1)S(1)} async-done(((bf16[16,9,64,128]{3,2,1,0:T(8,128)(2,1)}), bf16[16,9,64,128]{3,2,1,0:T(8,128)(2,1)S(1)}, u32[]{:S(2)}, u32[]{:S(2)}) %all-to-all-start.3) | async-done | bytes 2359328 | tf_op jit(solution)/shard_map/all_to_all | solution.py:434
  165.6 0.4 merge.1
  166.1 14.7 %all_to_all.31 = bf16[8,16,640]{2,1,0:T(8,128)(2,1)S(1)} all-to-all(bf16[8,16,640]{2,1,0:T(8,128)(2,1)S(1)} %merge.1), channel_id=1, replica_groups=mesh['xh'=2,'z'=8,'co'=2,'xl'=2,'y'=4] {'z'}, dimensions={0} | all-to-all | bytes 327680 | tf_op jit(solution)/shard_map/all_to_all | solution.py:456
  181.2 0.2 multiply_reduce_fusion
  181.5 0.2 fusion.58
  182.0 2.5 %collective-permute-start.4 = (bf16[1,640]{1,0:T(2,128)(2,1)S(1)}, bf16[1,640]{1,0:T(2,128)(2,1)S(1)}, u32[]{:S(2)}, u32[]{:S(2)}) collective-permute-start(bf16[1,640]{1,0:T(2,128)(2,1)S(1)} %pad_maximum_fusion.9), channel_id=1, source_target_pairs={{0,1},{1,2},{2,3},{3,8},{8,9},{9,10},{10,11},{11,16},{16,17},{17,1... | collective-permute-start | bytes 3848 | tf_op jit(solution)/shard_map/ppermute | solution.py:483
  184.5 8.1 %collective-permute-done.4 = bf16[1,640]{1,0:T(2,128)(2,1)S(1)} collective-permute-done((bf16[1,640]{1,0:T(2,128)(2,1)S(1)}, bf16[1,640]{1,0:T(2,128)(2,1)S(1)}, u32[]{:S(2)}, u32[]{:S(2)}) %collective-permute-start.4) | collective-permute-done | bytes 1312 | tf_op jit(solution)/shard_map/ppermute | solution.py:483
  193.0 10.1 %all_to_all.32 = bf16[8,16,1280]{2,1,0:T(8,128)(2,1)S(1)} all-to-all(bf16[8,16,1280]{2,1,0:T(8,128)(2,1)S(1)} %broadcast_in_dim.98), channel_id=1, replica_groups=mesh['xh'=2,'z'=8,'co'=2,'xl'=2,'y'=4] {'xl','y'}, dimensions={0} | all-to-all | bytes 655360 | tf_op jit(solution)/shard_map/all_to_all | solution.py:75
  203.1 0.2 add_reduce_fusion
  203.3 1.1 fusion.4
  204.4 1.1 fusion.5
  (66 shorter events, 2.0 us)
Async XLA Ops:
  0.6 20.3 %copy-start = (bf16[896,576]{0,1:T(8,128)(2,1)S(1)}, bf16[896,576]{0,1:T(8,128)(2,1)}, u32[]{:S(2)}) copy-start(bf16[896,576]{0,1:T(8,128)(2,1)} %param.16) | copy-start | bytes 3096580
  0.6 20.3 %copy-start.14 = (f32[896]{0:T(1024)S(1)}, f32[896]{0:T(1024)}, u32[]{:S(2)}) copy-start(f32[896]{0:T(1024)} %param.14) | copy-start | bytes 10756
  1.5 10.0 %collective-permute-start = (bf16[1,896]{1,0:T(2,128)(2,1)S(1)}, bf16[1,896]{1,0:T(2,128)(2,1)S(1)}, u32[]{:S(2)}, u32[]{:S(2)}) collective-permute-start(bf16[1,896]{1,0:T(2,128)(2,1)S(1)} %slice.103), channel_id=1, source_target_pairs={{8,0},{16,8},{24,16},{32,24},{40,32},{48,40},{56,48},{64,56},{72,6... | collective-permute-start | bytes 5384 | tf_op jit(solution)/shard_map/ppermute | solution.py:81
  12.2 8.6 %collective-permute-start.1 = (bf16[1,896]{1,0:T(2,128)(2,1)S(1)}, bf16[1,896]{1,0:T(2,128)(2,1)S(1)}, u32[]{:S(2)}, u32[]{:S(2)}) collective-permute-start(bf16[1,896]{1,0:T(2,128)(2,1)S(1)} %get-tuple-element.61), channel_id=1, source_target_pairs={{0,8},{8,16},{16,24},{24,32},{32,40},{40,48},{48,56},{56,64},{64,7... | collective-permute-start | bytes 5384 | tf_op jit(solution)/shard_map/ppermute | solution.py:81
  21.4 16.5 %copy-start.12 = (f32[512]{0:T(512)S(1)}, f32[512]{0:T(512)}, u32[]{:S(2)}) copy-start(f32[512]{0:T(512)} %param.17) | copy-start | bytes 6148
  22.6 14.8 %all-to-all-start = ((f32[8,16,1280]{2,1,0:T(8,128)}), f32[8,16,1280]{2,1,0:T(8,128)S(1)}, u32[]{:S(2)}, u32[]{:S(2)}) async-start(f32[8,16,1280]{2,1,0:T(8,128)} %bitcast.2), calls=%async_computation | async-start | bytes 1310720 | tf_op jit(solution)/shard_map/all_to_all | solution.py:382
  53.7 4.5 %copy-start.8 = (bf16[512,1024]{1,0:T(8,128)(2,1)S(1)}, bf16[512,1024]{1,0:T(8,128)(2,1)}, u32[]{:S(2)}) copy-start(bf16[512,1024]{1,0:T(8,128)(2,1)} %param.18) | copy-start | bytes 3145732
  53.7 30.0 %all-to-all-start.2 = ((bf16[8,9,128,128]{3,2,1,0:T(8,128)(2,1)}), bf16[8,9,128,128]{3,2,1,0:T(8,128)(2,1)}, u32[]{:S(2)}, u32[]{:S(2)}) async-start(bf16[8,9,128,128]{3,2,1,0:T(8,128)(2,1)} %broadcast_in_dim.39), calls=%async_computation.2 | async-start | bytes 4718592 | tf_op jit(solution)/shard_map/all_to_all | solution.py:75
  58.3 1.2 copy-start.9
  58.3 2.5 %copy-start.11 = (bf16[128,1024]{1,0:T(8,128)(2,1)S(1)}, bf16[128,1024]{1,0:T(8,128)(2,1)}, u32[]{:S(2)}) copy-start(bf16[128,1024]{1,0:T(8,128)(2,1)} %param.21) | copy-start | bytes 786436
  58.6 7.5 %copy-start.2 = (bf16[64,8,8,128]{3,2,1,0:T(8,128)(2,1)}, bf16[64,8,8,128]{3,2,1,0:T(8,128)(2,1)S(1)}, u32[]{:S(2)}) copy-start(bf16[64,8,8,128]{3,2,1,0:T(8,128)(2,1)S(1)} %copy.120) | copy-start | bytes 3145732
  59.8 7.2 %copy-start.3 = (bf16[64,8,8,128]{3,2,1,0:T(8,128)(2,1)}, bf16[64,8,8,128]{3,2,1,0:T(8,128)(2,1)S(1)}, u32[]{:S(2)}) copy-start(bf16[64,8,8,128]{3,2,1,0:T(8,128)(2,1)S(1)} %copy.122) | copy-start | bytes 3145732
  66.6 1.0 copy-start.7
  67.0 2.4 %copy-start.1 = (bf16[2,8,64,576]{3,2,1,0:T(8,128)(2,1)}, bf16[2,8,64,576]{3,2,1,0:T(8,128)(2,1)S(1)}, u32[]{:S(2)}) copy-start(bf16[2,8,64,576]{3,2,1,0:T(8,128)(2,1)S(1)} %copy.91) | copy-start | bytes 3538948
  68.1 20.6 %copy-start.4 = (bf16[2,8,64,512]{3,2,1,0:T(8,128)(2,1)}, bf16[2,8,64,512]{3,2,1,0:T(8,128)(2,1)S(1)}, u32[]{:S(2)}) copy-start(bf16[2,8,64,512]{3,2,1,0:T(8,128)(2,1)S(1)} %copy.95) | copy-start | bytes 3145732
  83.7 4.9 %collective-permute-start.2 = (bf16[8,9,128,128]{3,2,1,0:T(8,128)(2,1)}, bf16[8,9,128,128]{3,2,1,0:T(8,128)(2,1)}, u32[]{:S(2)}, u32[]{:S(2)}) collective-permute-start(bf16[8,9,128,128]{3,2,1,0:T(8,128)(2,1)} %all-to-all-done.2.mine_ref), channel_id=1, source_target_pairs={{0,8},{8,0},{1,9},{9,1},{2,10},{10,2},{3,11},{11,3},{4,12},{12,4},... | collective-permute-start | bytes 7077896 | tf_op jit(solution)/shard_map/ppermute | solution.py:425
  118.0 4.8 %collective-permute-start.3 = (bf16[16,9,64,128]{3,2,1,0:T(8,128)(2,1)}, bf16[16,9,64,128]{3,2,1,0:T(8,128)(2,1)S(1)}, u32[]{:S(2)}, u32[]{:S(2)}) collective-permute-start(bf16[16,9,64,128]{3,2,1,0:T(8,128)(2,1)} %get-tuple-element.29), channel_id=1, source_target_pairs={{0,8},{8,0},{1,9},{9,1},{2,10},{10,2},{3,11},{11,3},{4,12},{12,4},... | collective-permute-start | bytes 7077896 | tf_op jit(solution)/shard_map/ppermute | solution.py:432
  127.0 38.7 %all-to-all-start.3 = ((bf16[16,9,64,128]{3,2,1,0:T(8,128)(2,1)}), bf16[16,9,64,128]{3,2,1,0:T(8,128)(2,1)S(1)}, u32[]{:S(2)}, u32[]{:S(2)}) async-start(bf16[16,9,64,128]{3,2,1,0:T(8,128)(2,1)} %add_convert_fusion), calls=%async_computation.3 | async-start | bytes 4718592 | tf_op jit(solution)/shard_map/all_to_all | solution.py:434
  166.1 37.2 %copy-start.10 = (bf16[128,896]{1,0:T(8,128)(2,1)S(1)}, bf16[128,896]{1,0:T(8,128)(2,1)}, u32[]{:S(2)}) copy-start(bf16[128,896]{1,0:T(8,128)(2,1)} %param.12) | copy-start | bytes 688132
  166.1 38.3 %copy-start.5 = (bf16[896,576]{0,1:T(8,128)(2,1)S(1)}, bf16[896,576]{0,1:T(8,128)(2,1)}, u32[]{:S(2)}) copy-start(bf16[896,576]{0,1:T(8,128)(2,1)} %param.15) | copy-start | bytes 3096580
  166.1 38.3 %copy-start.6 = (bf16[128,896]{1,0:T(8,128)(2,1)S(1)}, bf16[128,896]{1,0:T(8,128)(2,1)}, u32[]{:S(2)}) copy-start(bf16[128,896]{1,0:T(8,128)(2,1)} %param.11) | copy-start | bytes 688132
  166.1 38.3 %copy-start.13 = (f32[896]{0:T(1024)S(1)}, f32[896]{0:T(1024)}, u32[]{:S(2)}) copy-start(f32[896]{0:T(1024)} %param.13) | copy-start | bytes 10756
  182.0 10.6 %collective-permute-start.4 = (bf16[1,640]{1,0:T(2,128)(2,1)S(1)}, bf16[1,640]{1,0:T(2,128)(2,1)S(1)}, u32[]{:S(2)}, u32[]{:S(2)}) collective-permute-start(bf16[1,640]{1,0:T(2,128)(2,1)S(1)} %pad_maximum_fusion.9), channel_id=1, source_target_pairs={{0,1},{1,2},{2,3},{3,8},{8,9},{9,10},{10,11},{11,16},{16,17},{17,1... | collective-permute-start | bytes 3848 | tf_op jit(solution)/shard_map/ppermute | solution.py:483

commit v6 on v5

--- a/solution.py
+++ b/solution.py
@@ -79,6 +79,43 @@
     down = [(i + 1, i) for i in range(N_CTX - 1)]
     up = [(i, i + 1) for i in range(N_CTX - 1)]
     return lax.ppermute(first_row, CTX, down), lax.ppermute(second_row, CTX, up)
+
+
+def project_kernel(
+    where_ref, hidden_ref, embed_ref, after_ref, before_ref, gh_ref, ge_ref, ph_ref, pe_ref, out_ref
+):
+    def put(at, values, gain, weights):
+        squares = jnp.sum(values * values, axis=1, keepdims=True)
+        scaled = (values * gain).astype(bf16)
+        out_ref[:, at : at + KEYW] = lax.dot_general(
+            scaled, weights, (((1,), (1,)), ((), ())), preferred_element_type=f32
+        )
+        out_ref[:, at + KEYW : at + WIDE] = jnp.broadcast_to(squares, (ROWS, WIDE - KEYW))
+
+    put(0, hidden_ref[...].astype(f32), gh_ref[...], ph_ref[...])
+    own = embed_ref[...].astype(f32)
+    row = lax.broadcasted_iota(jnp.int32, (ROWS, 1), 0)
+    after = jnp.where(
+        where_ref[0] == N_CTX - 1, own[HALF : HALF + 1], after_ref[...].astype(f32)
+    )
+    following = jnp.where(row == HALF - 1, after, pltpu.roll(own, ROWS - 1, 0))
+    following = jnp.where(row == ROWS - 1, before_ref[...].astype(f32), following)
+    put(WIDE, following, ge_ref[...], pe_ref[...])
+
+
+def project(where, *operands):
+    vmem = pl.BlockSpec(memory_space=pltpu.VMEM)
+    return pl.pallas_call(
+        project_kernel,
+        in_specs=[pl.BlockSpec(memory_space=pltpu.SMEM)] + [vmem] * 8,
+        out_specs=vmem,
+        out_shape=jax.ShapeDtypeStruct((ROWS, 2 * WIDE), f32),
+        compiler_params=pltpu.CompilerParams(vmem_limit_bytes=60 * 1024 * 1024),
+        cost_estimate=pl.CostEstimate(
+            flops=270_000_000, bytes_accessed=3_200_000, transcendentals=0
+        ),
+        name="project",
+    )(where, *operands)
 
 
 def pack_keys(rows):
@@ -140,6 +177,7 @@
     dqt_buf,
     ot_out,
     lead_out,
+    tail_out,
     dk_buf,
     dk_out,
     sems,
@@ -151,10 +189,12 @@
         pltpu.make_async_copy(source, target, sems.at[n])
         for n, (source, target) in enumerate(
             [
-                (mine_ref, keys.at[core]),
+                (mine_ref.at[pl.ds(0, 4)], keys.at[core, pl.ds(0, 4)]),
+                (other_ref.at[pl.ds(0, 4)], keys.at[1 - core, pl.ds(0, 4)]),
                 (qt_hbm, qt_ref),
                 (gt_hbm, gt_ref),
-                (other_ref, keys.at[1 - core]),
+                (mine_ref.at[pl.ds(4, 4)], keys.at[core, pl.ds(4, 4)]),
+                (other_ref.at[pl.ds(4, 4)], keys.at[1 - core, pl.ds(4, 4)]),
                 (q_hbm, q_ref),
                 (g_hbm, g_ref),
             ]
@@ -209,6 +249,11 @@
         return jnp.dot(a, b, preferred_element_type=f32)
 
     def first(i, carry):
+        @pl.when(i == early_steps + 4)
+        def _():
+            for copy in copies[4:6]:
+                copy.wait()
+
         seg, half, block = locate(i)
         k = slab(half, block)
         idx = lax.broadcasted_iota(jnp.int32, (BLOCK, 1), 0)
@@ -237,12 +282,49 @@
         return carry
 
     lax.fori_loop(0, STEPS, first, 0)
-    for copy in copies[4:]:
+    for copy in copies[6:]:
         copy.wait()
     a_buf[...] = a_buf[...] / l_buf[...]
     m_buf[...] = m_buf[...] + jnp.log2(l_buf[...])
 
+    sends = []
+
+    def send(source, target):
+        sends.append(pltpu.make_async_copy(source, target, out_sems.at[len(sends)]))
+
+    for xl in range(2):
+        for core_first, target in ((0, dother_ref), (1, dmine_ref)):
+            for xh in range(2):
+                four = pl.ds((xh * 2 + xl) * 4, 4)
+                send(dk_out.at[core_first, four], target.at[four])
+    for seg in range(2):
+        send(ot_out.at[seg], ot_hbm.at[seg])
+        send(lead_out.at[seg], leadt_hbm.at[seg])
+        send(tail_out.at[seg], tailt_hbm.at[seg])
+
+    def put_keys(xl):
+        for slot, source in ((0, 1 - core), (1, core)):
+            for xh in range(2):
+                at = (xh * 2 + xl) * 4
+                dk_out[slot, at : at + 4] = dk_buf[source, at : at + 4].astype(bf16)
+                sends[xl * 4 + slot * 2 + xh].start()
+
+    def put_rows(seg):
+        ot_out[seg] = ot_buf[seg].astype(bf16)
+        lead_out[seg] = dqt_buf[seg, :LAT].astype(bf16)
+        tail_out[seg] = dqt_buf[seg, LAT:]
+        for copy in sends[8 + seg * 3 : 11 + seg * 3]:
+            copy.start()
+
     def second(i, carry):
+        @pl.when(i == early_steps)
+        def _():
+            put_rows(0)
+
+        @pl.when(i == early_steps + 4)
+        def _():
+            put_keys(0)
+
         seg, half, block = locate(i)
         k = slab(half, block)
         kt = k.T
@@ -272,25 +354,8 @@
 
     lax.fori_loop(0, STEPS, second, 0)
 
-    sends = []
-
-    def send(source, target):
-        copy = pltpu.make_async_copy(source, target, out_sems.at[len(sends)])
-        copy.start()
-        sends.append(copy)
-
-    send(dqt_buf.at[:, pl.ds(LAT, ROPE)], tailt_hbm)
-    for t in range(0, N_XY, 2):
-        dk_out[0, t : t + 2] = dk_buf[1 - core, t : t + 2].astype(bf16)
-        send(dk_out.at[0, pl.ds(t, 2)], dother_ref.at[pl.ds(t, 2)])
-    for t in range(0, N_XY, 2):
-        dk_out[1, t : t + 2] = dk_buf[core, t : t + 2].astype(bf16)
-        send(dk_out.at[1, pl.ds(t, 2)], dmine_ref.at[pl.ds(t, 2)])
-    for seg in range(2):
-        ot_out[seg] = ot_buf[seg].astype(bf16)
-        send(ot_out.at[seg], ot_hbm.at[seg])
-        lead_out[seg] = dqt_buf[seg, :LAT].astype(bf16)
-        send(lead_out.at[seg], leadt_hbm.at[seg])
+    put_keys(1)
+    put_rows(1)
     for copy in sends:
         copy.wait()
 
@@ -325,10 +390,11 @@
             pltpu.VMEM((2, KEYW, SEG), f32),
             pltpu.VMEM((2, LAT, SEG), bf16),
             pltpu.VMEM((2, LAT, SEG), bf16),
+            pltpu.VMEM((2, ROPE, SEG), f32),
             pltpu.VMEM((2,) + half_grads, f32),
             pltpu.VMEM((2,) + half_grads, bf16),
-            pltpu.SemaphoreType.DMA((6,)),
-            pltpu.SemaphoreType.DMA((21,)),
+            pltpu.SemaphoreType.DMA((8,)),
+            pltpu.SemaphoreType.DMA((14,)),
         ],
         compiler_params=pltpu.CompilerParams(vmem_limit_bytes=60 * 1024 * 1024),
         cost_estimate=pl.CostEstimate(
@@ -354,30 +420,19 @@
     ctx = lax.axis_index(CTX)
     core = lax.axis_index("co")
     tp = lax.axis_index(TP)
-    last = ctx == N_CTX - 1
 
     after, before = edge_exchange(embed[0:1], embed[HALF : HALF + 1])
-    after_early = jnp.where(last, embed[HALF : HALF + 1], after)
-    next_embed = jnp.concatenate(
-        [embed[1:HALF], after_early, embed[HALF + 1 :], before], axis=0
-    )
-    hidden_wide = hidden.astype(f32)
-    next_wide = next_embed.astype(f32)
-    part_hidden = jnp.dot(
-        (hidden_wide * gain_hidden).astype(bf16), proj_hidden, preferred_element_type=f32
-    )
-    part_next = jnp.dot(
-        (next_wide * gain_embed).astype(bf16), proj_embed, preferred_element_type=f32
-    )
-    spread = (ROWS, WIDE - KEYW)
-    parts = jnp.concatenate(
-        [
-            part_hidden,
-            jnp.broadcast_to(jnp.sum(hidden_wide * hidden_wide, axis=1, keepdims=True), spread),
-            part_next,
-            jnp.broadcast_to(jnp.sum(next_wide * next_wide, axis=1, keepdims=True), spread),
-        ],
-        axis=1,
+    where = jnp.stack([ctx, core]).astype(jnp.int32)
+    parts = project(
+        where,
+        hidden,
+        embed,
+        after,
+        before,
+        gain_hidden[None],
+        gain_embed[None],
+        proj_hidden.T,
+        proj_embed.T,
     ).reshape(N_TP, PIECE, 2 * WIDE)
     parts = lax.all_to_all(parts, TP, split_axis=0, concat_axis=0, tiled=True)
 
@@ -424,7 +479,6 @@
     mine, q, qt, g, gt = lax.optimization_barrier((mine, q, qt, g, gt))
     other = lax.ppermute(mine, "co", [(0, 1), (1, 0)])
 
-    where = jnp.stack([ctx, core]).astype(jnp.int32)
     ot, leadt, tailt, dmine, dother = attention(
         where, mine, other, q, qt, g, gt
     )
@@ -494,7 +548,7 @@
     grad_hidden = (
         gain_hidden
         * jnp.einsum("rc,dc->rd", dpart_hidden, proj_hidden, preferred_element_type=f32)
-        - coef_hidden * hidden_wide
+        - coef_hidden * hidden.astype(f32)
     ).astype(bf16)
 
     dpart_next, coef_next = whole(packed[:, WIDE:])

time: 207 us -> 205 us (level)
  local copies, waits for them, and re-layouts: 27.6 us -> 19.1 us
  waiting for transfers between devices: 58.1 us -> 65.3 us
  blocking collectives: 38.2 us -> 42.6 us
  other arithmetic: 12.7 us -> 8.57 us
  Pallas kernels: 29.8 us -> 32 us
  matrix products: 9.25 us -> 7.06 us
    all_to_all x1, waiting for transfers between devices: 13.9 us -> 20.3 us  [on_device(): dkey = lax.all_to_all(dkey, XY, split_axis=0, concat_axis=0, tiled=True)]
    all_to_all x1, waiting for transfers between devices: 12.9 us -> 18.7 us  [gather_copies(): return lax.all_to_all(copies, axes, split_axis=0, concat_axis=0, tiled=True)]
    ppermute x1, waiting for transfers between devices: 5.64 us -> 0.01 us  [edge_exchange(): lax.ppermute(second_row, CTX, up)]
    all_to_all x2, blocking collectives: 23.5 us -> 28.1 us  [gather_copies(): return lax.all_to_all(copies, axes, split_axis=0, concat_axis=0, tiled=True)]
    reshape x2, local copies, waits for them, and re-layouts: 3.94 us -> 0.36 us  [on_device(): tailt.reshape(2, ROPE, HEADS, HALF).transpose(0, 2, 3, 1)]
    pallas_call x0 -> x1, Pallas kernels: none -> 3.54 us  [project(): pl.pallas_call(project_kernel, in_specs=[pl.BlockSpec(memory_space=pltpu....]
    broadcast_in_dim x2, local copies, waits for them, and re-layouts: 0.01 us -> 2.53 us  [the longest x1 1.27 us: on_device(): gain_embed[None]]
    dot_general x2 -> x0, matrix products: 2.23 us -> none  [the longest x1 1.8 us: on_device(): jnp.dot((hidden_wide * gain_hidden).astype(bf16), proj_hidden, preferred_...]
  transfers between devices with their start and end apart: 8 -> 8, of which waited for: 7 -> 6; matrix products, arithmetic and copies ran while one was open for 17% -> 11% of each run, Pallas kernels for 0% -> 0%
where the time goes in v6:
time: 205 us
  waiting for transfers between devices  65.3 us (32%)
  blocking collectives  42.6 us (21%)
  Pallas kernels  32 us (16%)
  starting transfers between devices  28.9 us (14%)
  local copies, waits for them, and re-layouts  19.1 us (9%)
  other arithmetic  8.57 us (4%)
  matrix products  7.06 us (3%)
    all_to_all x2, blocking collectives, gather_copies(): return lax.all_to_all(copies, axes, split_axis=0, concat_axis=0, tiled=True)  28.1 us
    pallas_call x1, Pallas kernels, attention(): pl.pallas_call(attention_kernel, in_specs=[pl.BlockSpec(memory_space=pltp...  28 us
    all_to_all x1, waiting for transfers between devices, on_device(): dkey = lax.all_to_all(dkey, XY, split_axis=0, concat_axis=0, tiled=True)  20.3 us
    all_to_all x1, waiting for transfers between devices, gather_copies(): return lax.all_to_all(copies, axes, split_axis=0, concat_axis=0, tiled=True)  18.7 us
    all_to_all x1, blocking collectives, on_device(): lax.all_to_all(merge(dkey), 'z', split_axis=0, concat_axis=0, tiled=True)  14.4 us
    all_to_all x1, waiting for transfers between devices, on_device(): parts = lax.all_to_all(parts, TP, split_axis=0, concat_axis=0, tiled=True)  8.7 us
    ppermute x1, waiting for transfers between devices, on_device(): lax.ppermute(packed_next[-1:], ALL, list(zip(ORDER[:-1], ORDER[1:])))  8.15 us
    ppermute x1, starting transfers between devices, edge_exchange(): lax.ppermute(first_row, CTX, down)  7.26 us
  transfers between devices with their start and end apart: 8, of which 6 were waited for; matrix products, arithmetic and copies ran while one was open for 11% of the time, Pallas kernels for 0%

profile of v6, /device:TPU:4, one launch (start us, length us, event | category | flops | bytes accessed | tf_op | source)
XLA Modules:
  0.0 204.5 jit_solution(8185934360260857203)
XLA Ops:
  0.6 0.7 fusion.52
  1.4 1.9 collective-permute-start.1
  3.3 7.3 %collective-permute-start = (bf16[1,896]{1,0:T(2,128)(2,1)S(1)}, bf16[1,896]{1,0:T(2,128)(2,1)S(1)}, u32[]{:S(2)}, u32[]{:S(2)}) collective-permute-start(bf16[1,896]{1,0:T(2,128)(2,1)S(1)} %get-tuple-element.59), channel_id=1, source_target_pairs={{8,0},{16,8},{24,16},{32,24},{40,32},{48,40},{56,48},{64,56},{72,6... | collective-permute-start | bytes 5384 | tf_op jit(solution)/shard_map/ppermute | solution.py:81
  10.6 0.6 pad_add_fusion.where_ref
  11.1 1.3 broadcast_in_dim.34.gh_ref
  12.4 1.3 broadcast_in_dim.35.ge_ref
  13.7 0.6 copy-done.21
  14.2 3.5 %project.1 = f32[128,1280]{1,0:T(8,128)} custom-call(s32[2]{0:T(128)} %pad_add_fusion.where_ref, bf16[128,896]{1,0:T(8,128)(2,1)} %hidden_ref.1, bf16[128,896]{1,0:T(8,128)(2,1)} %embed_ref.1, bf16[1,896]{1,0:T(2,128)(2,1)} %copy-done.22, bf16[1,896]{1,0:T(2,128)(2,1)} %copy-done.21, f32[1,896]{1,0:T(1,128)} %broadcast_in_dim.34.gh_ref, ...), custom_call_target="tpu_custom_call" | custom-call | flops 270000000 | bytes 3200000 | tf_op jit(solution)/shard_map/project/pallas_call | solution.py:108
  17.8 5.9 %all-to-all-start = ((f32[8,16,1280]{2,1,0:T(8,128)}), f32[8,16,1280]{2,1,0:T(8,128)S(1)}, u32[]{:S(2)}, u32[]{:S(2)}) async-start(f32[8,16,1280]{2,1,0:T(8,128)} %bitcast.69), calls=%async_computation | async-start | bytes 1310720 | tf_op jit(solution)/shard_map/all_to_all | solution.py:437
  23.8 8.7 %all-to-all-done = f32[8,16,1280]{2,1,0:T(8,128)S(1)} async-done(((f32[8,16,1280]{2,1,0:T(8,128)}), f32[8,16,1280]{2,1,0:T(8,128)S(1)}, u32[]{:S(2)}, u32[]{:S(2)}) %all-to-all-start) | async-done | bytes 655392 | tf_op jit(solution)/shard_map/all_to_all | solution.py:437
  32.5 0.2 fusion.43
  32.8 0.1 multiply_reduce_fusion.3
  32.9 0.6 multiply_multiply_fusion.2
  33.5 0.1 fusion.28
  33.8 18.0 %all_to_all.30 = bf16[16,16,640]{2,1,0:T(8,128)(2,1)S(1)} all-to-all(bf16[16,16,640]{2,1,0:T(8,128)(2,1)S(1)} %broadcast_in_dim.37), channel_id=1, replica_groups=mesh['xh'=2,'z'=8,'co'=2,'xl'=2,'y'=4] {'xh','z'}, dimensions={0} | all-to-all | bytes 655360 | tf_op jit(solution)/shard_map/all_to_all | solution.py:75
  51.9 0.1 maximum_bitcast_fusion.1
  52.1 2.0 broadcast_in_dim.39
  54.1 4.5 %all-to-all-start.2 = ((bf16[8,9,128,128]{3,2,1,0:T(8,128)(2,1)}), bf16[8,9,128,128]{3,2,1,0:T(8,128)(2,1)}, u32[]{:S(2)}, u32[]{:S(2)}) async-start(bf16[8,9,128,128]{3,2,1,0:T(8,128)(2,1)} %broadcast_in_dim.39), calls=%async_computation.2 | async-start | bytes 4718592 | tf_op jit(solution)/shard_map/all_to_all | solution.py:75
  58.6 0.3 copy.116
  58.9 0.3 copy.118
  59.2 0.3 multiply_cosine_fusion
  59.6 1.5 reshape.136
  61.1 0.1 copy.136
  61.3 0.3 subtract_convert_fusion.1
  61.6 0.5 fusion
  62.0 0.2 pad_maximum_fusion
  62.3 0.1 copy.87
  62.4 0.5 fusion.1
  63.0 1.3 copy.92
  64.3 1.4 copy.88
  65.8 18.7 %all-to-all-done.2.mine_ref = bf16[8,9,128,128]{3,2,1,0:T(8,128)(2,1)} async-done(((bf16[8,9,128,128]{3,2,1,0:T(8,128)(2,1)}), bf16[8,9,128,128]{3,2,1,0:T(8,128)(2,1)}, u32[]{:S(2)}, u32[]{:S(2)}) %all-to-all-start.2) | async-done | bytes 2359328 | tf_op jit(solution)/shard_map/all_to_all | solution.py:75
  84.4 4.9 %collective-permute-done.2.other_ref = bf16[8,9,128,128]{3,2,1,0:T(8,128)(2,1)} collective-permute-done((bf16[8,9,128,128]{3,2,1,0:T(8,128)(2,1)}, bf16[8,9,128,128]{3,2,1,0:T(8,128)(2,1)}, u32[]{:S(2)}, u32[]{:S(2)}) %collective-permute-start.2) | collective-permute-done | bytes 2359328 | tf_op jit(solution)/shard_map/ppermute | solution.py:480
  89.3 28.0 %attention.1 = (bf16[2,512,512]{2,1,0:T(8,128)(2,1)}, bf16[2,512,512]{2,1,0:T(8,128)(2,1)}, f32[2,64,512]{2,1,0:T(8,128)}, bf16[16,9,64,128]{3,2,1,0:T(8,128)(2,1)}, bf16[16,9,64,128]{3,2,1,0:T(8,128)(2,1)}) custom-call(s32[2]{0:T(128)} %pad_add_fusion.where_ref, bf16[8,9,128,128]{3,2,1,0:T(8,128)(2,1)} %all-to-all-done.2.mine_ref, ...), custom_call_target="tpu_custom_call" | custom-call | flops 14000000000 | bytes 20000000 | tf_op jit(solution)/shard_map/attention/pallas_call | solution.py:367
  117.3 0.2 collective-permute-start.3
  117.5 4.6 %collective-permute-done.3 = bf16[16,9,64,128]{3,2,1,0:T(8,128)(2,1)S(1)} collective-permute-done((bf16[16,9,64,128]{3,2,1,0:T(8,128)(2,1)}, bf16[16,9,64,128]{3,2,1,0:T(8,128)(2,1)S(1)}, u32[]{:S(2)}, u32[]{:S(2)}) %collective-permute-start.3) | collective-permute-done | bytes 2359328 | tf_op jit(solution)/shard_map/ppermute | solution.py:486
  122.2 4.2 %add_convert_fusion = bf16[16,9,64,128]{3,2,1,0:T(8,128)(2,1)} fusion(bf16[16,9,64,128]{3,2,1,0:T(8,128)(2,1)S(1)} %collective-permute-done.3, bf16[16,9,64,128]{3,2,1,0:T(8,128)(2,1)} %get-tuple-element.28), kind=kLoop, calls=%fused_computation | loop fusion | flops 4718592 | bytes 7077888 | tf_op jit(solution)/shard_map/convert_element_type | solution.py:487
  126.3 6.6 %all-to-all-start.3 = ((bf16[16,9,64,128]{3,2,1,0:T(8,128)(2,1)}), bf16[16,9,64,128]{3,2,1,0:T(8,128)(2,1)S(1)}, u32[]{:S(2)}, u32[]{:S(2)}) async-start(bf16[16,9,64,128]{3,2,1,0:T(8,128)(2,1)} %add_convert_fusion), calls=%async_computation.3 | async-start | bytes 4718592 | tf_op jit(solution)/shard_map/all_to_all | solution.py:488
  132.9 0.1 reshape.145
  133.0 0.2 copy.100
  133.3 2.3 %copy.93 = bf16[2,512,512]{1,2,0:T(8,128)(2,1)} copy(bf16[2,512,512]{2,1,0:T(8,128)(2,1)} %get-tuple-element.30) | data formatting | bytes 2097152 | tf_op jit(solution)/shard_map/attention/pallas_call | solution.py:367
  135.6 2.0 fusion.6
  137.6 0.2 copy.96
  137.8 0.8 copy.137
  138.5 2.3 %copy.97 = bf16[2,512,512]{1,2,0:T(8,128)(2,1)} copy(bf16[2,512,512]{2,1,0:T(8,128)(2,1)} %get-tuple-element.31) | data formatting | bytes 2097152 | tf_op jit(solution)/shard_map/attention/pallas_call | solution.py:367
  140.8 0.3 add_convert_fusion.1
  141.1 2.0 fusion.7
  143.1 0.2 maximum_bitcast_fusion
  143.3 0.3 copy.101
  143.6 1.2 reshape.146
  144.7 20.3 %all-to-all-done.3.in_ref = bf16[16,9,64,128]{3,2,1,0:T(8,128)(2,1)S(1)} async-done(((bf16[16,9,64,128]{3,2,1,0:T(8,128)(2,1)}), bf16[16,9,64,128]{3,2,1,0:T(8,128)(2,1)S(1)}, u32[]{:S(2)}, u32[]{:S(2)}) %all-to-all-start.3) | async-done | bytes 2359328 | tf_op jit(solution)/shard_map/all_to_all | solution.py:488
  165.0 0.4 merge.1
  165.5 14.4 %all_to_all.31 = bf16[8,16,640]{2,1,0:T(8,128)(2,1)S(1)} all-to-all(bf16[8,16,640]{2,1,0:T(8,128)(2,1)S(1)} %merge.1), channel_id=1, replica_groups=mesh['xh'=2,'z'=8,'co'=2,'xl'=2,'y'=4] {'z'}, dimensions={0} | all-to-all | bytes 327680 | tf_op jit(solution)/shard_map/all_to_all | solution.py:510
  179.9 0.1 multiply_reduce_fusion.2
  180.0 0.1 fusion.31
  180.3 0.2 multiply_reduce_fusion
  180.5 0.1 copy.102
  180.6 0.2 fusion.48
  181.1 2.5 %collective-permute-start.4 = (bf16[1,640]{1,0:T(2,128)(2,1)S(1)}, bf16[1,640]{1,0:T(2,128)(2,1)S(1)}, u32[]{:S(2)}, u32[]{:S(2)}) collective-permute-start(bf16[1,640]{1,0:T(2,128)(2,1)S(1)} %pad_maximum_fusion.6), channel_id=1, source_target_pairs={{0,1},{1,2},{2,3},{3,8},{8,9},{9,10},{10,11},{11,16},{16,17},{17,1... | collective-permute-start | bytes 3848 | tf_op jit(solution)/shard_map/ppermute | solution.py:537
  183.6 8.1 %collective-permute-done.4 = bf16[1,640]{1,0:T(2,128)(2,1)S(1)} collective-permute-done((bf16[1,640]{1,0:T(2,128)(2,1)S(1)}, bf16[1,640]{1,0:T(2,128)(2,1)S(1)}, u32[]{:S(2)}, u32[]{:S(2)}) %collective-permute-start.4) | collective-permute-done | bytes 1312 | tf_op jit(solution)/shard_map/ppermute | solution.py:537
  192.0 0.1 concatenate.46
  192.1 10.1 %all_to_all.32 = bf16[8,16,1280]{2,1,0:T(8,128)(2,1)S(1)} all-to-all(bf16[8,16,1280]{2,1,0:T(8,128)(2,1)S(1)} %broadcast_in_dim.90), channel_id=1, replica_groups=mesh['xh'=2,'z'=8,'co'=2,'xl'=2,'y'=4] {'xl','y'}, dimensions={0} | all-to-all | bytes 655360 | tf_op jit(solution)/shard_map/all_to_all | solution.py:75
  202.2 0.2 add_reduce_fusion
  202.4 1.0 fusion.4
  203.5 1.0 fusion.5
  (81 shorter events, 1.5 us)
Async XLA Ops:
  1.4 12.3 %collective-permute-start.1 = (bf16[1,896]{1,0:T(2,128)(2,1)S(1)}, bf16[1,896]{1,0:T(2,128)(2,1)S(1)}, u32[]{:S(2)}, u32[]{:S(2)}) collective-permute-start(bf16[1,896]{1,0:T(2,128)(2,1)S(1)} %get-tuple-element.58), channel_id=1, source_target_pairs={{0,8},{8,16},{16,24},{24,32},{32,40},{40,48},{48,56},{56,64},{64,7... | collective-permute-start | bytes 5384 | tf_op jit(solution)/shard_map/ppermute | solution.py:81
  3.3 10.4 %collective-permute-start = (bf16[1,896]{1,0:T(2,128)(2,1)S(1)}, bf16[1,896]{1,0:T(2,128)(2,1)S(1)}, u32[]{:S(2)}, u32[]{:S(2)}) collective-permute-start(bf16[1,896]{1,0:T(2,128)(2,1)S(1)} %get-tuple-element.59), channel_id=1, source_target_pairs={{8,0},{16,8},{24,16},{32,24},{40,32},{48,40},{56,48},{64,56},{72,6... | collective-permute-start | bytes 5384 | tf_op jit(solution)/shard_map/ppermute | solution.py:81
  13.7 0.6 copy-start.21
  13.7 0.6 copy-start.22
  14.2 19.4 %copy-start.16 = (f32[512]{0:T(512)S(1)}, f32[512]{0:T(512)}, u32[]{:S(2)}) copy-start(f32[512]{0:T(512)} %param.17) | copy-start | bytes 6148
  17.8 14.7 %all-to-all-start = ((f32[8,16,1280]{2,1,0:T(8,128)}), f32[8,16,1280]{2,1,0:T(8,128)S(1)}, u32[]{:S(2)}, u32[]{:S(2)}) async-start(f32[8,16,1280]{2,1,0:T(8,128)} %bitcast.69), calls=%async_computation | async-start | bytes 1310720 | tf_op jit(solution)/shard_map/all_to_all | solution.py:437
  23.8 30.3 %copy-start.19 = (f32[16]{0:T(128)}, f32[16]{0:T(128)S(1)}, u32[]{:S(2)}) copy-start(f32[16]{0:T(128)S(1)} %fusion.50) | copy-start | bytes 196
  33.5 20.6 %copy-start.23 = (f32[16]{0:T(128)}, f32[16]{0:T(128)S(1)}, u32[]{:S(2)}) copy-start(f32[16]{0:T(128)S(1)} %get-tuple-element.69) | copy-start | bytes 196
  54.1 4.5 %copy-start.6 = (bf16[512,1024]{1,0:T(8,128)(2,1)S(1)}, bf16[512,1024]{1,0:T(8,128)(2,1)}, u32[]{:S(2)}) copy-start(bf16[512,1024]{1,0:T(8,128)(2,1)} %param.18) | copy-start | bytes 3145732
  54.1 4.8 %copy-start.7 = (bf16[512,1024]{1,0:T(8,128)(2,1)S(1)}, bf16[512,1024]{1,0:T(8,128)(2,1)}, u32[]{:S(2)}) copy-start(bf16[512,1024]{1,0:T(8,128)(2,1)} %param.19) | copy-start | bytes 3145732
  54.1 30.3 %all-to-all-start.2 = ((bf16[8,9,128,128]{3,2,1,0:T(8,128)(2,1)}), bf16[8,9,128,128]{3,2,1,0:T(8,128)(2,1)}, u32[]{:S(2)}, u32[]{:S(2)}) async-start(bf16[8,9,128,128]{3,2,1,0:T(8,128)(2,1)} %broadcast_in_dim.39), calls=%async_computation.2 | async-start | bytes 4718592 | tf_op jit(solution)/shard_map/all_to_all | solution.py:75
  58.6 1.0 copy-start.15
  58.9 2.7 %copy-start.1 = (bf16[64,8,8,128]{3,2,1,0:T(8,128)(2,1)}, bf16[64,8,8,128]{3,2,1,0:T(8,128)(2,1)S(1)}, u32[]{:S(2)}) copy-start(bf16[64,8,8,128]{3,2,1,0:T(8,128)(2,1)S(1)} %copy.116) | copy-start | bytes 3145732
  59.2 3.2 %copy-start.2 = (bf16[64,8,8,128]{3,2,1,0:T(8,128)(2,1)}, bf16[64,8,8,128]{3,2,1,0:T(8,128)(2,1)S(1)}, u32[]{:S(2)}) copy-start(bf16[64,8,8,128]{3,2,1,0:T(8,128)(2,1)S(1)} %copy.118) | copy-start | bytes 3145732
  59.5 2.0 copy-start.10
  59.5 2.0 copy-start.12
  62.4 1.9 copy-start
  63.0 26.3 %copy-start.3 = (bf16[2,8,64,512]{3,2,1,0:T(8,128)(2,1)}, bf16[2,8,64,512]{3,2,1,0:T(8,128)(2,1)S(1)}, u32[]{:S(2)}) copy-start(bf16[2,8,64,512]{3,2,1,0:T(8,128)(2,1)S(1)} %copy.91) | copy-start | bytes 3145732
  84.4 4.9 %collective-permute-start.2 = (bf16[8,9,128,128]{3,2,1,0:T(8,128)(2,1)}, bf16[8,9,128,128]{3,2,1,0:T(8,128)(2,1)}, u32[]{:S(2)}, u32[]{:S(2)}) collective-permute-start(bf16[8,9,128,128]{3,2,1,0:T(8,128)(2,1)} %all-to-all-done.2.mine_ref), channel_id=1, source_target_pairs={{0,8},{8,0},{1,9},{9,1},{2,10},{10,2},{3,11},{11,3},{4,12},{12,4},... | collective-permute-start | bytes 7077896 | tf_op jit(solution)/shard_map/ppermute | solution.py:480
  117.3 4.8 %collective-permute-start.3 = (bf16[16,9,64,128]{3,2,1,0:T(8,128)(2,1)}, bf16[16,9,64,128]{3,2,1,0:T(8,128)(2,1)S(1)}, u32[]{:S(2)}, u32[]{:S(2)}) collective-permute-start(bf16[16,9,64,128]{3,2,1,0:T(8,128)(2,1)} %get-tuple-element.29), channel_id=1, source_target_pairs={{0,8},{8,0},{1,9},{9,1},{2,10},{10,2},{3,11},{11,3},{4,12},{12,4},... | collective-permute-start | bytes 7077896 | tf_op jit(solution)/shard_map/ppermute | solution.py:486
  126.3 6.6 %copy-start.14 = (f32[2,64,512]{2,1,0:T(8,128)S(1)}, f32[2,64,512]{2,1,0:T(8,128)}, u32[]{:S(2)}) copy-start(f32[2,64,512]{2,1,0:T(8,128)} %get-tuple-element.32) | copy-start | bytes 786436
  126.3 38.7 %all-to-all-start.3 = ((bf16[16,9,64,128]{3,2,1,0:T(8,128)(2,1)}), bf16[16,9,64,128]{3,2,1,0:T(8,128)(2,1)S(1)}, u32[]{:S(2)}, u32[]{:S(2)}) async-start(bf16[16,9,64,128]{3,2,1,0:T(8,128)(2,1)} %add_convert_fusion), calls=%async_computation.3 | async-start | bytes 4718592 | tf_op jit(solution)/shard_map/all_to_all | solution.py:488
  135.5 5.2 %copy-start.11 = (f32[2,64,32]{2,1,0:T(8,128)S(1)}, f32[2,64,32]{2,1,0:T(8,128)}, u32[]{:S(2)}) copy-start(f32[2,64,32]{2,1,0:T(8,128)} %copy-done.10) | copy-start | bytes 49156
  135.6 5.2 %copy-start.13 = (f32[2,64,32]{2,1,0:T(8,128)S(1)}, f32[2,64,32]{2,1,0:T(8,128)}, u32[]{:S(2)}) copy-start(f32[2,64,32]{2,1,0:T(8,128)} %copy-done.12) | copy-start | bytes 49156
  143.2 36.8 %copy-start.20 = (f32[16]{0:T(128)S(1)}, f32[16]{0:T(128)}, u32[]{:S(2)}) copy-start(f32[16]{0:T(128)} %copy-done.19) | copy-start | bytes 196
  143.3 36.9 %copy-start.24 = (f32[16]{0:T(128)S(1)}, f32[16]{0:T(128)}, u32[]{:S(2)}) copy-start(f32[16]{0:T(128)} %copy-done.23) | copy-start | bytes 196
  143.3 36.9 %copy-start.25 = (f32[16]{0:T(128)S(1)}, f32[16]{0:T(128)}, u32[]{:S(2)}) copy-start(f32[16]{0:T(128)} %get-tuple-element.68) | copy-start | bytes 196
  165.0 37.4 %copy-start.4 = (bf16[896,576]{0,1:T(8,128)(2,1)S(1)}, bf16[896,576]{0,1:T(8,128)(2,1)}, u32[]{:S(2)}) copy-start(bf16[896,576]{0,1:T(8,128)(2,1)} %param.16) | copy-start | bytes 3096580
  165.0 37.4 %copy-start.17 = (f32[896]{0:T(1024)S(1)}, f32[896]{0:T(1024)}, u32[]{:S(2)}) copy-start(f32[896]{0:T(1024)} %param.14) | copy-start | bytes 10756
  165.4 37.0 %copy-start.8 = (bf16[128,896]{1,0:T(8,128)(2,1)S(1)}, bf16[128,896]{1,0:T(8,128)(2,1)}, u32[]{:S(2)}) copy-start(bf16[128,896]{1,0:T(8,128)(2,1)} %embed_ref.1) | copy-start | bytes 688132
  165.4 38.0 %copy-start.5 = (bf16[896,576]{0,1:T(8,128)(2,1)S(1)}, bf16[896,576]{0,1:T(8,128)(2,1)}, u32[]{:S(2)}) copy-start(bf16[896,576]{0,1:T(8,128)(2,1)} %param.15) | copy-start | bytes 3096580
  165.5 38.0 %copy-start.9 = (bf16[128,896]{1,0:T(8,128)(2,1)S(1)}, bf16[128,896]{1,0:T(8,128)(2,1)}, u32[]{:S(2)}) copy-start(bf16[128,896]{1,0:T(8,128)(2,1)} %hidden_ref.1) | copy-start | bytes 688132
  165.5 38.0 %copy-start.18 = (f32[896]{0:T(1024)S(1)}, f32[896]{0:T(1024)}, u32[]{:S(2)}) copy-start(f32[896]{0:T(1024)} %param.13) | copy-start | bytes 10756
  181.1 10.6 %collective-permute-start.4 = (bf16[1,640]{1,0:T(2,128)(2,1)S(1)}, bf16[1,640]{1,0:T(2,128)(2,1)S(1)}, u32[]{:S(2)}, u32[]{:S(2)}) collective-permute-start(bf16[1,640]{1,0:T(2,128)(2,1)S(1)} %pad_maximum_fusion.6), channel_id=1, source_target_pairs={{0,1},{1,2},{2,3},{3,8},{8,9},{9,10},{10,11},{11,16},{16,17},{17,1... | collective-permute-start | bytes 3848 | tf_op jit(solution)/shard_map/ppermute | solution.py:537
